TPU v7x, 128 devices: a whole 4x4x4 slice. The times are simulated.
128 devices in a mesh: row: 8 (over y, z_lo), col: 16 (over z_hi, x, core).
Axes of the slice: x: 4, y: 4, z: 4 (z_hi: 2, z_lo: 2; z = z_hi * 2 + z_lo), core: 2. Of those that a mesh axis runs over, the one named last changes fastest.
Arguments:
- initial_kelvin_state: float32 [8, 1024, 2048], P(None, 'row', 'col'), may hold values from -6 to 6
- substance_region: int32 [8, 1024, 2048], P(None, 'row', 'col'), may hold values from 0 to 2, as said below
- source_energy: float32 [8, 1024, 2048], P(None, 'row', 'col'), may hold values from 0.2 to 5
- substance_transfer_magnitude: float32 [3], replicated, may hold values from 0.02 to 6, as said below
- substance_softening_rate: float32 [3], replicated, may hold values from 0.05 to 0.25
Outputs:
- new_temperature: float32 [8, 1024, 2048], P(None, 'row', 'col')
Inputs may be any that keep to these rules, and one draw needn't show every extreme that they name: `substance_region`: 0 die, 1 thermal interface material, 2 spreader. `substance_transfer_magnitude`: positive conductivity scales of die, interface material and spreader, in that order.
All inputs are finite; a program needn't handle non-finite values.
Results may differ from a plain program's by a relative error of at most 0.0027.
Values sent between devices are 32-bit elements; how exact they have to be, the bound alone decides.
No kernel may reach another device: no remote copies, remote signals or barrier semaphores. Data moves between devices by JAX's collectives and lax.ppermute only.
A program may use at most 192 MiB of HBM per device.

v0:
```python
import jax
import jax.numpy as jnp
from jax import lax
from jax.sharding import PartitionSpec as P

inplane_ratio = 1000.0
depth_ratio = 0.08


def padded_2(cells, sides, width):
    for axis, dim in sides:
        count = lax.axis_size(axis)
        ends = count - 1
        head = lax.slice_in_dim(cells, 0, width, axis=dim)
        tail = lax.slice_in_dim(cells, cells.shape[dim] - width, cells.shape[dim], axis=dim)
        cells = jnp.concatenate(
            [
                lax.ppermute(tail, axis, [(i, (i + 1) % count) for i in range(ends)]),
                cells,
                lax.ppermute(head, axis, [((i + 1) % count, i) for i in range(ends)]),
            ],
            axis=dim,
        )
    return cells


def transfer_coefficient_array(
    initial_kelvin_state, substance_region, substance_transfer_magnitude, substance_softening_rate
):
    nodal_transfer_coefficient = jnp.where(
        substance_region == 0,
        substance_transfer_magnitude[0],
        jnp.where(
            substance_region == 1, substance_transfer_magnitude[1], substance_transfer_magnitude[2]
        ),
    )
    nodal_thermal_softening = jnp.where(
        substance_region == 0,
        substance_softening_rate[0],
        jnp.where(substance_region == 1, substance_softening_rate[1], substance_softening_rate[2]),
    )
    return nodal_transfer_coefficient * jnp.exp(-nodal_thermal_softening * initial_kelvin_state)


def face_conductance(center, beside):
    return 2.0 * center * beside / (center + beside)


def forward_diffusion_parts(field_padded, cond_padded):
    field_center = field_padded[:, 1:-1, 1:-1]
    cond_center = cond_padded[:, 1:-1, 1:-1]

    def flux(field_beside, cond_beside):
        return face_conductance(cond_center, cond_beside) * (field_beside - field_center)

    implicit_pass_first_axis = inplane_ratio * (
        flux(field_padded[:, 1:-1, 2:], cond_padded[:, 1:-1, 2:])
        + flux(field_padded[:, 1:-1, :-2], cond_padded[:, 1:-1, :-2])
    )
    implicit_pass_second_axis = inplane_ratio * (
        flux(field_padded[:, 2:, 1:-1], cond_padded[:, 2:, 1:-1])
        + flux(field_padded[:, :-2, 1:-1], cond_padded[:, :-2, 1:-1])
    )
    field_layers = jnp.pad(field_center, ((1, 1), (0, 0), (0, 0)))
    cond_layers = jnp.pad(cond_center, ((1, 1), (0, 0), (0, 0)))
    implicit_pass_third_axis = depth_ratio * (
        flux(field_layers[2:], cond_layers[2:]) + flux(field_layers[:-2], cond_layers[:-2])
    )
    bottom = (lax.broadcasted_iota(jnp.int32, field_center.shape, 0) == 0).astype(
        field_center.dtype
    )
    implicit_pass_third_axis = (
        implicit_pass_third_axis - depth_ratio * bottom * cond_center * field_center
    )
    return (implicit_pass_first_axis, implicit_pass_second_axis, implicit_pass_third_axis)


def line_system(cond_lines, line_axis, ratio):
    length = cond_lines.shape[line_axis]
    plate_thicknesses = [(0, 0)] * cond_lines.ndim
    plate_thicknesses[line_axis] = (1, 1)
    cond_padded = jnp.pad(cond_lines, plate_thicknesses)
    before = lax.slice_in_dim(cond_padded, 0, length, axis=line_axis)
    after = lax.slice_in_dim(cond_padded, 2, length + 2, axis=line_axis)
    lower_band = -0.5 * ratio * face_conductance(cond_lines, before)
    upper_band = -0.5 * ratio * face_conductance(cond_lines, after)
    main_band = 1.0 - lower_band - upper_band
    return (lower_band, main_band, upper_band)


def append_slab(values, filler, line_axis):
    slab_shape = list(values.shape)
    slab_shape[line_axis] = 1
    return jnp.concatenate([values, jnp.full(slab_shape, filler, values.dtype)], line_axis)


def prepend_slab(values, filler, line_axis):
    slab_shape = list(values.shape)
    slab_shape[line_axis] = 1
    return jnp.concatenate([jnp.full(slab_shape, filler, values.dtype), values], line_axis)


def reduce_solve(lower_band, main_band, upper_band, right_side, line_axis):
    length = right_side.shape[line_axis]
    if length == 1:
        return right_side / main_band
    padded_length = right_side.shape[line_axis]
    half_length = padded_length // 2
    outer_shape = right_side.shape[:line_axis]
    inner_shape = right_side.shape[line_axis + 1 :]

    def paired(values):
        return values.reshape(outer_shape + (half_length, 2) + inner_shape)

    def evens(values):
        return lax.index_in_dim(paired(values), 0, line_axis + 1, keepdims=False)

    def odds(values):
        return lax.index_in_dim(paired(values), 1, line_axis + 1, keepdims=False)

    def following(values, filler):
        return append_slab(
            lax.slice_in_dim(evens(values), 1, half_length, axis=line_axis), filler, line_axis
        )

    left_factor = -odds(lower_band) / evens(main_band)
    right_factor = -odds(upper_band) / following(main_band, 1.0)
    new_lower = left_factor * evens(lower_band)
    new_upper = right_factor * following(upper_band, 0.0)
    new_main = (
        odds(main_band)
        + left_factor * evens(upper_band)
        + right_factor * following(lower_band, 0.0)
    )
    new_right = (
        odds(right_side)
        + left_factor * evens(right_side)
        + right_factor * following(right_side, 0.0)
    )
    odd_values = reduce_solve(new_lower, new_main, new_upper, new_right, line_axis)
    earlier = prepend_slab(
        lax.slice_in_dim(odd_values, 0, half_length - 1, axis=line_axis), 0.0, line_axis
    )
    even_values = (
        evens(right_side) - evens(lower_band) * earlier - evens(upper_band) * odd_values
    ) / evens(main_band)
    joined_shape = list(right_side.shape)
    joined = jnp.stack([even_values, odd_values], line_axis + 1).reshape(joined_shape)
    return joined


def solve_xlines(pieces):
    cond_lines, side_lines = pieces
    lower_band, main_band, upper_band = line_system(cond_lines, 2, inplane_ratio)
    return reduce_solve(lower_band, main_band, upper_band, side_lines, 2)


def solve_ylines(pieces):
    cond_lines, side_lines = pieces
    lower_band, main_band, upper_band = line_system(cond_lines, 1, inplane_ratio)
    return reduce_solve(lower_band, main_band, upper_band, side_lines, 1)


def across_x(transfer_coefficient_volume, first_boundary_face):
    return solve_xlines(
        (
            lax.all_to_all(
                transfer_coefficient_volume, "col", split_axis=1, concat_axis=2, tiled=True
            ),
            lax.all_to_all(first_boundary_face, "col", split_axis=1, concat_axis=2, tiled=True),
        )
    )


def local(
    initial_kelvin_state,
    substance_region,
    source_energy,
    substance_transfer_magnitude,
    substance_softening_rate,
):
    transfer_coefficient_volume = transfer_coefficient_array(
        initial_kelvin_state,
        substance_region,
        substance_transfer_magnitude,
        substance_softening_rate,
    )
    plate_pile = jnp.stack([initial_kelvin_state, transfer_coefficient_volume])
    padded = padded_2(plate_pile, (("row", 2), ("col", 3)), 1)
    implicit_pass_first_axis, implicit_pass_second_axis, implicit_pass_third_axis = (
        forward_diffusion_parts(padded[0], padded[1])
    )
    first_boundary_face = (
        initial_kelvin_state
        + 0.5 * implicit_pass_first_axis
        + implicit_pass_second_axis
        + implicit_pass_third_axis
        + source_energy
    )
    half_along_y = 0.5 * implicit_pass_second_axis
    half_step = across_x(transfer_coefficient_volume, first_boundary_face)
    half_home = lax.all_to_all(half_step, "col", split_axis=2, concat_axis=1, tiled=True)
    second_side = half_home - half_along_y
    new_ylines = solve_ylines(
        (
            lax.all_to_all(
                transfer_coefficient_volume, "row", split_axis=0, concat_axis=1, tiled=True
            ),
            lax.all_to_all(second_side, "row", split_axis=0, concat_axis=1, tiled=True),
        )
    )
    return lax.all_to_all(new_ylines, "row", split_axis=1, concat_axis=0, tiled=True)


def solution(mesh):
    in_specs = (P(None, "row", "col"), P(None, "row", "col"), P(None, "row", "col"), P(), P())
    out_specs = P(None, "row", "col")
    return jax.shard_map(local, mesh=mesh, in_specs=in_specs, out_specs=out_specs, check_vma=False)
```

profile of v0, /device:TPU:0, one launch (start us, length us, event | category | flops | bytes accessed | tf_op | source)
XLA Modules:
  0.0 271.1 jit_solution(5360164779684135227)
XLA Ops:
  2.8 6.0 %exponential_multiply_fusion = f32[8,128,128]{2,1,0:T(8,128)} fusion(f32[8,128,128]{2,1,0:T(8,128)} %param.5, s32[8,128,128]{2,1,0:T(8,128)} %param.6, f32[]{:T(128)} %bitcast.6, f32[]{:T(128)} %bitcast.5, f32[]{:T(128)} %bitcast.4, f32[]{:T(128)} %bitcast.3, f32[]{:T(128)} %bitcast.2, f32[]{:T(128)} %bitcast.1), kind=kLoop, calls=%fused_computation.133 | loop fusion | flops 1179648 | bytes 1572888 | tf_op jit(solution)/shard_map/mul | solution.py:42
  9.6 3.9 %collective-permute-start = (f32[2,8,1,128]{3,2,1,0:T(1,128)S(1)}, f32[2,8,1,128]{3,2,1,0:T(1,128)S(1)}, u32[]{:S(2)}, u32[]{:S(2)}) collective-permute-start(f32[2,8,1,128]{3,2,1,0:T(1,128)S(1)} %get-tuple-element.37), channel_id=1, source_target_pairs={{0,16},{16,32},{32,48},{48,64},{64,80},{80,96},{96,112},{1,17},{17... | collective-permute-start | bytes 24584 | tf_op jit(solution)/shard_map/ppermute | solution.py:18
  14.9 6.6 %all-to-all-start.4 = ((f32[8,128,128]{2,1,0:T(8,128)}), f32[8,128,128]{2,1,0:T(8,128)S(1)}, u32[]{:S(2)}, u32[]{:S(2)}) async-start(f32[8,128,128]{2,1,0:T(8,128)} %exponential_multiply_fusion), calls=%async_computation.4 | async-start | bytes 1048576 | tf_op jit(solution)/shard_map/all_to_all | solution.py:206
  37.2 11.8 %all-to-all-start.1 = ((f32[8,128,128]{2,0,1:T(8,128)}), f32[8,128,128]{2,0,1:T(8,128)S(1)}, u32[]{:S(2)}, u32[]{:S(2)}) async-start(f32[8,128,128]{2,0,1:T(8,128)} %copy.681), calls=%async_computation.1 | async-start | bytes 1048576 | tf_op jit(solution)/shard_map/all_to_all | solution.py:167
  52.9 8.6 %all-to-all-done.1 = f32[8,128,128]{2,0,1:T(8,128)S(1)} async-done(((f32[8,128,128]{2,0,1:T(8,128)}), f32[8,128,128]{2,0,1:T(8,128)S(1)}, u32[]{:S(2)}, u32[]{:S(2)}) %all-to-all-start.1) | async-done | bytes 524320 | tf_op jit(solution)/shard_map/all_to_all | solution.py:167
  61.5 3.8 %all-to-all-start = ((f32[8,128,128]{2,0,1:T(8,128)}), f32[8,128,128]{2,0,1:T(8,128)S(1)}, u32[]{:S(2)}, u32[]{:S(2)}) async-start(f32[8,128,128]{2,0,1:T(8,128)} %copy.679), calls=%async_computation | async-start | bytes 1048576 | tf_op jit(solution)/shard_map/all_to_all | solution.py:170
  65.2 4.6 %copy.682 = f32[8,8,16,128]{1,0,3,2:T(8,128)} copy(f32[8,8,16,128]{3,0,1,2:T(8,128)S(1)} %bitcast.1536) | data formatting | bytes 1048576 | tf_op jit(solution)/shard_map/all_to_all | solution.py:167
  69.8 14.2 %subtract_subtract_fusion = (f32[8,8,2048]{1,0,2:T(8,128)S(1)}, f32[8,8,2048]{1,0,2:T(8,128)S(1)}, f32[8,8,2048]{1,0,2:T(8,128)}) fusion(f32[8,8,2048]{1,0,2:T(8,128)} %bitcast.1439), kind=kLoop, calls=%fused_computation.2 | loop fusion | flops 1441792 | bytes 2097152 | tf_op jit(solution)/shard_map/sub | solution.py:87
  92.8 4.0 %slice_bitcast_fusion = f32[8,8,1024]{1,0,2:T(8,128)S(1)} fusion(f32[8,8,1024,2]{1,0,3,2:T(8,128)} %bitcast.1413), kind=kLoop, calls=%fused_computation.4 | loop fusion | bytes 524288 | tf_op jit(solution)/shard_map/squeeze | solution.py:116
  107.5 4.6 %copy.680 = f32[8,16,8,128]{2,0,3,1:T(8,128)} copy(f32[8,16,8,128]{3,0,2,1:T(8,128)S(1)} %bitcast.1535) | data formatting | bytes 1048576 | tf_op jit(solution)/shard_map/all_to_all | solution.py:170
  116.9 19.9 %fusion.7 = (f32[8,8,1024]{1,0,2:T(8,128)}, f32[8,8,1024]{1,0,2:T(8,128)}, f32[8,8,1024]{1,0,2:T(8,128)}) fusion(f32[8,8,1024,2]{1,0,3,2:T(8,128)} %bitcast.1419, f32[8,8,1023]{1,0,2:T(8,128)} %slice.1351, f32[8,8,1024,2]{1,0,3,2:T(8,128)} %bitcast.1409, f32[8,8,1024,2]{1,0,3,2:T(8,128)} %bitcast.1403, f32[8,8,1023]{1,0,2:T(8,128)} %slice.1350, ...), kind=kLoop, calls=%fused_computation.16 | loop fusion | flops 851968 | bytes 3668992 | tf_op jit(solution)/shard_map/add | solution.py:136
  150.8 3.8 %fusion.15 = (f32[8,8,512]{1,0,2:T(8,128)S(1)}, f32[8,8,512]{1,0,2:T(8,128)S(1)}, f32[8,8,512]{1,0,2:T(8,128)S(1)}) fusion(f32[8,8,512,2]{1,0,3,2:T(8,128)S(1)} %bitcast.1432, f32[8,8,511]{1,0,2:T(8,128)} %slice.1363, f32[8,8,512,2]{1,0,3,2:T(8,128)S(1)} %bitcast.1425, f32[8,8,512,2]{1,0,3,2:T(8,128)S(1)} %bitcast.1429, f32[8,8,511]{1,0,2:T(8,128)S(1)} %slice-done.6, ...), kind=kLoop, calls=%fused_computation.39 | loop fusion | flops 425984 | bytes 1833984 | tf_op jit(solution)/shard_map/add | solution.py:136
  161.0 4.1 %fusion.23 = (f32[8,8,256]{1,0,2:T(8,128)}, f32[8,8,256]{1,0,2:T(8,128)S(1)}, f32[8,8,256]{1,0,2:T(8,128)}) fusion(f32[8,8,256,2]{1,0,3,2:T(8,128)S(1)} %bitcast.1451, f32[8,8,255]{1,0,2:T(8,128)} %slice.1375, f32[8,8,256,2]{1,0,3,2:T(8,128)S(1)} %bitcast.1448, f32[8,8,256,2]{1,0,3,2:T(8,128)S(1)} %bitcast.1444, f32[8,8,255]{1,0,2:T(8,128)} %slice.1374, ...), kind=kLoop, calls=%fused_computation.64 | loop fusion | flops 212992 | bytes 916480 | tf_op jit(solution)/shard_map/add | solution.py:136
  182.2 6.9 %divide_bitcast_fusion = f32[8,8,1024,1]{1,0,2,3:T(8,128)} fusion(f32[8,8,1023]{1,0,2:T(8,128)} %slice.1481, f32[8,8,512,2]{1,0,3,2:T(8,128)} %copy-done.2, f32[8,8,1024,2]{1,0,3,2:T(8,128)S(1)} %bitcast.1406, f32[8,8,1024,2]{1,0,3,2:T(8,128)S(1)} %bitcast.1412, f32[8,8,1024,2]{1,0,3,2:T(8,128)} %bitcast.1420, f32[8,8,1024,2]{1,0,3,2:T(8,128)S(1)} %bitcast.1417), kind=kLoop, calls=%fused_computation.22 | loop fusion | flops 327680 | bytes 1834752 | tf_op jit(solution)/shard_map/stack | solution.py:148
  189.1 4.0 %pad_maximum_fusion = f32[8,8,1024,2]{1,0,2,3:T(8,128)S(1)} fusion(f32[8,8,1024,1]{1,0,2,3:T(8,128)} %bitcast.1422, f32[8,8,1024,1]{1,0,2,3:T(8,128)} %divide_bitcast_fusion), kind=kLoop, calls=%fused_computation | loop fusion | flops 131072 | bytes 1048576 | tf_op jit(solution)/shard_map/stack | solution.py:148
  193.1 3.9 %copy.770 = f32[8,8,1024,2]{1,0,3,2:T(8,128)} copy(f32[8,8,1024,2]{1,0,2,3:T(8,128)S(1)} %pad_maximum_fusion) | data formatting | bytes 1048576 | tf_op jit(solution)/shard_map/stack | solution.py:148
  197.1 7.4 %reshape.2193 = f32[16,1,8192]{2,1,0:T(1,128)} reshape(f32[2048,8,8]{2,1,0:T(8,128)} %bitcast.1437) | data formatting | bytes 1048576
  204.5 7.0 %all-to-all-start.2 = ((f32[16,1,8192]{2,1,0:T(1,128)}), f32[16,1,8192]{2,1,0:T(1,128)S(1)}, u32[]{:S(2)}, u32[]{:S(2)}) async-start(f32[16,1,8192]{2,1,0:T(1,128)} %reshape.2193), calls=%async_computation.2 | async-start | bytes 1048576 | tf_op jit(solution)/shard_map/all_to_all | solution.py:202
  212.4 11.5 %all-to-all-done.2 = f32[16,1,8192]{2,1,0:T(1,128)S(1)} async-done(((f32[16,1,8192]{2,1,0:T(1,128)}), f32[16,1,8192]{2,1,0:T(1,128)S(1)}, u32[]{:S(2)}, u32[]{:S(2)}) %all-to-all-start.2) | async-done | bytes 524320 | tf_op jit(solution)/shard_map/all_to_all | solution.py:202
  226.2 6.7 %reshape.2194 = f32[2048,8,8]{2,1,0:T(8,128)} reshape(f32[16,8192]{1,0:T(8,128)S(1)} %reduce) | data formatting | bytes 1048576
  233.0 5.2 %copy.771 = f32[8,16,8,128]{3,2,1,0:T(8,128)S(1)} copy(f32[8,16,8,128]{2,0,3,1:T(8,128)} %bitcast.1438) | data formatting | bytes 1048576 | tf_op jit(solution)/shard_map/all_to_all | solution.py:202
  239.0 5.1 %all-to-all-start.3 = ((f32[8,128,128]{2,1,0:T(8,128)}), f32[8,128,128]{2,1,0:T(8,128)S(1)}, u32[]{:S(2)}, u32[]{:S(2)}) async-start(f32[8,128,128]{2,1,0:T(8,128)} %bitcast_subtract_fusion), calls=%async_computation.3 | async-start | bytes 1048576 | tf_op jit(solution)/shard_map/all_to_all | solution.py:209
  244.4 8.8 %all-to-all-done.3 = f32[8,128,128]{2,1,0:T(8,128)S(1)} async-done(((f32[8,128,128]{2,1,0:T(8,128)}), f32[8,128,128]{2,1,0:T(8,128)S(1)}, u32[]{:S(2)}, u32[]{:S(2)}) %all-to-all-start.3) | async-done | bytes 524320 | tf_op jit(solution)/shard_map/all_to_all | solution.py:209
  257.9 12.4 %all_to_all.84 = f32[1,1024,128]{2,0,1:T(1,128)S(1)} all-to-all(f32[1,1024,128]{2,0,1:T(1,128)S(1)} %bitcast.1541), channel_id=1, replica_groups=mesh['row'=8,'col'=16] {'row'}, dimensions={1} | all-to-all | bytes 1048576 | tf_op jit(solution)/shard_map/all_to_all | solution.py:212
  (346 shorter events, 94.2 us)
Async XLA Ops:
  9.6 11.8 %collective-permute-start = (f32[2,8,1,128]{3,2,1,0:T(1,128)S(1)}, f32[2,8,1,128]{3,2,1,0:T(1,128)S(1)}, u32[]{:S(2)}, u32[]{:S(2)}) collective-permute-start(f32[2,8,1,128]{3,2,1,0:T(1,128)S(1)} %get-tuple-element.37), channel_id=1, source_target_pairs={{0,16},{16,32},{32,48},{48,64},{64,80},{80,96},{96,112},{1,17},{17... | collective-permute-start | bytes 24584 | tf_op jit(solution)/shard_map/ppermute | solution.py:18
  13.6 7.9 %collective-permute-start.1 = (f32[2,8,1,128]{3,2,1,0:T(1,128)S(1)}, f32[2,8,1,128]{3,2,1,0:T(1,128)S(1)}, u32[]{:S(2)}, u32[]{:S(2)}) collective-permute-start(f32[2,8,1,128]{3,2,1,0:T(1,128)S(1)} %get-tuple-element.38), channel_id=1, source_target_pairs={{16,0},{32,16},{48,32},{64,48},{80,64},{96,80},{112,96},{17,1},{33... | collective-permute-start | bytes 24584 | tf_op jit(solution)/shard_map/ppermute | solution.py:20
  14.9 22.4 %all-to-all-start.4 = ((f32[8,128,128]{2,1,0:T(8,128)}), f32[8,128,128]{2,1,0:T(8,128)S(1)}, u32[]{:S(2)}, u32[]{:S(2)}) async-start(f32[8,128,128]{2,1,0:T(8,128)} %exponential_multiply_fusion), calls=%async_computation.4 | async-start | bytes 1048576 | tf_op jit(solution)/shard_map/all_to_all | solution.py:206
  22.7 8.1 %copy-start.10 = (f32[8,128,128]{2,1,0:T(8,128)S(1)}, f32[8,128,128]{2,1,0:T(8,128)}, u32[]{:S(2)}) copy-start(f32[8,128,128]{2,1,0:T(8,128)} %param.5) | copy-start | bytes 1572868
  23.7 5.4 %collective-permute-start.2 = (f32[2,8,130,1]{2,1,3,0:T(8,128)S(1)}, f32[2,8,130,1]{2,1,3,0:T(8,128)S(1)}, u32[]{:S(2)}, u32[]{:S(2)}) collective-permute-start(f32[2,8,130,1]{2,1,3,0:T(8,128)S(1)} %copy.675), channel_id=1, source_target_pairs={{0,1},{1,2},{2,3},{3,4},{4,5},{5,6},{6,7},{7,8},{8,9},{9,10},{10,1... | collective-permute-start | bytes 24968 | tf_op jit(solution)/shard_map/ppermute | solution.py:18
  25.6 4.8 %collective-permute-start.3 = (f32[2,8,130,1]{2,1,3,0:T(8,128)S(1)}, f32[2,8,130,1]{2,1,3,0:T(8,128)S(1)}, u32[]{:S(2)}, u32[]{:S(2)}) collective-permute-start(f32[2,8,130,1]{2,1,3,0:T(8,128)S(1)} %copy.676), channel_id=1, source_target_pairs={{1,0},{2,1},{3,2},{4,3},{5,4},{6,5},{7,6},{8,7},{9,8},{10,9},{11,1... | collective-permute-start | bytes 24968 | tf_op jit(solution)/shard_map/ppermute | solution.py:20
  37.2 24.2 %all-to-all-start.1 = ((f32[8,128,128]{2,0,1:T(8,128)}), f32[8,128,128]{2,0,1:T(8,128)S(1)}, u32[]{:S(2)}, u32[]{:S(2)}) async-start(f32[8,128,128]{2,0,1:T(8,128)} %copy.681), calls=%async_computation.1 | async-start | bytes 1048576 | tf_op jit(solution)/shard_map/all_to_all | solution.py:167
  61.5 46.1 %all-to-all-start = ((f32[8,128,128]{2,0,1:T(8,128)}), f32[8,128,128]{2,0,1:T(8,128)S(1)}, u32[]{:S(2)}, u32[]{:S(2)}) async-start(f32[8,128,128]{2,0,1:T(8,128)} %copy.679), calls=%async_computation | async-start | bytes 1048576 | tf_op jit(solution)/shard_map/all_to_all | solution.py:170
  84.0 5.7 %copy-start = (f32[8,8,2048]{1,0,2:T(8,128)}, f32[8,8,2048]{1,0,2:T(8,128)S(1)}, u32[]{:S(2)}) copy-start(f32[8,8,2048]{1,0,2:T(8,128)S(1)} %get-tuple-element.12) | copy-start | bytes 1572868
  84.0 8.3 %copy-start.1 = (f32[8,8,2048]{1,0,2:T(8,128)}, f32[8,8,2048]{1,0,2:T(8,128)S(1)}, u32[]{:S(2)}) copy-start(f32[8,8,2048]{1,0,2:T(8,128)S(1)} %get-tuple-element.11) | copy-start | bytes 1572868
  92.8 13.1 %copy-start.4 = (f32[8,8,1024,1]{1,0,2,3:T(8,128)}, f32[8,8,1024,1]{1,0,2,3:T(8,128)S(1)}, u32[]{:S(2)}) copy-start(f32[8,8,1024,1]{1,0,2,3:T(8,128)S(1)} %bitcast_multiply_fusion) | copy-start | bytes 786436
  170.7 5.9 %slice-start.4 = ((s8[8388608]{0:T(1024)(128)(4,1)}), s8[4194304]{0:T(1024)(128)(4,1)S(1)}, s32[]{:S(2)}) async-start(s8[8388608]{0:T(1024)(128)(4,1)} %bitcast.1415), calls=%async_computation.10 | async-start | bytes 8388608
  171.4 5.2 %slice-start = ((s8[8388608]{0:T(1024)(128)(4,1)}), s8[4194304]{0:T(1024)(128)(4,1)S(1)}, s32[]{:S(2)}) async-start(s8[8388608]{0:T(1024)(128)(4,1)} %bitcast.1404), calls=%async_computation.6 | async-start | bytes 8388608
  171.4 7.1 %slice-start.2 = ((s8[8388608]{0:T(1024)(128)(4,1)}), s8[4194304]{0:T(1024)(128)(4,1)S(1)}, s32[]{:S(2)}) async-start(s8[8388608]{0:T(1024)(128)(4,1)} %bitcast.1410), calls=%async_computation.8 | async-start | bytes 8388608
  171.4 8.3 %slice-start.5 = ((s8[8388608]{0:T(1024)(128)(4,1)}), s8[4194304]{0:T(1024)(128)(4,1)S(1)}, s32[]{:S(2)}) async-start(s8[8388608]{0:T(1024)(128)(4,1)} %bitcast.1415), calls=%async_computation.11 | async-start | bytes 8388608
  171.7 9.3 %slice-start.1 = ((s8[8388608]{0:T(1024)(128)(4,1)}), s8[4194304]{0:T(1024)(128)(4,1)S(1)}, s32[]{:S(2)}) async-start(s8[8388608]{0:T(1024)(128)(4,1)} %bitcast.1404), calls=%async_computation.7 | async-start | bytes 8388608
  171.7 10.5 %slice-start.3 = ((s8[8388608]{0:T(1024)(128)(4,1)}), s8[4194304]{0:T(1024)(128)(4,1)S(1)}, s32[]{:S(2)}) async-start(s8[8388608]{0:T(1024)(128)(4,1)} %bitcast.1410), calls=%async_computation.9 | async-start | bytes 8388608
  197.1 14.4 %copy-start.19 = (f32[1,1024,128]{2,1,0:T(8,128)S(1)}, f32[1,1024,128]{2,1,0:T(8,128)}, u32[]{:S(2)}) copy-start(f32[1,1024,128]{2,1,0:T(8,128)} %get-tuple-element.16) | copy-start | bytes 1572868
  197.1 14.8 %copy-start.18 = (f32[1,1024,128]{2,1,0:T(8,128)S(1)}, f32[1,1024,128]{2,1,0:T(8,128)}, u32[]{:S(2)}) copy-start(f32[1,1024,128]{2,1,0:T(8,128)} %get-tuple-element.15) | copy-start | bytes 1572868
  204.5 19.4 %all-to-all-start.2 = ((f32[16,1,8192]{2,1,0:T(1,128)}), f32[16,1,8192]{2,1,0:T(1,128)S(1)}, u32[]{:S(2)}, u32[]{:S(2)}) async-start(f32[16,1,8192]{2,1,0:T(1,128)} %reshape.2193), calls=%async_computation.2 | async-start | bytes 1048576 | tf_op jit(solution)/shard_map/all_to_all | solution.py:202
  233.0 11.2 %copy-start.15 = (f32[1,512,1,128]{3,2,1,0:T(1,128)S(1)}, f32[1,512,1,128]{3,2,1,0:T(1,128)}, u32[]{:S(2)}) copy-start(f32[1,512,1,128]{3,2,1,0:T(1,128)} %copy-done.14) | copy-start | bytes 786436
  238.2 15.5 %copy-start.20 = (f32[1,511,128]{2,1,0:T(8,128)S(1)}, f32[1,511,128]{2,1,0:T(8,128)}, u32[]{:S(2)}) copy-start(f32[1,511,128]{2,1,0:T(8,128)} %slice.1488) | copy-start | bytes 784900
  238.2 15.5 %copy-start.21 = (f32[1,512,1,128]{3,2,1,0:T(1,128)S(1)}, f32[1,512,1,128]{3,2,1,0:T(1,128)}, u32[]{:S(2)}) copy-start(f32[1,512,1,128]{3,2,1,0:T(1,128)} %get-tuple-element.49) | copy-start | bytes 786436
  239.0 14.2 %all-to-all-start.3 = ((f32[8,128,128]{2,1,0:T(8,128)}), f32[8,128,128]{2,1,0:T(8,128)S(1)}, u32[]{:S(2)}, u32[]{:S(2)}) async-start(f32[8,128,128]{2,1,0:T(8,128)} %bitcast_subtract_fusion), calls=%async_computation.3 | async-start | bytes 1048576 | tf_op jit(solution)/shard_map/all_to_all | solution.py:209
  (16 other events, 42.7 us)
where the time goes:
time: 272 us; the launch traced here: 271 us
  local copies, waits for them, and re-layouts  107 us (39%)
  other arithmetic  77.5 us (28%)
  starting transfers between devices  42 us (15%)
  waiting for transfers between devices  29.7 us (11%)
  blocking collectives  12.4 us (5%)
    unnamed x61, local copies, waits for them, and re-layouts  37.7 us
    add x17, other arithmetic, reduce_solve(): odds(right_side) + left_factor * evens(right_side)  29.1 us
    slice x78, local copies, waits for them, and re-layouts, following(): lax.slice_in_dim(evens(values), 1, half_length, axis=line_axis)  19 us
    sub x2, other arithmetic, line_system(): main_band = 1.0 - lower_band - upper_band  15.4 us
    squeeze x38, local copies, waits for them, and re-layouts, evens(): return lax.index_in_dim(paired(values), 0, line_axis + 1, keepdims=False)  14.5 us
    another operation x38, other arithmetic, reduce_solve(): jnp.stack([even_values, odd_values], line_axis + 1).reshape(joined_shape)  13.5 us
    all_to_all x1, blocking collectives, local(): lax.all_to_all(new_ylines, 'row', split_axis=1, concat_axis=0, tiled=True)  12.4 us
    all_to_all x1, starting transfers between devices, across_x(): lax.all_to_all(transfer_coefficient_volume, 'col', split_axis=1, concat_a...  11.8 us
  transfers between devices with their start and end apart: 9, of which 4 were waited for; matrix products, arithmetic and copies ran while one was open for 20% of the time, Pallas kernels for 0%

commit v1 on v0

v1 whole, which is shorter than its diff:
```python
import jax
import jax.numpy as jnp
from jax import lax
from jax.experimental import pallas as pl
from jax.experimental.pallas import tpu as pltpu
from jax.sharding import PartitionSpec as P

Z, N = 8, 128
ROWS = Z * N
CHUNKS, STEP = 8, 16
F32 = jnp.float32
VM = pltpu.VMEM


def rcp(x):
    r = pl.reciprocal(x, approx=True)
    return r * (2.0 - x * r)


def link(a, b):
    return a * b * rcp(a + b)


def at(i):
    return pl.ds(pl.multiple_of(i * Z, Z), Z)


def strided(i):
    return pl.ds(i, Z, stride=N)


def conductivity(t, reg, mag, soft):
    m = jnp.where(reg == 0, mag[0] * 1000.0, jnp.where(reg == 1, mag[1] * 1000.0, mag[2] * 1000.0))
    b = jnp.where(reg == 0, soft[0], jnp.where(reg == 1, soft[1], soft[2]))
    return m * jnp.exp(-(b * t))


def turn(src, dst):
    def body(z, _):
        lines = pl.ds(z, N, stride=Z)
        dst[lines, :] = src[lines, :].T
        return 0

    lax.fori_loop(0, Z, body, 0, unroll=2)


def factor(c_ref, pr_ref, gr_ref, rr_ref, sep_ref, net_ref):
    one = jnp.ones((Z, N), F32)
    zero = jnp.zeros((Z, N), F32)

    def cell(c, j, p, t, s, here):
        i = c * STEP + j
        beyond = c_ref[at(i + 1), :]
        g = link(here, beyond)
        r = rcp(p + g + t)
        pr, gr = p * r, g * r
        pr_ref[at(i), :] = pr
        gr_ref[at(i), :] = gr
        rr_ref[at(i), :] = r
        return pr * g, 1.0 + gr * t, s + pr * t, beyond

    start = []
    for c in range(CHUNKS):
        here = c_ref[at(c * STEP + 1), :]
        start.append((link(c_ref[at(c * STEP), :], here), one, zero, here))

    def body(j, state):
        return [cell(c, j, *state[c]) for c in range(CHUNKS)]

    state = lax.fori_loop(1, STEP - 1, body, start)
    state = [cell(c, STEP - 1, *state[c]) for c in range(CHUNKS - 1)] + [state[-1]]
    q = state[0][0]
    left = 1.0 + state[0][2]
    t = state[0][1] + state[1][2]
    for c in range(1, CHUNKS):
        g = state[c][0]
        r = rcp(q + g + t)
        qr, gr = q * r, g * r
        sep_ref[0, c] = qr
        sep_ref[1, c] = gr
        sep_ref[2, c] = r
        left = left + qr * t
        t = state[c][1] + gr * t
        if c + 1 < CHUNKS:
            t = t + state[c + 1][2]
        q = qr * g
    net_ref[0] = q
    net_ref[1] = left
    net_ref[2] = t
    net_ref[3] = c_ref[at(0), :]
    net_ref[4] = c_ref[at(N - 1), :]


def sweep(rhs, pr_ref, gr_ref, rr_ref, sep_ref, net_ref, rd_ref, srd_ref, out_ref):
    def cell(c, j, d, s):
        i = c * STEP + j
        rd_ref[at(i), :] = rr_ref[at(i), :] * d
        return rhs(i + 1) + gr_ref[at(i), :] * d, s + pr_ref[at(i), :] * d

    def body(j, state):
        return [cell(c, j, *state[c]) for c in range(CHUNKS)]

    start = [(rhs(c * STEP + 1), jnp.zeros((Z, N), F32)) for c in range(CHUNKS)]
    state = lax.fori_loop(1, STEP - 1, body, start)
    state = [cell(c, STEP - 1, *state[c]) for c in range(CHUNKS - 1)] + [state[-1]]
    left = rhs(0) + state[0][1]
    d = state[0][0] + state[1][1]
    for c in range(1, CHUNKS):
        left = left + sep_ref[0, c] * d
        srd_ref[c] = sep_ref[2, c] * d
        d = state[c][0] + sep_ref[1, c] * d
        if c + 1 < CHUNKS:
            d = d + state[c + 1][1]
    out_ref[0] = net_ref[0]
    out_ref[1] = net_ref[1]
    out_ref[2] = net_ref[2]
    out_ref[3] = left
    out_ref[4] = d
    out_ref[5] = net_ref[3]
    out_ref[6] = net_ref[4]


def back(ul, ur, pr_ref, gr_ref, rd_ref, sep_ref, srd_ref, put):
    seps = [None] * CHUNKS + [ur]
    for c in range(CHUNKS - 1, 0, -1):
        seps[c] = srd_ref[c] + sep_ref[0, c] * ul + sep_ref[1, c] * seps[c + 1]
    seps[0] = ul
    for c in range(CHUNKS):
        put(c * STEP, seps[c])
    put(N - 1, ur)

    def cell(c, j, u):
        i = c * STEP + j
        v = rd_ref[at(i), :] + pr_ref[at(i), :] * seps[c] + gr_ref[at(i), :] * u
        put(i, v)
        return v

    state = [cell(c, STEP - 1, seps[c + 1]) for c in range(CHUNKS - 1)] + [ur]

    def body(k, state):
        return [cell(c, STEP - 2 - k, state[c]) for c in range(CHUNKS)]

    lax.fori_loop(0, STEP - 2, body, state)


def joined(own, other, left):
    a = [jnp.where(left, own[k], other[k]) for k in range(7)]
    b = [jnp.where(left, other[k], own[k]) for k in range(7)]
    between = link(a[6], b[5])
    r = rcp(a[0] + between + a[2])
    f, h = a[0] * r, between * r
    g1 = f * between
    s1 = b[1] + h * a[2]
    d1 = b[3] + h * a[4]
    left_s = a[1] + f * a[2]
    left_d = a[3] + f * a[4]
    r = rcp(g1 + b[0] + s1)
    f, h = g1 * r, b[0] * r
    return [f * b[0], left_s + f * s1, b[2] + h * s1, left_d + f * d1, b[4] + h * d1, a[5], b[6]]


def ends(me, levels, owns, others):
    zero = jnp.zeros((Z, N), F32)
    yl = il = yr = ir = zero
    for k in reversed(range(levels)):
        p, m = others[k], owns[k]
        left = (me >> k) % 2 == 1
        far_s = jnp.where(left, p[1] + yl, p[2] + yr)
        far_d = jnp.where(left, p[3] + il, p[4] + ir)
        near_s = jnp.where(left, p[2], p[1])
        near_d = jnp.where(left, p[4], p[3])
        between = jnp.where(left, link(p[6], m[5]), link(p[5], m[6]))
        f = p[0] * rcp(p[0] + far_s)
        s, d = near_s + f * far_s, near_d + f * far_d
        f = between * rcp(between + s)
        y, i = f * s, f * d
        yl, il = jnp.where(left, y, yl), jnp.where(left, i, il)
        yr, ir = jnp.where(left, yr, y), jnp.where(left, ir, i)
    m = owns[0]
    sl, dl, sr, dr = m[1] + yl, m[3] + il, m[2] + yr, m[4] + ir
    r = rcp(m[0] + sl)
    f = m[0] * r
    ur = (dr + f * dl) * rcp(sr + f * sl)
    ul = (dl + m[0] * ur) * r
    return ul, ur


def edge_kernel(t_ref, reg_ref, mag, soft, up_ref, down_ref):
    for row, out in ((0, up_ref), (N - 1, down_ref)):
        t = t_ref[strided(row), :]
        out[0] = t
        out[1] = conductivity(t, reg_ref[strided(row), :], mag, soft)


def first_kernel(
    t_ref, reg_ref, s_ref, mag, soft,
    ty_ref, cy_ref, r_ref, pr_ref, gr_ref, rr_ref, sep_ref, net_ref, cx_ref,
):
    z = lax.broadcasted_iota(jnp.int32, (Z, N), 0)
    inner = jnp.where(z < Z - 1, 1.6e-4, 0.0)
    ground = jnp.where(z == 0, 8e-5, 0.0)

    def load(y):
        t = t_ref[strided(y), :]
        c = conductivity(t, reg_ref[strided(y), :], mag, soft)
        ty_ref[at(y), :] = t
        cy_ref[at(y), :] = c
        return t, c

    def row(y, t, c, before, after):
        flux = link(c, pltpu.roll(c, Z - 1, 0)) * (pltpu.roll(t, Z - 1, 0) - t) * inner
        up = flux - pltpu.roll(flux, 1, 0) - ground * (c * t)
        r_ref[at(y), :] = 2.0 * t + s_ref[strided(y), :] + 2.0 * (after - before) + up

    def body(k, state):
        t, c, before = state
        for j in range(8):
            y = k * 8 + j
            tn, cn = load(y + 1)
            after = link(c, cn) * (tn - t)
            row(y, t, c, before, after)
            t, c, before = tn, cn, after
        return t, c, before

    t, c = load(0)
    state = lax.fori_loop(0, N // 8 - 1, body, (t, c, jnp.zeros((Z, N), F32)))
    t, c, before = state
    for y in range(N - 8, N - 1):
        tn, cn = load(y + 1)
        after = link(c, cn) * (tn - t)
        row(y, t, c, before, after)
        t, c, before = tn, cn, after
    row(N - 1, t, c, before, jnp.zeros((Z, N), F32))
    turn(cy_ref, cx_ref)
    factor(cx_ref, pr_ref, gr_ref, rr_ref, sep_ref, net_ref)


def side_call(
    r_ref, ty_ref, cy_ref, north_ref, south_ref, pr_ref, gr_ref, rr_ref, sep_ref, net_ref,
    rd_ref, srd_ref, out_ref, rx_ref, ry_ref,
):
    me = lax.axis_index("row")
    ry_ref[...] = r_ref[...]
    for row, halo, there in ((0, north_ref, me > 0), (N - 1, south_ref, me < lax.axis_size("row") - 1)):
        i = slice(row * Z, row * Z + Z)
        flux = link(cy_ref[i, :], halo[1]) * (halo[0] - ty_ref[i, :])
        ry_ref[i, :] = r_ref[i, :] + jnp.where(there, 2.0 * flux, 0.0)
    turn(ry_ref, rx_ref)
    sweep(
        lambda i: rx_ref[at(i), :],
        pr_ref, gr_ref, rr_ref, sep_ref, net_ref, rd_ref, srd_ref, out_ref,
    )


def merge_kernel(axis, level, own_ref, other_ref, out_ref):
    left = (lax.axis_index(axis) >> level) % 2 == 0
    new = joined([own_ref[k] for k in range(7)], [other_ref[k] for k in range(7)], left)
    for k in range(7):
        out_ref[k] = new[k]


def middle_kernel(
    levels, *refs,
):
    owns, others, refs = refs[:levels], refs[levels : 2 * levels], refs[2 * levels :]
    (
        pr_ref, gr_ref, rd_ref, sep_ref, srd_ref, ty_ref,
        ypr_ref, ygr_ref, yrr_ref, ysep_ref, ynet_ref,
        yrd_ref, ysrd_ref, out_ref, wx_ref, wy_ref,
    ) = refs
    ul, ur = ends(lax.axis_index("col"), levels, owns, others)

    def put(i, v):
        wx_ref[at(i), :] = v

    back(ul, ur, pr_ref, gr_ref, rd_ref, sep_ref, srd_ref, put)
    turn(wx_ref, wy_ref)
    sweep(
        lambda i: wy_ref[at(i), :] - 2.0 * ty_ref[at(i), :],
        ypr_ref, ygr_ref, yrr_ref, ysep_ref, ynet_ref, yrd_ref, ysrd_ref, out_ref,
    )


def last_kernel(levels, *refs):
    owns, others, refs = refs[:levels], refs[levels : 2 * levels], refs[2 * levels :]
    pr_ref, gr_ref, rd_ref, sep_ref, srd_ref, ty_ref, out_ref = refs
    ul, ur = ends(lax.axis_index("row"), levels, owns, others)

    def put(i, v):
        out_ref[strided(i), :] = v + ty_ref[at(i), :]

    back(ul, ur, pr_ref, gr_ref, rd_ref, sep_ref, srd_ref, put)


FIELD = (ROWS, N)
NET = (7, Z, N)
PART = (5, Z, N)
SEPS = (3, CHUNKS, Z, N)
SEPD = (CHUNKS, Z, N)


def vm(shape):
    return VM(shape, F32)


def call(kernel, args, outs, scratch=(), scalars=(), flops=0, inplace=None):
    args = [pltpu.with_memory_space_constraint(a, VM) for a in args]
    whole = pl.BlockSpec(memory_space=VM)
    small = pl.BlockSpec(memory_space=pltpu.SMEM)
    many = isinstance(outs, tuple)
    return pl.pallas_call(
        kernel,
        in_specs=[whole] * len(args) + [small] * len(scalars),
        out_specs=(whole,) * len(outs) if many else whole,
        out_shape=outs,
        scratch_shapes=list(scratch),
        cost_estimate=pl.CostEstimate(flops=flops, bytes_accessed=flops, transcendentals=0),
        compiler_params=pltpu.CompilerParams(vmem_limit_bytes=16 * 1024 * 1024),
    )(*args, *scalars)


def partner(x, axis, mask):
    return lax.ppermute(x, axis, [(i, i ^ mask) for i in range(lax.axis_size(axis))])


def spread(net, axis, masks):
    owns, others = [net], []
    for level, mask in enumerate(masks):
        others.append(partner(owns[-1], axis, mask))
        if level + 1 < len(masks):
            owns.append(
                call(
                    lambda *refs, level=level: merge_kernel(axis, level, *refs),
                    [owns[-1], others[-1]],
                    vm(NET),
                )
            )
    return owns, others


def local(t, region, source, mag, soft):
    t, region, source = (a.reshape(FIELD) for a in (t, region, source))
    n = lax.axis_size("row")
    up, down = call(edge_kernel, [t, region], (vm((2, Z, N)), vm((2, Z, N))), scalars=(mag, soft))
    south = lax.ppermute(up, "row", [((i + 1) % n, i) for i in range(n)])
    north = lax.ppermute(down, "row", [(i, (i + 1) % n) for i in range(n)])
    ty, cy, r, pr, gr, rr, sep, net = call(
        first_kernel,
        [t, region, source],
        (vm(FIELD),) * 6 + (vm(SEPS), vm(PART)),
        scratch=[vm(FIELD)],
        scalars=(mag, soft),
        flops=20_000_000,
    )
    rd, srd, own = call(
        side_call,
        [r, ty, cy, north, south, pr, gr, rr, sep, net],
        (vm(FIELD), vm(SEPD), vm(NET)),
        scratch=[vm(FIELD), vm(FIELD)],
    )
    ypr, ygr, yrr, ysep, ynet = call(
        factor, [cy], (vm(FIELD),) * 3 + (vm(SEPS), vm(PART)), flops=5_000_000
    )
    owns, others = spread(own, "col", (1, 2, 6, 8))
    yrd, ysrd, own = call(
        lambda *refs: middle_kernel(4, *refs),
        owns + others + [pr, gr, rd, sep, srd, ty, ypr, ygr, yrr, ysep, ynet],
        (vm(FIELD), vm(SEPD), vm(NET)),
        scratch=[vm(FIELD), vm(FIELD)],
    )
    owns, others = spread(own, "row", (1, 2, 6))
    out = call(
        lambda *refs: last_kernel(3, *refs),
        owns + others + [ypr, ygr, yrd, ysep, ysrd, ty],
        jax.ShapeDtypeStruct(FIELD, F32),
    )
    return out.reshape((Z, N, N))


def solution(mesh):
    specs = (P(None, "row", "col"),) * 3 + (P(), P())
    return jax.shard_map(
        local, mesh=mesh, in_specs=specs, out_specs=P(None, "row", "col"), check_vma=False
    )
```

time: 272 us -> 43.9 us (0.16)
  local copies, waits for them, and re-layouts: 107 us -> 2.76 us
  other arithmetic: 77.5 us -> 0 us
  starting transfers between devices: 42 us -> 15.1 us
  blocking collectives: 12.4 us -> 0 us
  waiting for transfers between devices: 29.7 us -> 17.7 us
  Pallas kernels: 0 us -> 7.97 us
    unnamed x61 -> x10, local copies, waits for them, and re-layouts: 37.7 us -> 2.76 us
    all_to_all x5 -> x0, starting transfers between devices: 34.2 us -> none  [the longest x1 11.8 us: across_x(): lax.all_to_all(transfer_coefficient_volume, 'col', split_axis=1, concat_a...]
    add x18 -> x0, other arithmetic: 31.3 us -> none  [the longest x17 29.1 us: reduce_solve(): odds(right_side) + left_factor * evens(right_side)]
    slice x132 -> x0, local copies, waits for them, and re-layouts: 30.5 us -> none  [the longest x78 19 us: following(): lax.slice_in_dim(evens(values), 1, half_length, axis=line_axis)]
    all_to_all x5 -> x0, waiting for transfers between devices: 28.8 us -> none  [the longest x1 11.5 us: local(): lax.all_to_all(half_step, 'col', split_axis=2, concat_axis=1, tiled=True)]
    ppermute x4 -> x9, waiting for transfers between devices: 0.92 us -> 17.7 us  [the longest x7 17.7 us: partner(): lax.ppermute(x, axis, [(i, i ^ mask) for i in range(lax.axis_size(axis))])]
    sub x3 -> x0, other arithmetic: 16.3 us -> none  [the longest x2 15.4 us: line_system(): main_band = 1.0 - lower_band - upper_band]
    all_to_all x4 -> x0, local copies, waits for them, and re-layouts: 15 us -> none  [the longest x2 5.69 us: local(): lax.all_to_all(half_step, 'col', split_axis=2, concat_axis=1, tiled=True)]
  transfers between devices with their start and end apart: 9 -> 9, of which waited for: 4 -> 7; matrix products, arithmetic and copies ran while one was open for 20% -> 0% of each run, Pallas kernels for 0% -> 9%
where the time goes in v1:
time: 43.9 us; the launch traced here: 43.7 us
  waiting for transfers between devices  17.7 us (40%)
  starting transfers between devices  15.1 us (34%)
  Pallas kernels  7.97 us (18%)
  local copies, waits for them, and re-layouts  2.76 us (6%)
    ppermute x7, waiting for transfers between devices, partner(): lax.ppermute(x, axis, [(i, i ^ mask) for i in range(lax.axis_size(axis))])  17.7 us
    ppermute x7, starting transfers between devices, partner(): lax.ppermute(x, axis, [(i, i ^ mask) for i in range(lax.axis_size(axis))])  10.5 us
    pallas_call x11, Pallas kernels, call(): pl.pallas_call(kernel, in_specs=[whole] * len(args) + [small] * len(scala...  7.97 us
    unnamed x10, local copies, waits for them, and re-layouts  2.76 us
    ppermute x1, starting transfers between devices, local(): south = lax.ppermute(up, 'row', [((i + 1) % n, i) for i in range(n)])  2.53 us
    ppermute x1, starting transfers between devices, local(): north = lax.ppermute(down, 'row', [(i, (i + 1) % n) for i in range(n)])  2.07 us
  transfers between devices with their start and end apart: 9, of which 7 were waited for; matrix products, arithmetic and copies ran while one was open for 0% of the time, Pallas kernels for 9%

profile of v1, /device:TPU:0, one launch (start us, length us, event | category | flops | bytes accessed | tf_op | source)
XLA Modules:
  0.0 43.7 jit_solution(816858250041714944)
XLA Ops:
  0.0 0.7 %copy-done.3 = f32[3]{0:T(128)S(1)} copy-done((f32[3]{0:T(128)S(1)}, f32[3]{0:T(128)}, u32[]{:S(2)}) %copy-start.3) | copy-done | bytes 36
  0.7 1.0 %copy-done = f32[8,128,128]{2,1,0:T(8,128)S(1)} copy-done((f32[8,128,128]{2,1,0:T(8,128)S(1)}, f32[8,128,128]{2,1,0:T(8,128)}, u32[]{:S(2)}) %copy-start) | copy-done | bytes 524312
  1.7 1.0 %copy-done.1 = s32[8,128,128]{2,1,0:T(8,128)S(1)} copy-done((s32[8,128,128]{2,1,0:T(8,128)S(1)}, s32[8,128,128]{2,1,0:T(8,128)}, u32[]{:S(2)}) %copy-start.1) | copy-done | bytes 524312
  2.8 0.6 %shard_map.56 = (f32[2,8,128]{2,1,0:T(8,128)S(1)}, f32[2,8,128]{2,1,0:T(8,128)S(1)}) custom-call(f32[1024,128]{1,0:T(8,128)S(1)} %bitcast.4, s32[1024,128]{1,0:T(8,128)S(1)} %bitcast.6, f32[3]{0:T(128)S(1)} %copy-done.3, f32[3]{0:T(128)S(1)} %copy-done.4), custom_call_target="tpu_custom_call" | custom-call | tf_op jit(solution)/shard_map/pallas_call | solution.py:311
  3.3 2.1 %collective-permute-start = (f32[2,8,128]{2,1,0:T(8,128)S(1)}, f32[2,8,128]{2,1,0:T(8,128)S(1)}, u32[]{:S(2)}, u32[]{:S(2)}) collective-permute-start(f32[2,8,128]{2,1,0:T(8,128)S(1)} %get-tuple-element.29), channel_id=1, source_target_pairs={{0,16},{16,32},{32,48},{48,64},{64,80},{80,96},{96,112},{112,0},{1... | collective-permute-start | bytes 24584 | tf_op jit(solution)/shard_map/ppermute | solution.py:346
  5.4 2.5 %collective-permute-start.1 = (f32[2,8,128]{2,1,0:T(8,128)S(1)}, f32[2,8,128]{2,1,0:T(8,128)S(1)}, u32[]{:S(2)}, u32[]{:S(2)}) collective-permute-start(f32[2,8,128]{2,1,0:T(8,128)S(1)} %get-tuple-element.30), channel_id=1, source_target_pairs={{16,0},{32,16},{48,32},{64,48},{80,64},{96,80},{112,96},{0,112},{1... | collective-permute-start | bytes 24584 | tf_op jit(solution)/shard_map/ppermute | solution.py:345
  7.9 3.2 %shard_map.55 = (f32[1024,128]{1,0:T(8,128)S(1)}, f32[1024,128]{1,0:T(8,128)S(1)}, f32[1024,128]{1,0:T(8,128)S(1)}, f32[1024,128]{1,0:T(8,128)S(1)}, f32[1024,12...) custom-call(f32[1024,128]{1,0:T(8,128)S(1)} %bitcast.5, ...), custom_call_target="tpu_custom_call" | custom-call | flops 20000000 | bytes 20000000 | tf_op jit(solution)/shard_map/pallas_call | solution.py:311
  11.2 0.7 %shard_map.57 = (f32[1024,128]{1,0:T(8,128)S(1)}, f32[8,8,128]{2,1,0:T(8,128)S(1)}, f32[7,8,128]{2,1,0:T(8,128)S(1)}) custom-call(f32[1024,128]{1,0:T(8,128)S(1)} %get-tuple-element.26.r_ref, f32[1024,128]{1,0:T(8,128)S(1)} %get-tuple-element.27.ty_ref.refs_13_.refs_11_, f32[1024,128]{1,0:T(8,128)S(1)} %get-tuple-element.28.cy_ref.c_ref, ...), custom_call_target="tpu_custom_call" | custom-call | tf_op jit(solution)/shard_map/pallas_call | solution.py:311
  12.0 1.2 %collective-permute-done.2.refs_1_.refs_4_ = f32[7,8,128]{2,1,0:T(8,128)S(1)} collective-permute-done((f32[7,8,128]{2,1,0:T(8,128)S(1)}, f32[7,8,128]{2,1,0:T(8,128)S(1)}, u32[]{:S(2)}, u32[]{:S(2)}) %collective-permute-start.2) | collective-permute-done | bytes 28704 | tf_op jit(solution)/shard_map/ppermute | solution.py:323
  13.2 1.6 %collective-permute-start.3 = (f32[7,8,128]{2,1,0:T(8,128)S(1)}, f32[7,8,128]{2,1,0:T(8,128)S(1)}, u32[]{:S(2)}, u32[]{:S(2)}) collective-permute-start(f32[7,8,128]{2,1,0:T(8,128)S(1)} %shard_map.58.refs_0_.refs_1_), channel_id=1, source_target_pairs={{0,2},{1,3},{2,0},{3,1},{4,6},{5,7},{6,4},{7,5},{8,10},{9,11},{10,... | collective-permute-start | bytes 86024 | tf_op jit(solution)/shard_map/ppermute | solution.py:323
  14.8 2.4 %collective-permute-done.3.refs_1_.refs_5_ = f32[7,8,128]{2,1,0:T(8,128)S(1)} collective-permute-done((f32[7,8,128]{2,1,0:T(8,128)S(1)}, f32[7,8,128]{2,1,0:T(8,128)S(1)}, u32[]{:S(2)}, u32[]{:S(2)}) %collective-permute-start.3) | collective-permute-done | bytes 28704 | tf_op jit(solution)/shard_map/ppermute | solution.py:323
  17.2 2.8 %collective-permute-start.4 = (f32[7,8,128]{2,1,0:T(8,128)S(1)}, f32[7,8,128]{2,1,0:T(8,128)S(1)}, u32[]{:S(2)}, u32[]{:S(2)}) collective-permute-start(f32[7,8,128]{2,1,0:T(8,128)S(1)} %shard_map.59.refs_0_.refs_2_), channel_id=1, source_target_pairs={{0,6},{1,7},{2,4},{3,5},{4,2},{5,3},{6,0},{7,1},{8,14},{9,15},{10,... | collective-permute-start | bytes 86024 | tf_op jit(solution)/shard_map/ppermute | solution.py:323
  20.0 2.3 %collective-permute-done.4.refs_1_.refs_6_ = f32[7,8,128]{2,1,0:T(8,128)S(1)} collective-permute-done((f32[7,8,128]{2,1,0:T(8,128)S(1)}, f32[7,8,128]{2,1,0:T(8,128)S(1)}, u32[]{:S(2)}, u32[]{:S(2)}) %collective-permute-start.4) | collective-permute-done | bytes 28704 | tf_op jit(solution)/shard_map/ppermute | solution.py:323
  22.4 3.7 %collective-permute-start.5 = (f32[7,8,128]{2,1,0:T(8,128)S(1)}, f32[7,8,128]{2,1,0:T(8,128)S(1)}, u32[]{:S(2)}, u32[]{:S(2)}) collective-permute-start(f32[7,8,128]{2,1,0:T(8,128)S(1)} %shard_map.60.refs_3_), channel_id=1, source_target_pairs={{0,8},{1,9},{2,10},{3,11},{4,12},{5,13},{6,14},{7,15},{8,0},{9,1},... | collective-permute-start | bytes 86024 | tf_op jit(solution)/shard_map/ppermute | solution.py:323
  26.1 0.7 %shard_map.61 = (f32[1024,128]{1,0:T(8,128)S(1)}, f32[1024,128]{1,0:T(8,128)S(1)}, f32[1024,128]{1,0:T(8,128)S(1)}, f32[3,8,8,128]{3,2,1,0:T(8,128)S(1)}, f32[5,8,128]{2,1,0:T(8,128)S(1)}) custom-call(f32[1024,128]{1,0:T(8,128)S(1)} %get-tuple-element.28.cy_ref.c_ref), custom_call_target="tpu_custom_call" | custom-call | flops 5000000 | bytes 5000000 | tf_op jit(solution)/shard_map/pallas_call | solution.py:311
  26.8 1.1 %collective-permute-done.5.refs_7_ = f32[7,8,128]{2,1,0:T(8,128)S(1)} collective-permute-done((f32[7,8,128]{2,1,0:T(8,128)S(1)}, f32[7,8,128]{2,1,0:T(8,128)S(1)}, u32[]{:S(2)}, u32[]{:S(2)}) %collective-permute-start.5) | collective-permute-done | bytes 28704 | tf_op jit(solution)/shard_map/ppermute | solution.py:323
  27.9 1.1 %shard_map.62 = (f32[1024,128]{1,0:T(8,128)S(1)}, f32[8,8,128]{2,1,0:T(8,128)S(1)}, f32[7,8,128]{2,1,0:T(8,128)S(1)}) custom-call(f32[7,8,128]{2,1,0:T(8,128)S(1)} %get-tuple-element.36.refs_0_, f32[7,8,128]{2,1,0:T(8,128)S(1)} %shard_map.58.refs_0_.refs_1_, f32[7,8,128]{2,1,0:T(8,128)S(1)} %shard_map.59.refs_0_.refs_2_, ...), custom_call_target="tpu_custom_call" | custom-call | tf_op jit(solution)/shard_map/pallas_call | solution.py:311
  29.1 0.1 collective-permute-start.6
  29.2 3.9 %collective-permute-done.6.refs_1_.refs_3_ = f32[7,8,128]{2,1,0:T(8,128)S(1)} collective-permute-done((f32[7,8,128]{2,1,0:T(8,128)S(1)}, f32[7,8,128]{2,1,0:T(8,128)S(1)}, u32[]{:S(2)}, u32[]{:S(2)}) %collective-permute-start.6) | collective-permute-done | bytes 28704 | tf_op jit(solution)/shard_map/ppermute | solution.py:323
  33.1 0.4 collective-permute-start.7
  33.5 3.5 %collective-permute-done.7.refs_1_.refs_4_ = f32[7,8,128]{2,1,0:T(8,128)S(1)} collective-permute-done((f32[7,8,128]{2,1,0:T(8,128)S(1)}, f32[7,8,128]{2,1,0:T(8,128)S(1)}, u32[]{:S(2)}, u32[]{:S(2)}) %collective-permute-start.7) | collective-permute-done | bytes 28704 | tf_op jit(solution)/shard_map/ppermute | solution.py:323
  37.0 1.9 %collective-permute-start.8 = (f32[7,8,128]{2,1,0:T(8,128)S(1)}, f32[7,8,128]{2,1,0:T(8,128)S(1)}, u32[]{:S(2)}, u32[]{:S(2)}) collective-permute-start(f32[7,8,128]{2,1,0:T(8,128)S(1)} %shard_map.64.refs_2_), channel_id=1, source_target_pairs={{0,96},{16,112},{32,64},{48,80},{64,32},{80,48},{96,0},{112,16},{1... | collective-permute-start | bytes 86024 | tf_op jit(solution)/shard_map/ppermute | solution.py:323
  38.9 3.3 %collective-permute-done.8.refs_5_ = f32[7,8,128]{2,1,0:T(8,128)S(1)} collective-permute-done((f32[7,8,128]{2,1,0:T(8,128)S(1)}, f32[7,8,128]{2,1,0:T(8,128)S(1)}, u32[]{:S(2)}, u32[]{:S(2)}) %collective-permute-start.8) | collective-permute-done | bytes 28704 | tf_op jit(solution)/shard_map/ppermute | solution.py:323
  42.2 1.5 %shard_map.65 = f32[1024,128]{1,0:T(8,128)} custom-call(f32[7,8,128]{2,1,0:T(8,128)S(1)} %get-tuple-element.44.refs_0_, f32[7,8,128]{2,1,0:T(8,128)S(1)} %shard_map.63.refs_0_.refs_1_, f32[7,8,128]{2,1,0:T(8,128)S(1)} %shard_map.64.refs_2_, f32[7,8,128]{2,1,0:T(8,128)S(1)} %collective-permute-done.6.refs_1_.refs_3_, ...), custom_call_target="tpu_custom_call" | custom-call | tf_op jit(solution)/shard_map/pallas_call | solution.py:311
  (15 shorter events, 0.3 us)
Async XLA Ops:
  0.0 0.7 %copy-start.3 = (f32[3]{0:T(128)S(1)}, f32[3]{0:T(128)}, u32[]{:S(2)}) copy-start(f32[3]{0:T(128)} %mag.3) | copy-start | bytes 40
  0.0 0.7 %copy-start.4 = (f32[3]{0:T(128)S(1)}, f32[3]{0:T(128)}, u32[]{:S(2)}) copy-start(f32[3]{0:T(128)} %soft.3) | copy-start | bytes 40
  0.7 1.0 %copy-start = (f32[8,128,128]{2,1,0:T(8,128)S(1)}, f32[8,128,128]{2,1,0:T(8,128)}, u32[]{:S(2)}) copy-start(f32[8,128,128]{2,1,0:T(8,128)} %param.5) | copy-start | bytes 1572868
  1.7 1.0 %copy-start.1 = (s32[8,128,128]{2,1,0:T(8,128)S(1)}, s32[8,128,128]{2,1,0:T(8,128)}, u32[]{:S(2)}) copy-start(s32[8,128,128]{2,1,0:T(8,128)} %param.6) | copy-start | bytes 1572868
  2.8 5.2 %copy-start.2 = (f32[8,128,128]{2,1,0:T(8,128)S(1)}, f32[8,128,128]{2,1,0:T(8,128)}, u32[]{:S(2)}) copy-start(f32[8,128,128]{2,1,0:T(8,128)} %param.7) | copy-start | bytes 1572868
  3.3 7.8 %collective-permute-start = (f32[2,8,128]{2,1,0:T(8,128)S(1)}, f32[2,8,128]{2,1,0:T(8,128)S(1)}, u32[]{:S(2)}, u32[]{:S(2)}) collective-permute-start(f32[2,8,128]{2,1,0:T(8,128)S(1)} %get-tuple-element.29), channel_id=1, source_target_pairs={{0,16},{16,32},{32,48},{48,64},{64,80},{80,96},{96,112},{112,0},{1... | collective-permute-start | bytes 24584 | tf_op jit(solution)/shard_map/ppermute | solution.py:346
  5.4 5.8 %collective-permute-start.1 = (f32[2,8,128]{2,1,0:T(8,128)S(1)}, f32[2,8,128]{2,1,0:T(8,128)S(1)}, u32[]{:S(2)}, u32[]{:S(2)}) collective-permute-start(f32[2,8,128]{2,1,0:T(8,128)S(1)} %get-tuple-element.30), channel_id=1, source_target_pairs={{16,0},{32,16},{48,32},{64,48},{80,64},{96,80},{112,96},{0,112},{1... | collective-permute-start | bytes 24584 | tf_op jit(solution)/shard_map/ppermute | solution.py:345
  11.9 1.3 %collective-permute-start.2 = (f32[7,8,128]{2,1,0:T(8,128)S(1)}, f32[7,8,128]{2,1,0:T(8,128)S(1)}, u32[]{:S(2)}, u32[]{:S(2)}) collective-permute-start(f32[7,8,128]{2,1,0:T(8,128)S(1)} %get-tuple-element.36.refs_0_), channel_id=1, source_target_pairs={{0,1},{1,0},{2,3},{3,2},{4,5},{5,4},{6,7},{7,6},{8,9},{9,8},{10,11... | collective-permute-start | bytes 86024 | tf_op jit(solution)/shard_map/ppermute | solution.py:323
  13.2 4.0 %collective-permute-start.3 = (f32[7,8,128]{2,1,0:T(8,128)S(1)}, f32[7,8,128]{2,1,0:T(8,128)S(1)}, u32[]{:S(2)}, u32[]{:S(2)}) collective-permute-start(f32[7,8,128]{2,1,0:T(8,128)S(1)} %shard_map.58.refs_0_.refs_1_), channel_id=1, source_target_pairs={{0,2},{1,3},{2,0},{3,1},{4,6},{5,7},{6,4},{7,5},{8,10},{9,11},{10,... | collective-permute-start | bytes 86024 | tf_op jit(solution)/shard_map/ppermute | solution.py:323
  17.2 5.2 %collective-permute-start.4 = (f32[7,8,128]{2,1,0:T(8,128)S(1)}, f32[7,8,128]{2,1,0:T(8,128)S(1)}, u32[]{:S(2)}, u32[]{:S(2)}) collective-permute-start(f32[7,8,128]{2,1,0:T(8,128)S(1)} %shard_map.59.refs_0_.refs_2_), channel_id=1, source_target_pairs={{0,6},{1,7},{2,4},{3,5},{4,2},{5,3},{6,0},{7,1},{8,14},{9,15},{10,... | collective-permute-start | bytes 86024 | tf_op jit(solution)/shard_map/ppermute | solution.py:323
  22.4 5.5 %collective-permute-start.5 = (f32[7,8,128]{2,1,0:T(8,128)S(1)}, f32[7,8,128]{2,1,0:T(8,128)S(1)}, u32[]{:S(2)}, u32[]{:S(2)}) collective-permute-start(f32[7,8,128]{2,1,0:T(8,128)S(1)} %shard_map.60.refs_3_), channel_id=1, source_target_pairs={{0,8},{1,9},{2,10},{3,11},{4,12},{5,13},{6,14},{7,15},{8,0},{9,1},... | collective-permute-start | bytes 86024 | tf_op jit(solution)/shard_map/ppermute | solution.py:323
  29.1 3.9 %collective-permute-start.6 = (f32[7,8,128]{2,1,0:T(8,128)S(1)}, f32[7,8,128]{2,1,0:T(8,128)S(1)}, u32[]{:S(2)}, u32[]{:S(2)}) collective-permute-start(f32[7,8,128]{2,1,0:T(8,128)S(1)} %get-tuple-element.44.refs_0_), channel_id=1, source_target_pairs={{0,16},{16,0},{32,48},{48,32},{64,80},{80,64},{96,112},{112,96},{1... | collective-permute-start | bytes 86024 | tf_op jit(solution)/shard_map/ppermute | solution.py:323
  33.1 4.0 %collective-permute-start.7 = (f32[7,8,128]{2,1,0:T(8,128)S(1)}, f32[7,8,128]{2,1,0:T(8,128)S(1)}, u32[]{:S(2)}, u32[]{:S(2)}) collective-permute-start(f32[7,8,128]{2,1,0:T(8,128)S(1)} %shard_map.63.refs_0_.refs_1_), channel_id=1, source_target_pairs={{0,32},{16,48},{32,0},{48,16},{64,96},{80,112},{96,64},{112,80},{1... | collective-permute-start | bytes 86024 | tf_op jit(solution)/shard_map/ppermute | solution.py:323
  37.0 5.2 %collective-permute-start.8 = (f32[7,8,128]{2,1,0:T(8,128)S(1)}, f32[7,8,128]{2,1,0:T(8,128)S(1)}, u32[]{:S(2)}, u32[]{:S(2)}) collective-permute-start(f32[7,8,128]{2,1,0:T(8,128)S(1)} %shard_map.64.refs_2_), channel_id=1, source_target_pairs={{0,96},{16,112},{32,64},{48,80},{64,32},{80,48},{96,0},{112,16},{1... | collective-permute-start | bytes 86024 | tf_op jit(solution)/shard_map/ppermute | solution.py:323

commit v2 on v1

--- a/solution.py
+++ b/solution.py
@@ -30,9 +30,9 @@
 
 
 def conductivity(t, reg, mag, soft):
-    m = jnp.where(reg == 0, mag[0] * 1000.0, jnp.where(reg == 1, mag[1] * 1000.0, mag[2] * 1000.0))
+    m = jnp.where(reg == 0, mag[0], jnp.where(reg == 1, mag[1], mag[2]))
     b = jnp.where(reg == 0, soft[0], jnp.where(reg == 1, soft[1], soft[2]))
-    return m * jnp.exp(-(b * t))
+    return m * jnp.exp(b * t)
 
 
 def turn(src, dst):
@@ -185,17 +185,38 @@
     return ul, ur
 
 
-def edge_kernel(t_ref, reg_ref, mag, soft, up_ref, down_ref):
+def edge_kernel(
+    t_hbm, reg_hbm, s_hbm, mag_hbm, soft_hbm,
+    t_ref, reg_ref, s_ref, up_ref, down_ref, par_ref, mag_ref, soft_ref, sem,
+):
+    pairs = (
+        (mag_hbm, mag_ref), (soft_hbm, soft_ref), (t_hbm, t_ref), (reg_hbm, reg_ref), (s_hbm, s_ref),
+    )
+    copies = [pltpu.make_async_copy(a, b, sem.at[k]) for k, (a, b) in enumerate(pairs)]
+    for copy in copies:
+        copy.start()
+    copies[0].wait()
+    copies[1].wait()
+    mag = [jnp.full((Z, N), mag_ref[k] * 1000.0) for k in range(3)]
+    soft = [jnp.full((Z, N), -soft_ref[k]) for k in range(3)]
+    for k in range(3):
+        par_ref[k] = mag[k]
+        par_ref[3 + k] = soft[k]
+    copies[2].wait()
+    copies[3].wait()
     for row, out in ((0, up_ref), (N - 1, down_ref)):
         t = t_ref[strided(row), :]
         out[0] = t
         out[1] = conductivity(t, reg_ref[strided(row), :], mag, soft)
+    copies[4].wait()
 
 
 def first_kernel(
-    t_ref, reg_ref, s_ref, mag, soft,
+    t_ref, reg_ref, s_ref, par_ref,
     ty_ref, cy_ref, r_ref, pr_ref, gr_ref, rr_ref, sep_ref, net_ref, cx_ref,
 ):
+    mag = [par_ref[k] for k in range(3)]
+    soft = [par_ref[3 + k] for k in range(3)]
     z = lax.broadcasted_iota(jnp.int32, (Z, N), 0)
     inner = jnp.where(z < Z - 1, 1.6e-4, 0.0)
     ground = jnp.where(z == 0, 8e-5, 0.0)
@@ -252,11 +273,46 @@
     )
 
 
-def merge_kernel(axis, level, own_ref, other_ref, out_ref):
-    left = (lax.axis_index(axis) >> level) % 2 == 0
+def merge_kernel(axis, own_ref, other_ref, out_ref):
+    left = lax.axis_index(axis) % 2 == 0
     new = joined([own_ref[k] for k in range(7)], [other_ref[k] for k in range(7)], left)
     for k in range(7):
         out_ref[k] = new[k]
+
+
+def ring_kernel(axis, own_ref, before_ref, after_ref, across_ref, *outs):
+    place = lax.axis_index(axis) // 2 % 4
+    even = place % 2 == 0
+    own, before, after, across = (
+        [r[k] for k in range(7)] for r in (own_ref, before_ref, after_ref, across_ref)
+    )
+    near = [jnp.where(even, a, b) for a, b in zip(after, before)]
+    far = [jnp.where(even, b, a) for a, b in zip(after, before)]
+    pair = joined(own, near, even)
+    rest = joined(across, far, even)
+    every = joined(pair, rest, place < 2)
+    for out, net in zip(outs, (near, pair, rest, every)):
+        for k in range(7):
+            out[k] = net[k]
+
+
+def gather_kernel(net_ref, out_ref):
+    for b in range(8):
+        out_ref[b] = net_ref[...]
+
+
+def tree_kernel(axis, all_ref, *outs):
+    me = lax.axis_index(axis)
+    own = [all_ref[me, k] for k in range(7)]
+    place = lambda m: [all_ref[me ^ m, k] for k in range(7)]
+    l0, l1, l2 = (me >> 0) % 2 == 0, (me >> 1) % 2 == 0, (me >> 2) % 2 == 0
+    own1 = joined(own, place(1), l0)
+    far1 = joined(place(2), place(3), l0)
+    own2 = joined(own1, far1, l1)
+    far2 = joined(joined(place(4), place(5), l0), joined(place(6), place(7), l0), l1)
+    for out, net in zip(outs, (place(1), own1, far1, own2, far2)):
+        for k in range(7):
+            out[k] = net[k]
 
 
 def middle_kernel(
@@ -303,53 +359,68 @@
     return VM(shape, F32)
 
 
-def call(kernel, args, outs, scratch=(), scalars=(), flops=0, inplace=None):
+def call(kernel, args, outs, scratch=(), flops=0):
     args = [pltpu.with_memory_space_constraint(a, VM) for a in args]
     whole = pl.BlockSpec(memory_space=VM)
-    small = pl.BlockSpec(memory_space=pltpu.SMEM)
     many = isinstance(outs, tuple)
     return pl.pallas_call(
         kernel,
-        in_specs=[whole] * len(args) + [small] * len(scalars),
+        in_specs=[whole] * len(args),
         out_specs=(whole,) * len(outs) if many else whole,
         out_shape=outs,
         scratch_shapes=list(scratch),
         cost_estimate=pl.CostEstimate(flops=flops, bytes_accessed=flops, transcendentals=0),
         compiler_params=pltpu.CompilerParams(vmem_limit_bytes=16 * 1024 * 1024),
-    )(*args, *scalars)
+    )(*args)
 
 
 def partner(x, axis, mask):
     return lax.ppermute(x, axis, [(i, i ^ mask) for i in range(lax.axis_size(axis))])
 
 
-def spread(net, axis, masks):
-    owns, others = [net], []
-    for level, mask in enumerate(masks):
-        others.append(partner(owns[-1], axis, mask))
-        if level + 1 < len(masks):
-            owns.append(
-                call(
-                    lambda *refs, level=level: merge_kernel(axis, level, *refs),
-                    [owns[-1], others[-1]],
-                    vm(NET),
-                )
-            )
-    return owns, others
+def around(x, axis, shift):
+    n = lax.axis_size(axis)
+    to = lambda i: i // 8 * 8 + (i // 2 + shift) % 4 * 2 + i % 2
+    return lax.ppermute(x, axis, [(i, to(i)) for i in range(n)])
+
+
+def spread_col(net, axis):
+    owns, others = [net], [partner(net, axis, 1)]
+    own = call(lambda *refs: merge_kernel(axis, *refs), [net, others[0]], vm(NET))
+    near, pair, rest, every = call(
+        lambda *refs: ring_kernel(axis, *refs),
+        [own, around(own, axis, 1), around(own, axis, 3), around(own, axis, 2)],
+        (vm(NET),) * 4,
+    )
+    return [net, own, pair, every], others + [near, rest, partner(every, axis, 8)]
+
+
+def spread_row(net, axis):
+    send = call(gather_kernel, [net], vm((8,) + NET))
+    got = lax.all_to_all(send, axis, 0, 0, tiled=True)
+    near, own1, far1, own2, far2 = call(lambda *refs: tree_kernel(axis, *refs), [got], (vm(NET),) * 5)
+    return [net, own1, own2], [near, far1, far2]
 
 
 def local(t, region, source, mag, soft):
     t, region, source = (a.reshape(FIELD) for a in (t, region, source))
     n = lax.axis_size("row")
-    up, down = call(edge_kernel, [t, region], (vm((2, Z, N)), vm((2, Z, N))), scalars=(mag, soft))
+    t, region, source, up, down, par = pl.pallas_call(
+        edge_kernel,
+        in_specs=[pl.BlockSpec(memory_space=pl.ANY)] * 5,
+        out_specs=(pl.BlockSpec(memory_space=VM),) * 6,
+        out_shape=(vm(FIELD), VM(FIELD, jnp.int32), vm(FIELD), vm((2, Z, N)), vm((2, Z, N)), vm((6, Z, N))),
+        scratch_shapes=[
+            pltpu.SMEM((3,), F32), pltpu.SMEM((3,), F32), pltpu.SemaphoreType.DMA((5,)),
+        ],
+    )(t, region, source, mag, soft)
     south = lax.ppermute(up, "row", [((i + 1) % n, i) for i in range(n)])
     north = lax.ppermute(down, "row", [(i, (i + 1) % n) for i in range(n)])
     ty, cy, r, pr, gr, rr, sep, net = call(
         first_kernel,
-        [t, region, source],
+        [t, region, source, par],
         (vm(FIELD),) * 6 + (vm(SEPS), vm(PART)),
         scratch=[vm(FIELD)],
-        scalars=(mag, soft),
         flops=20_000_000,
     )
     rd, srd, own = call(
@@ -361,14 +432,14 @@
     ypr, ygr, yrr, ysep, ynet = call(
         factor, [cy], (vm(FIELD),) * 3 + (vm(SEPS), vm(PART)), flops=5_000_000
     )
-    owns, others = spread(own, "col", (1, 2, 6, 8))
+    owns, others = spread_col(own, "col")
     yrd, ysrd, own = call(
         lambda *refs: middle_kernel(4, *refs),
         owns + others + [pr, gr, rd, sep, srd, ty, ypr, ygr, yrr, ysep, ynet],
         (vm(FIELD), vm(SEPD), vm(NET)),
         scratch=[vm(FIELD), vm(FIELD)],
     )
-    owns, others = spread(own, "row", (1, 2, 6))
+    owns, others = spread_row(own, "row")
     out = call(
         lambda *refs: last_kernel(3, *refs),
         owns + others + [ypr, ygr, yrd, ysep, ysrd, ty],

time: 43.9 us -> 39.4 us (0.90)
  waiting for transfers between devices: 17.7 us -> 6.53 us
  blocking collectives: 0 us -> 10.9 us
  local copies, waits for them, and re-layouts: 2.76 us -> 0 us
  starting transfers between devices: 15.1 us -> 13.5 us
    ppermute x7 -> x2, waiting for transfers between devices: 17.7 us -> 2.33 us  [partner(): lax.ppermute(x, axis, [(i, i ^ mask) for i in range(lax.axis_size(axis))])]
    all_to_all x0 -> x1, blocking collectives: none -> 10.9 us  [spread_row(): got = lax.all_to_all(send, axis, 0, 0, tiled=True)]
    ppermute x7 -> x2, starting transfers between devices: 10.5 us -> 3.75 us  [partner(): lax.ppermute(x, axis, [(i, i ^ mask) for i in range(lax.axis_size(axis))])]
    ppermute x0 -> x3, starting transfers between devices: none -> 5.13 us  [around(): return lax.ppermute(x, axis, [(i, to(i)) for i in range(n)])]
    ppermute x0 -> x3, waiting for transfers between devices: none -> 4.19 us  [around(): return lax.ppermute(x, axis, [(i, to(i)) for i in range(n)])]
    unnamed x10 -> x0, local copies, waits for them, and re-layouts: 2.76 us -> none
    pallas_call x11 -> x10, Pallas kernels: 7.97 us -> 8.26 us  [the longest x9 6.86 us: call(): pl.pallas_call(kernel, in_specs=[whole] * len(args), out_specs=(whole,) *...]
  transfers between devices with their start and end apart: 9 -> 7, of which waited for: 7 -> 5; matrix products, arithmetic and copies ran while one was open for 0% -> 0% of each run, Pallas kernels for 9% -> 8%
where the time goes in v2:
time: 39.4 us; the launch traced here: 39.3 us
  starting transfers between devices  13.5 us (34%)
  blocking collectives  10.9 us (28%)
  Pallas kernels  8.26 us (21%)
  waiting for transfers between devices  6.53 us (17%)
    all_to_all x1, blocking collectives, spread_row(): got = lax.all_to_all(send, axis, 0, 0, tiled=True)  10.9 us
    pallas_call x9, Pallas kernels, call(): pl.pallas_call(kernel, in_specs=[whole] * len(args), out_specs=(whole,) *...  6.86 us
    ppermute x3, starting transfers between devices, around(): return lax.ppermute(x, axis, [(i, to(i)) for i in range(n)])  5.13 us
    ppermute x3, waiting for transfers between devices, around(): return lax.ppermute(x, axis, [(i, to(i)) for i in range(n)])  4.19 us
    ppermute x2, starting transfers between devices, partner(): lax.ppermute(x, axis, [(i, i ^ mask) for i in range(lax.axis_size(axis))])  3.75 us
    ppermute x1, starting transfers between devices, local(): south = lax.ppermute(up, 'row', [((i + 1) % n, i) for i in range(n)])  2.53 us
    ppermute x2, waiting for transfers between devices, partner(): lax.ppermute(x, axis, [(i, i ^ mask) for i in range(lax.axis_size(axis))])  2.33 us
    ppermute x1, starting transfers between devices, local(): north = lax.ppermute(down, 'row', [(i, (i + 1) % n) for i in range(n)])  2.07 us
  transfers between devices with their start and end apart: 7, of which 5 were waited for; matrix products, arithmetic and copies ran while one was open for 0% of the time, Pallas kernels for 8%

profile of v2, /device:TPU:0, one launch (start us, length us, event | category | flops | bytes accessed | tf_op | source)
XLA Modules:
  0.0 39.3 jit_solution(6992715873486861886)
XLA Ops:
  0.0 1.4 %shard_map.55 = (f32[1024,128]{1,0:T(8,128)S(1)}, s32[1024,128]{1,0:T(8,128)S(1)}, f32[1024,128]{1,0:T(8,128)S(1)}, f32[2,8,128]{2,1,0:T(8,128)S(1)}, f32[2,8,12...) custom-call(f32[1024,128]{1,0:T(8,128)} %bitcast.4, s32[1024,128]{1,0:T(8,128)} %bitcast.5, f32[1024,128]{1,0:T(8,128)} %bitcast.6, ...), custom_call_target="tpu_custom_call" | custom-call | tf_op jit(solution)/shard_map/pallas_call | solution.py:408
  1.4 2.1 %collective-permute-start = (f32[2,8,128]{2,1,0:T(8,128)S(1)}, f32[2,8,128]{2,1,0:T(8,128)S(1)}, u32[]{:S(2)}, u32[]{:S(2)}) collective-permute-start(f32[2,8,128]{2,1,0:T(8,128)S(1)} %get-tuple-element.46), channel_id=1, source_target_pairs={{0,16},{16,32},{32,48},{48,64},{64,80},{80,96},{96,112},{112,0},{1... | collective-permute-start | bytes 24584 | tf_op jit(solution)/shard_map/ppermute | solution.py:418
  3.5 2.5 %collective-permute-start.1 = (f32[2,8,128]{2,1,0:T(8,128)S(1)}, f32[2,8,128]{2,1,0:T(8,128)S(1)}, u32[]{:S(2)}, u32[]{:S(2)}) collective-permute-start(f32[2,8,128]{2,1,0:T(8,128)S(1)} %get-tuple-element.47), channel_id=1, source_target_pairs={{16,0},{32,16},{48,32},{64,48},{80,64},{96,80},{112,96},{0,112},{1... | collective-permute-start | bytes 24584 | tf_op jit(solution)/shard_map/ppermute | solution.py:417
  6.0 2.6 %shard_map.56 = (f32[1024,128]{1,0:T(8,128)S(1)}, f32[1024,128]{1,0:T(8,128)S(1)}, f32[1024,128]{1,0:T(8,128)S(1)}, f32[1024,128]{1,0:T(8,128)S(1)}, f32[1024,12...) custom-call(f32[1024,128]{1,0:T(8,128)S(1)} %get-tuple-element.39.t_ref, ...), custom_call_target="tpu_custom_call" | custom-call | flops 20000000 | bytes 20000000 | tf_op jit(solution)/shard_map/pallas_call | solution.py:366
  8.6 0.0 collective-permute-done.north_ref
  8.6 0.0 collective-permute-done.1.south_ref
  8.6 0.7 %shard_map.57 = (f32[1024,128]{1,0:T(8,128)S(1)}, f32[8,8,128]{2,1,0:T(8,128)S(1)}, f32[7,8,128]{2,1,0:T(8,128)S(1)}) custom-call(f32[1024,128]{1,0:T(8,128)S(1)} %get-tuple-element.43.r_ref, f32[1024,128]{1,0:T(8,128)S(1)} %get-tuple-element.44.ty_ref.refs_13_.refs_11_, f32[1024,128]{1,0:T(8,128)S(1)} %get-tuple-element.45.cy_ref.c_ref, ...), custom_call_target="tpu_custom_call" | custom-call | tf_op jit(solution)/shard_map/pallas_call | solution.py:366
  9.4 0.1 collective-permute-start.2
  9.5 1.2 %collective-permute-done.2.refs_1_.refs_4_ = f32[7,8,128]{2,1,0:T(8,128)S(1)} collective-permute-done((f32[7,8,128]{2,1,0:T(8,128)S(1)}, f32[7,8,128]{2,1,0:T(8,128)S(1)}, u32[]{:S(2)}, u32[]{:S(2)}) %collective-permute-start.2) | collective-permute-done | bytes 28704 | tf_op jit(solution)/shard_map/ppermute | solution.py:378
  10.7 3.1 %collective-permute-start.5 = (f32[7,8,128]{2,1,0:T(8,128)S(1)}, f32[7,8,128]{2,1,0:T(8,128)S(1)}, u32[]{:S(2)}, u32[]{:S(2)}) collective-permute-start(f32[7,8,128]{2,1,0:T(8,128)S(1)} %shard_map.58.refs_0_.refs_1_), channel_id=1, source_target_pairs={{0,4},{1,5},{2,6},{3,7},{4,0},{5,1},{6,2},{7,3},{8,12},{9,13},{10,... | collective-permute-start | bytes 86024 | tf_op jit(solution)/shard_map/ppermute | solution.py:384
  13.8 1.1 %collective-permute-start.4 = (f32[7,8,128]{2,1,0:T(8,128)S(1)}, f32[7,8,128]{2,1,0:T(8,128)S(1)}, u32[]{:S(2)}, u32[]{:S(2)}) collective-permute-start(f32[7,8,128]{2,1,0:T(8,128)S(1)} %shard_map.58.refs_0_.refs_1_), channel_id=1, source_target_pairs={{0,6},{1,7},{2,0},{3,1},{4,2},{5,3},{6,4},{7,5},{8,14},{9,15},{10,... | collective-permute-start | bytes 86024 | tf_op jit(solution)/shard_map/ppermute | solution.py:384
  14.9 0.9 %collective-permute-start.3 = (f32[7,8,128]{2,1,0:T(8,128)S(1)}, f32[7,8,128]{2,1,0:T(8,128)S(1)}, u32[]{:S(2)}, u32[]{:S(2)}) collective-permute-start(f32[7,8,128]{2,1,0:T(8,128)S(1)} %shard_map.58.refs_0_.refs_1_), channel_id=1, source_target_pairs={{0,2},{1,3},{2,4},{3,5},{4,6},{5,7},{6,0},{7,1},{8,10},{9,11},{10,... | collective-permute-start | bytes 86024 | tf_op jit(solution)/shard_map/ppermute | solution.py:384
  15.8 0.3 collective-permute-done.5.refs_3_
  16.2 1.5 %collective-permute-done.4.refs_2_ = f32[7,8,128]{2,1,0:T(8,128)S(1)} collective-permute-done((f32[7,8,128]{2,1,0:T(8,128)S(1)}, f32[7,8,128]{2,1,0:T(8,128)S(1)}, u32[]{:S(2)}, u32[]{:S(2)}) %collective-permute-start.4) | collective-permute-done | bytes 28704 | tf_op jit(solution)/shard_map/ppermute | solution.py:384
  17.7 2.4 %collective-permute-done.3.refs_1_ = f32[7,8,128]{2,1,0:T(8,128)S(1)} collective-permute-done((f32[7,8,128]{2,1,0:T(8,128)S(1)}, f32[7,8,128]{2,1,0:T(8,128)S(1)}, u32[]{:S(2)}, u32[]{:S(2)}) %collective-permute-start.3) | collective-permute-done | bytes 28704 | tf_op jit(solution)/shard_map/ppermute | solution.py:384
  20.0 0.1 shard_map.59
  20.1 3.7 %collective-permute-start.6 = (f32[7,8,128]{2,1,0:T(8,128)S(1)}, f32[7,8,128]{2,1,0:T(8,128)S(1)}, u32[]{:S(2)}, u32[]{:S(2)}) collective-permute-start(f32[7,8,128]{2,1,0:T(8,128)S(1)} %get-tuple-element.55.refs_3_), channel_id=1, source_target_pairs={{0,8},{1,9},{2,10},{3,11},{4,12},{5,13},{6,14},{7,15},{8,0},{9,1},... | collective-permute-start | bytes 86024 | tf_op jit(solution)/shard_map/ppermute | solution.py:378
  23.8 0.7 %shard_map.60 = (f32[1024,128]{1,0:T(8,128)S(1)}, f32[1024,128]{1,0:T(8,128)S(1)}, f32[1024,128]{1,0:T(8,128)S(1)}, f32[3,8,8,128]{3,2,1,0:T(8,128)S(1)}, f32[5,8,128]{2,1,0:T(8,128)S(1)}) custom-call(f32[1024,128]{1,0:T(8,128)S(1)} %get-tuple-element.45.cy_ref.c_ref), custom_call_target="tpu_custom_call" | custom-call | flops 5000000 | bytes 5000000 | tf_op jit(solution)/shard_map/pallas_call | solution.py:366
  24.5 1.1 %collective-permute-done.6.refs_7_ = f32[7,8,128]{2,1,0:T(8,128)S(1)} collective-permute-done((f32[7,8,128]{2,1,0:T(8,128)S(1)}, f32[7,8,128]{2,1,0:T(8,128)S(1)}, u32[]{:S(2)}, u32[]{:S(2)}) %collective-permute-start.6) | collective-permute-done | bytes 28704 | tf_op jit(solution)/shard_map/ppermute | solution.py:378
  25.6 1.1 %shard_map.61 = (f32[1024,128]{1,0:T(8,128)S(1)}, f32[8,8,128]{2,1,0:T(8,128)S(1)}, f32[7,8,128]{2,1,0:T(8,128)S(1)}) custom-call(f32[7,8,128]{2,1,0:T(8,128)S(1)} %get-tuple-element.53.refs_0_, f32[7,8,128]{2,1,0:T(8,128)S(1)} %shard_map.58.refs_0_.refs_1_, f32[7,8,128]{2,1,0:T(8,128)S(1)} %get-tuple-element.54.refs_2_, ...), custom_call_target="tpu_custom_call" | custom-call | tf_op jit(solution)/shard_map/pallas_call | solution.py:366
  26.8 10.9 %all_to_all.5.refs_0_ = f32[8,7,8,128]{3,2,1,0:T(8,128)S(1)} all-to-all(f32[8,7,8,128]{3,2,1,0:T(8,128)S(1)} %shard_map.62), channel_id=1, replica_groups=mesh['row'=8,'col'=16] {'row'}, dimensions={0} | all-to-all | bytes 458752 | tf_op jit(solution)/shard_map/all_to_all | solution.py:400
  37.7 0.1 shard_map.63
  37.8 1.5 %shard_map.64 = f32[1024,128]{1,0:T(8,128)} custom-call(f32[7,8,128]{2,1,0:T(8,128)S(1)} %get-tuple-element.65.net_ref.refs_0_, f32[7,8,128]{2,1,0:T(8,128)S(1)} %get-tuple-element.66.refs_1_, f32[7,8,128]{2,1,0:T(8,128)S(1)} %get-tuple-element.67.refs_2_, f32[7,8,128]{2,1,0:T(8,128)S(1)} %get-tuple-element.68.refs_3_, ...), custom_call_target="tpu_custom_call" | custom-call | tf_op jit(solution)/shard_map/pallas_call | solution.py:366
  (2 shorter events, 0.1 us)
Async XLA Ops:
  1.4 7.2 %collective-permute-start = (f32[2,8,128]{2,1,0:T(8,128)S(1)}, f32[2,8,128]{2,1,0:T(8,128)S(1)}, u32[]{:S(2)}, u32[]{:S(2)}) collective-permute-start(f32[2,8,128]{2,1,0:T(8,128)S(1)} %get-tuple-element.46), channel_id=1, source_target_pairs={{0,16},{16,32},{32,48},{48,64},{64,80},{80,96},{96,112},{112,0},{1... | collective-permute-start | bytes 24584 | tf_op jit(solution)/shard_map/ppermute | solution.py:418
  3.5 5.2 %collective-permute-start.1 = (f32[2,8,128]{2,1,0:T(8,128)S(1)}, f32[2,8,128]{2,1,0:T(8,128)S(1)}, u32[]{:S(2)}, u32[]{:S(2)}) collective-permute-start(f32[2,8,128]{2,1,0:T(8,128)S(1)} %get-tuple-element.47), channel_id=1, source_target_pairs={{16,0},{32,16},{48,32},{64,48},{80,64},{96,80},{112,96},{0,112},{1... | collective-permute-start | bytes 24584 | tf_op jit(solution)/shard_map/ppermute | solution.py:417
  9.4 1.3 %collective-permute-start.2 = (f32[7,8,128]{2,1,0:T(8,128)S(1)}, f32[7,8,128]{2,1,0:T(8,128)S(1)}, u32[]{:S(2)}, u32[]{:S(2)}) collective-permute-start(f32[7,8,128]{2,1,0:T(8,128)S(1)} %get-tuple-element.53.refs_0_), channel_id=1, source_target_pairs={{0,1},{1,0},{2,3},{3,2},{4,5},{5,4},{6,7},{7,6},{8,9},{9,8},{10,11... | collective-permute-start | bytes 86024 | tf_op jit(solution)/shard_map/ppermute | solution.py:378
  10.7 5.5 %collective-permute-start.5 = (f32[7,8,128]{2,1,0:T(8,128)S(1)}, f32[7,8,128]{2,1,0:T(8,128)S(1)}, u32[]{:S(2)}, u32[]{:S(2)}) collective-permute-start(f32[7,8,128]{2,1,0:T(8,128)S(1)} %shard_map.58.refs_0_.refs_1_), channel_id=1, source_target_pairs={{0,4},{1,5},{2,6},{3,7},{4,0},{5,1},{6,2},{7,3},{8,12},{9,13},{10,... | collective-permute-start | bytes 86024 | tf_op jit(solution)/shard_map/ppermute | solution.py:384
  13.8 3.9 %collective-permute-start.4 = (f32[7,8,128]{2,1,0:T(8,128)S(1)}, f32[7,8,128]{2,1,0:T(8,128)S(1)}, u32[]{:S(2)}, u32[]{:S(2)}) collective-permute-start(f32[7,8,128]{2,1,0:T(8,128)S(1)} %shard_map.58.refs_0_.refs_1_), channel_id=1, source_target_pairs={{0,6},{1,7},{2,0},{3,1},{4,2},{5,3},{6,4},{7,5},{8,14},{9,15},{10,... | collective-permute-start | bytes 86024 | tf_op jit(solution)/shard_map/ppermute | solution.py:384
  14.9 5.1 %collective-permute-start.3 = (f32[7,8,128]{2,1,0:T(8,128)S(1)}, f32[7,8,128]{2,1,0:T(8,128)S(1)}, u32[]{:S(2)}, u32[]{:S(2)}) collective-permute-start(f32[7,8,128]{2,1,0:T(8,128)S(1)} %shard_map.58.refs_0_.refs_1_), channel_id=1, source_target_pairs={{0,2},{1,3},{2,4},{3,5},{4,6},{5,7},{6,0},{7,1},{8,10},{9,11},{10,... | collective-permute-start | bytes 86024 | tf_op jit(solution)/shard_map/ppermute | solution.py:384
  20.1 5.5 %collective-permute-start.6 = (f32[7,8,128]{2,1,0:T(8,128)S(1)}, f32[7,8,128]{2,1,0:T(8,128)S(1)}, u32[]{:S(2)}, u32[]{:S(2)}) collective-permute-start(f32[7,8,128]{2,1,0:T(8,128)S(1)} %get-tuple-element.55.refs_3_), channel_id=1, source_target_pairs={{0,8},{1,9},{2,10},{3,11},{4,12},{5,13},{6,14},{7,15},{8,0},{9,1},... | collective-permute-start | bytes 86024 | tf_op jit(solution)/shard_map/ppermute | solution.py:378

commit v3 on v2

v3 whole, which is shorter than its diff:
```python
import jax
import jax.numpy as jnp
from jax import lax
from jax.experimental import pallas as pl
from jax.experimental.pallas import tpu as pltpu
from jax.sharding import PartitionSpec as P

Z, N = 8, 128
ROWS = Z * N
PITCH = N + 8
CHUNKS, STEP = 8, 16
F32 = jnp.float32
VM = pltpu.VMEM


def rcp(x):
    return pl.reciprocal(x, approx=True)


def link(a, b):
    return a * b * rcp(a + b)


def at(i):
    return pl.ds(pl.multiple_of(i * Z, Z), Z)


def strided(i):
    return pl.ds(i, Z, stride=PITCH)


def conductivity(t, reg, mag, soft):
    m = jnp.where(reg == 0, mag[0], jnp.where(reg == 1, mag[1], mag[2]))
    b = jnp.where(reg == 0, soft[0], jnp.where(reg == 1, soft[1], soft[2]))
    return m * jnp.exp(b * t)


def turn(src, dst):
    def body(z, _):
        lines = pl.ds(z, N, stride=Z)
        dst[lines, :] = src[lines, :].T
        return 0

    lax.fori_loop(0, Z, body, 0, unroll=2)


def factor(c_ref, pr_ref, gr_ref, rr_ref, sep_ref, net_ref, south=None, there=None):
    one = jnp.ones((Z, N), F32)
    zero = jnp.zeros((Z, N), F32)

    def cell(c, j, p, t, s, here, beyond=None):
        i = c * STEP + j
        edge = beyond is not None
        if not edge:
            beyond = c_ref[at(i + 1), :]
        g = link(here, beyond)
        if edge:
            g = jnp.where(there, g, 0.0)
        r = rcp(p + g + t)
        pr, gr = p * r, g * r
        pr_ref[at(i), :] = pr
        gr_ref[at(i), :] = gr
        rr_ref[at(i), :] = r
        return pr * g, gr * t if edge else 1.0 + gr * t, s + pr * t, beyond

    start = []
    for c in range(CHUNKS):
        here = c_ref[at(c * STEP + 1), :]
        start.append((link(c_ref[at(c * STEP), :], here), one, zero, here))

    def body(j, state):
        return [cell(c, j, *state[c]) for c in range(CHUNKS)]

    state = lax.fori_loop(1, STEP - 1, body, start)
    last = state[-1] if south is None else cell(CHUNKS - 1, STEP - 1, *state[-1], south)
    state = [cell(c, STEP - 1, *state[c]) for c in range(CHUNKS - 1)] + [last]
    q = state[0][0]
    left = 1.0 + state[0][2]
    t = state[0][1] + state[1][2]
    for c in range(1, CHUNKS):
        g = state[c][0]
        r = rcp(q + g + t)
        qr, gr = q * r, g * r
        sep_ref[0, c] = qr
        sep_ref[1, c] = gr
        sep_ref[2, c] = r
        left = left + qr * t
        t = state[c][1] + gr * t
        if c + 1 < CHUNKS:
            t = t + state[c + 1][2]
        q = qr * g
    net_ref[0] = q
    net_ref[1] = left
    net_ref[2] = t if south is None else jnp.where(there, t, 1.0)


def sweep(rhs, pr_ref, gr_ref, rr_ref, sep_ref, rd_ref, srd_ref, shared):
    def cell(c, j, d, s):
        i = c * STEP + j
        rd_ref[at(i), :] = rr_ref[at(i), :] * d
        beyond = gr_ref[at(i), :] * d
        if not (c == CHUNKS - 1 and j is STEP - 1):
            beyond = rhs(i + 1) + beyond
        return beyond, s + pr_ref[at(i), :] * d

    def body(j, state):
        return [cell(c, j, *state[c]) for c in range(CHUNKS)]

    start = [(rhs(c * STEP + 1), jnp.zeros((Z, N), F32)) for c in range(CHUNKS)]
    state = lax.fori_loop(1, STEP - 1, body, start)
    last = cell(CHUNKS - 1, STEP - 1, *state[-1]) if shared else state[-1]
    state = [cell(c, STEP - 1, *state[c]) for c in range(CHUNKS - 1)] + [last]
    left = rhs(0) + state[0][1]
    d = state[0][0] + state[1][1]
    for c in range(1, CHUNKS):
        left = left + sep_ref[0, c] * d
        srd_ref[c] = sep_ref[2, c] * d
        d = state[c][0] + sep_ref[1, c] * d
        if c + 1 < CHUNKS:
            d = d + state[c + 1][1]
    return left, d


def back(ul, ur, pr_ref, gr_ref, rd_ref, sep_ref, srd_ref, put, shared):
    seps = [None] * CHUNKS + [ur]
    for c in range(CHUNKS - 1, 0, -1):
        seps[c] = srd_ref[c] + sep_ref[0, c] * ul + sep_ref[1, c] * seps[c + 1]
    seps[0] = ul
    for c in range(CHUNKS):
        put(c * STEP, seps[c])

    def cell(c, j, u):
        i = c * STEP + j
        v = rd_ref[at(i), :] + pr_ref[at(i), :] * seps[c] + gr_ref[at(i), :] * u
        put(i, v)
        return v

    if not shared:
        put(N - 1, ur)
    last = cell(CHUNKS - 1, STEP - 1, ur) if shared else ur
    state = [cell(c, STEP - 1, seps[c + 1]) for c in range(CHUNKS - 1)] + [last]

    def body(k, state):
        return [cell(c, STEP - 2 - k, state[c]) for c in range(CHUNKS)]

    lax.fori_loop(0, STEP - 2, body, state)


def joined(own, other, left):
    a = [jnp.where(left, x, y) for x, y in zip(own, other)]
    b = [jnp.where(left, y, x) for x, y in zip(own, other)]
    if len(a) == 5:
        s, d = a[2] + b[1], a[4] + b[3]
        r = rcp(a[0] + b[0] + s)
        f, h = a[0] * r, b[0] * r
        return [f * b[0], a[1] + f * s, b[2] + h * s, a[3] + f * d, b[4] + h * d]
    between = link(a[6], b[5])
    r = rcp(a[0] + between + a[2])
    f, h = a[0] * r, between * r
    g1 = f * between
    s1 = b[1] + h * a[2]
    d1 = b[3] + h * a[4]
    left_s = a[1] + f * a[2]
    left_d = a[3] + f * a[4]
    r = rcp(g1 + b[0] + s1)
    f, h = g1 * r, b[0] * r
    return [f * b[0], left_s + f * s1, b[2] + h * s1, left_d + f * d1, b[4] + h * d1, a[5], b[6]]


def ends(me, owns, others):
    zero = jnp.zeros((Z, N), F32)
    yl = il = yr = ir = zero
    for k in reversed(range(len(others))):
        p, m = others[k], owns[k]
        left = (me >> k) % 2 == 1
        far_s = jnp.where(left, p[1] + yl, p[2] + yr)
        far_d = jnp.where(left, p[3] + il, p[4] + ir)
        near_s = jnp.where(left, p[2], p[1])
        near_d = jnp.where(left, p[4], p[3])
        f = p[0] * rcp(p[0] + far_s)
        y, i = near_s + f * far_s, near_d + f * far_d
        if len(p) == 7:
            between = link(jnp.where(left, p[6], p[5]), jnp.where(left, m[5], m[6]))
            f = between * rcp(between + y)
            y, i = f * y, f * i
        yl, il = jnp.where(left, y, yl), jnp.where(left, i, il)
        yr, ir = jnp.where(left, yr, y), jnp.where(left, ir, i)
    m = owns[0]
    sl, dl, sr, dr = m[1] + yl, m[3] + il, m[2] + yr, m[4] + ir
    r = rcp(m[0] + sl)
    f = m[0] * r
    ur = (dr + f * dl) * rcp(sr + f * sl)
    ul = (dl + m[0] * ur) * r
    return ul, ur


def edge_kernel(
    t_hbm, reg_hbm, s_hbm, mag_hbm, soft_hbm,
    t_ref, reg_ref, s_ref, up_ref, down_ref, par_ref, mag_ref, soft_ref, sem,
):
    pairs = (
        (mag_hbm, mag_ref), (soft_hbm, soft_ref), (t_hbm, t_ref), (reg_hbm, reg_ref), (s_hbm, s_ref),
    )
    copies = [
        pltpu.make_async_copy(a, b if k < 2 else b.at[:, pl.ds(0, N), :], sem.at[k])
        for k, (a, b) in enumerate(pairs)
    ]
    for copy in copies:
        copy.start()
    copies[0].wait()
    copies[1].wait()
    mag = [jnp.full((Z, N), mag_ref[k] * 1000.0) for k in range(3)]
    soft = [jnp.full((Z, N), -soft_ref[k]) for k in range(3)]
    for k in range(3):
        par_ref[k] = mag[k]
        par_ref[3 + k] = soft[k]
    copies[2].wait()
    copies[3].wait()
    for row, out in ((0, up_ref), (N - 1, down_ref)):
        t = t_ref[:, row, :]
        out[0] = t
        out[1] = conductivity(t, reg_ref[:, row, :], mag, soft)
    copies[4].wait()


def first_kernel(
    t_ref, reg_ref, s_ref, par_ref,
    ty_ref, cy_ref, r_ref, pr_ref, gr_ref, rr_ref, sep_ref, net_ref, cend_ref, cx_ref,
):
    mag = [par_ref[k] for k in range(3)]
    soft = [par_ref[3 + k] for k in range(3)]
    z = lax.broadcasted_iota(jnp.int32, (Z, N), 0)
    inner = jnp.where(z < Z - 1, 1.6e-4, 0.0)
    ground = jnp.where(z == 0, 8e-5, 0.0)

    def load(y):
        t = t_ref[strided(y), :]
        c = conductivity(t, reg_ref[strided(y), :], mag, soft)
        ty_ref[at(y), :] = t
        cy_ref[at(y), :] = c
        return t, c

    def row(y, t, c, before, after):
        flux = link(c, pltpu.roll(c, Z - 1, 0)) * (pltpu.roll(t, Z - 1, 0) - t) * inner
        up = flux - pltpu.roll(flux, 1, 0) - ground * (c * t)
        r_ref[at(y), :] = 2.0 * t + s_ref[strided(y), :] + 2.0 * (after - before) + up

    def body(k, state):
        t, c, before = state
        for j in range(8):
            y = k * 8 + j
            tn, cn = load(y + 1)
            after = link(c, cn) * (tn - t)
            row(y, t, c, before, after)
            t, c, before = tn, cn, after
        return t, c, before

    t, c = load(0)
    state = lax.fori_loop(0, N // 8 - 1, body, (t, c, jnp.zeros((Z, N), F32)))
    t, c, before = state
    for y in range(N - 8, N - 1):
        tn, cn = load(y + 1)
        after = link(c, cn) * (tn - t)
        row(y, t, c, before, after)
        t, c, before = tn, cn, after
    row(N - 1, t, c, before, jnp.zeros((Z, N), F32))
    turn(cy_ref, cx_ref)
    factor(cx_ref, pr_ref, gr_ref, rr_ref, sep_ref, net_ref)
    cend_ref[0] = cx_ref[at(0), :]
    cend_ref[1] = cx_ref[at(N - 1), :]


def side_kernel(
    r_ref, ty_ref, cy_ref, north_ref, south_ref, pr_ref, gr_ref, rr_ref, sep_ref, net_ref,
    cx_ref, rd_ref, srd_ref, out_ref, rx_ref, ry_ref,
):
    me = lax.axis_index("row")
    ry_ref[...] = r_ref[...]
    for row, halo, there in ((0, north_ref, me > 0), (N - 1, south_ref, me < lax.axis_size("row") - 1)):
        i = slice(row * Z, row * Z + Z)
        flux = link(cy_ref[i, :], halo[1]) * (halo[0] - ty_ref[i, :])
        ry_ref[i, :] = r_ref[i, :] + jnp.where(there, 2.0 * flux, 0.0)
    turn(ry_ref, rx_ref)
    left, right = sweep(
        lambda i: rx_ref[at(i), :], pr_ref, gr_ref, rr_ref, sep_ref, rd_ref, srd_ref, False
    )
    for k in range(3):
        out_ref[k] = net_ref[k]
    out_ref[3] = left
    out_ref[4] = right
    out_ref[5] = cx_ref[0]
    out_ref[6] = cx_ref[1]


def lines_kernel(c_ref, south_ref, *outs):
    there = lax.axis_index("row") < lax.axis_size("row") - 1
    factor(c_ref, *outs, south=south_ref[1], there=there)


def merge_kernel(axis, own_ref, other_ref, out_ref):
    left = lax.axis_index(axis) % 2 == 0
    new = joined([own_ref[k] for k in range(7)], [other_ref[k] for k in range(7)], left)
    for k in range(7):
        out_ref[k] = new[k]


def ring_kernel(axis, own_ref, before_ref, after_ref, across_ref, *outs):
    place = lax.axis_index(axis) // 2 % 4
    even = place % 2 == 0
    own, before, after, across = (
        [r[k] for k in range(7)] for r in (own_ref, before_ref, after_ref, across_ref)
    )
    near = [jnp.where(even, a, b) for a, b in zip(after, before)]
    far = [jnp.where(even, b, a) for a, b in zip(after, before)]
    pair = joined(own, near, even)
    rest = joined(across, far, even)
    every = joined(pair, rest, place < 2)
    for out, net in zip(outs, (near, pair, rest, every)):
        for k in range(7):
            out[k] = net[k]


def middle_kernel(*refs):
    owns, others, refs = refs[:4], refs[4:8], refs[8:]
    (
        pr_ref, gr_ref, rd_ref, sep_ref, srd_ref, ty_ref,
        ypr_ref, ygr_ref, yrr_ref, ysep_ref, ynet_ref,
        yrd_ref, ysrd_ref, out_ref, wx_ref, wy_ref,
    ) = refs
    nets = [[[r[k] for k in range(7)] for r in group] for group in (owns, others)]
    ul, ur = ends(lax.axis_index("col"), *nets)

    def put(i, v):
        wx_ref[at(i), :] = v

    back(ul, ur, pr_ref, gr_ref, rd_ref, sep_ref, srd_ref, put, False)
    turn(wx_ref, wy_ref)
    left, right = sweep(
        lambda i: wy_ref[at(i), :] - 2.0 * ty_ref[at(i), :],
        ypr_ref, ygr_ref, yrr_ref, ysep_ref, yrd_ref, ysrd_ref, True,
    )
    for b in range(out_ref.shape[0]):
        for k in range(3):
            out_ref[b, k] = ynet_ref[k]
        out_ref[b, 3] = left
        out_ref[b, 4] = right


def last_kernel(
    all_ref, pr_ref, gr_ref, rd_ref, sep_ref, srd_ref, ty_ref, out_hbm, new_ref, sem
):
    me = lax.axis_index("row")
    place = lambda m: [all_ref[me ^ m, k] for k in range(5)]
    one, two = me % 2 == 0, me // 2 % 2 == 0
    own = place(0)
    pair = joined(own, place(1), one)
    far = joined(place(2), place(3), one)
    half = joined(joined(place(4), place(5), one), joined(place(6), place(7), one), two)
    ul, ur = ends(me, [own, pair, None], [place(1), far, half])

    def put(i, v):
        new_ref[strided(i), :] = v + ty_ref[at(i), :]

    back(ul, ur, pr_ref, gr_ref, rd_ref, sep_ref, srd_ref, put, True)
    copies = [
        pltpu.make_async_copy(
            new_ref.at[pl.ds(z * PITCH, N), :], out_hbm.at[pl.ds(z * N, N), :], sem.at[z]
        )
        for z in range(Z)
    ]
    for copy in copies:
        copy.start()
    for copy in copies:
        copy.wait()


FIELD = (ROWS, N)
SPACED = (Z, PITCH, N)
NET = (7, Z, N)
SHARED = (5, Z, N)
PART = (3, Z, N)
SEPS = (3, CHUNKS, Z, N)
SEPD = (CHUNKS, Z, N)


def vm(shape):
    return VM(shape, F32)


def call(kernel, args, outs, scratch=(), flops=0, out_space=VM):
    args = [pltpu.with_memory_space_constraint(a, VM) for a in args]
    whole = pl.BlockSpec(memory_space=VM)
    many = isinstance(outs, tuple)
    return pl.pallas_call(
        kernel,
        in_specs=[whole] * len(args),
        out_specs=(whole,) * len(outs) if many else pl.BlockSpec(memory_space=out_space),
        out_shape=outs,
        scratch_shapes=list(scratch),
        cost_estimate=pl.CostEstimate(flops=flops, bytes_accessed=flops, transcendentals=0),
        compiler_params=pltpu.CompilerParams(vmem_limit_bytes=16 * 1024 * 1024),
    )(*args)


def partner(x, axis, mask):
    return lax.ppermute(x, axis, [(i, i ^ mask) for i in range(lax.axis_size(axis))])


def around(x, axis, shift):
    n = lax.axis_size(axis)
    to = lambda i: i // 8 * 8 + (i // 2 + shift) % 4 * 2 + (i + 1) % 2
    return lax.ppermute(x, axis, [(i, to(i)) for i in range(n)])


def spread_col(net, axis):
    owns, others = [net], [partner(net, axis, 1)]
    own = call(lambda *refs: merge_kernel(axis, *refs), [net, others[0]], vm(NET))
    near, pair, rest, every = call(
        lambda *refs: ring_kernel(axis, *refs),
        [own, around(own, axis, 1), around(own, axis, 3), around(own, axis, 2)],
        (vm(NET),) * 4,
    )
    return [net, own, pair, every], others + [near, rest, partner(every, axis, 9)]


def local(t, region, source, mag, soft):
    n = lax.axis_size("row")
    t, region, source, up, down, par = pl.pallas_call(
        edge_kernel,
        in_specs=[pl.BlockSpec(memory_space=pl.ANY)] * 5,
        out_specs=(pl.BlockSpec(memory_space=VM),) * 6,
        out_shape=(vm(SPACED), VM(SPACED, jnp.int32), vm(SPACED), vm((2, Z, N)), vm((2, Z, N)), vm((6, Z, N))),
        scratch_shapes=[
            pltpu.SMEM((3,), F32), pltpu.SMEM((3,), F32), pltpu.SemaphoreType.DMA((5,)),
        ],
    )(t, region, source, mag, soft)
    t, region, source = (a.reshape((Z * PITCH, N)) for a in (t, region, source))
    south = lax.ppermute(up, "row", [((i + 1) % n, i) for i in range(n)])
    north = lax.ppermute(down, "row", [(i, (i + 1) % n) for i in range(n)])
    ty, cy, r, pr, gr, rr, sep, net, cend = call(
        first_kernel,
        [t, region, source, par],
        (vm(FIELD),) * 6 + (vm(SEPS), vm(PART), vm((2, Z, N))),
        scratch=[vm(FIELD)],
        flops=20_000_000,
    )
    rd, srd, own = call(
        side_kernel,
        [r, ty, cy, north, south, pr, gr, rr, sep, net, cend],
        (vm(FIELD), vm(SEPD), vm(NET)),
        scratch=[vm(FIELD), vm(FIELD)],
    )
    ypr, ygr, yrr, ysep, ynet = call(
        lines_kernel, [cy, south], (vm(FIELD),) * 3 + (vm(SEPS), vm(PART)), flops=5_000_000
    )
    owns, others = spread_col(own, "col")
    yrd, ysrd, send = call(
        middle_kernel,
        owns + others + [pr, gr, rd, sep, srd, ty, ypr, ygr, yrr, ysep, ynet],
        (vm(FIELD), vm(SEPD), vm((n,) + SHARED)),
        scratch=[vm(FIELD), vm(FIELD)],
    )
    got = lax.all_to_all(send, "row", 0, 0, tiled=True)
    out = call(
        last_kernel,
        [got, ypr, ygr, yrd, ysep, ysrd, ty],
        jax.ShapeDtypeStruct(FIELD, F32),
        scratch=[vm((Z * PITCH, N)), pltpu.SemaphoreType.DMA((Z,))],
        out_space=pl.ANY,
    )
    return out.reshape((Z, N, N))


def solution(mesh):
    specs = (P(None, "row", "col"),) * 3 + (P(), P())
    return jax.shard_map(
        local, mesh=mesh, in_specs=specs, out_specs=P(None, "row", "col"), check_vma=False
    )
```

time: 39.4 us -> 37.4 us (0.949)
  Pallas kernels: 8.26 us -> 7.15 us
  starting transfers between devices: 13.5 us -> 12.7 us
  waiting for transfers between devices: 6.53 us -> 6 us
  blocking collectives: 10.9 us -> 11.3 us
    pallas_call x9 -> x7, Pallas kernels: 6.86 us -> 5.74 us  [call(): pl.pallas_call(kernel, in_specs=[whole] * len(args), out_specs=(whole,) *...]
    ppermute x3, starting transfers between devices: 5.13 us -> 4.62 us  [around(): return lax.ppermute(x, axis, [(i, to(i)) for i in range(n)])]
    all_to_all x1, blocking collectives: 10.9 us -> 11.3 us  [local(): got = lax.all_to_all(send, 'row', 0, 0, tiled=True)]
  transfers between devices with their start and end apart: 7 -> 7, of which waited for: 5 -> 5; matrix products, arithmetic and copies ran while one was open for 0% -> 0% of each run, Pallas kernels for 8% -> 7%
where the time goes in v3:
time: 37.4 us; the launch traced here: 37.3 us
  starting transfers between devices  12.7 us (34%)
  blocking collectives  11.3 us (30%)
  Pallas kernels  7.15 us (19%)
  waiting for transfers between devices  6 us (16%)
    all_to_all x1, blocking collectives, local(): got = lax.all_to_all(send, 'row', 0, 0, tiled=True)  11.3 us
    pallas_call x7, Pallas kernels, call(): pl.pallas_call(kernel, in_specs=[whole] * len(args), out_specs=(whole,) *...  5.74 us
    ppermute x3, starting transfers between devices, around(): return lax.ppermute(x, axis, [(i, to(i)) for i in range(n)])  4.62 us
    ppermute x3, waiting for transfers between devices, around(): return lax.ppermute(x, axis, [(i, to(i)) for i in range(n)])  3.85 us
    ppermute x2, starting transfers between devices, partner(): lax.ppermute(x, axis, [(i, i ^ mask) for i in range(lax.axis_size(axis))])  3.51 us
    ppermute x1, starting transfers between devices, local(): south = lax.ppermute(up, 'row', [((i + 1) % n, i) for i in range(n)])  2.53 us
    ppermute x2, waiting for transfers between devices, partner(): lax.ppermute(x, axis, [(i, i ^ mask) for i in range(lax.axis_size(axis))])  2.15 us
    ppermute x1, starting transfers between devices, local(): north = lax.ppermute(down, 'row', [(i, (i + 1) % n) for i in range(n)])  2.07 us
  transfers between devices with their start and end apart: 7, of which 5 were waited for; matrix products, arithmetic and copies ran while one was open for 0% of the time, Pallas kernels for 7%

profile of v3, /device:TPU:0, one launch (start us, length us, event | category | flops | bytes accessed | tf_op | source)
XLA Modules:
  0.0 37.3 jit_solution(8577403458670577274)
XLA Ops:
  0.0 1.4 %shard_map.55 = (f32[8,136,128]{2,1,0:T(8,128)S(1)}, s32[8,136,128]{2,1,0:T(8,128)S(1)}, f32[8,136,128]{2,1,0:T(8,128)S(1)}, f32[2,8,128]{2,1,0:T(8,128)S(1)}, f...) custom-call(f32[8,128,128]{2,1,0:T(8,128)} %t_hbm.1, s32[8,128,128]{2,1,0:T(8,128)} %reg_hbm.1, f32[8,128,128]{2,1,0:T(8,128)} %s_hbm.1, ...), custom_call_target="tpu_custom_call" | custom-call | tf_op jit(solution)/shard_map/pallas_call | solution.py:428
  1.4 2.1 %collective-permute-start = (f32[2,8,128]{2,1,0:T(8,128)S(1)}, f32[2,8,128]{2,1,0:T(8,128)S(1)}, u32[]{:S(2)}, u32[]{:S(2)}) collective-permute-start(f32[2,8,128]{2,1,0:T(8,128)S(1)} %get-tuple-element.42), channel_id=1, source_target_pairs={{0,16},{16,32},{32,48},{48,64},{64,80},{80,96},{96,112},{112,0},{1... | collective-permute-start | bytes 24584 | tf_op jit(solution)/shard_map/ppermute | solution.py:439
  3.5 2.5 %collective-permute-start.1 = (f32[2,8,128]{2,1,0:T(8,128)S(1)}, f32[2,8,128]{2,1,0:T(8,128)S(1)}, u32[]{:S(2)}, u32[]{:S(2)}) collective-permute-start(f32[2,8,128]{2,1,0:T(8,128)S(1)} %get-tuple-element.43), channel_id=1, source_target_pairs={{16,0},{32,16},{48,32},{64,48},{80,64},{96,80},{112,96},{0,112},{1... | collective-permute-start | bytes 24584 | tf_op jit(solution)/shard_map/ppermute | solution.py:438
  6.0 2.0 %shard_map.56 = (f32[1024,128]{1,0:T(8,128)S(1)}, f32[1024,128]{1,0:T(8,128)S(1)}, f32[1024,128]{1,0:T(8,128)S(1)}, f32[1024,128]{1,0:T(8,128)S(1)}, f32[1024,12...) custom-call(f32[1088,128]{1,0:T(8,128)S(1)} %bitcast.4, ...), custom_call_target="tpu_custom_call" | custom-call | flops 20000000 | bytes 20000000 | tf_op jit(solution)/shard_map/pallas_call | solution.py:394
  8.0 0.0 collective-permute-done.north_ref
  8.0 0.0 collective-permute-done.1.south_ref
  8.0 0.7 %shard_map.57 = (f32[1024,128]{1,0:T(8,128)S(1)}, f32[8,8,128]{2,1,0:T(8,128)S(1)}, f32[7,8,128]{2,1,0:T(8,128)S(1)}) custom-call(f32[1024,128]{1,0:T(8,128)S(1)} %get-tuple-element.39.r_ref, f32[1024,128]{1,0:T(8,128)S(1)} %get-tuple-element.40.ty_ref.refs_13_, f32[1024,128]{1,0:T(8,128)S(1)} %get-tuple-element.41.cy_ref.c_ref, ...), custom_call_target="tpu_custom_call" | custom-call | tf_op jit(solution)/shard_map/pallas_call | solution.py:394
  8.7 0.1 collective-permute-start.2
  8.8 1.2 %collective-permute-done.2.refs_1_.refs_4_ = f32[7,8,128]{2,1,0:T(8,128)S(1)} collective-permute-done((f32[7,8,128]{2,1,0:T(8,128)S(1)}, f32[7,8,128]{2,1,0:T(8,128)S(1)}, u32[]{:S(2)}, u32[]{:S(2)}) %collective-permute-start.2) | collective-permute-done | bytes 28704 | tf_op jit(solution)/shard_map/ppermute | solution.py:406
  10.0 2.9 %collective-permute-start.5 = (f32[7,8,128]{2,1,0:T(8,128)S(1)}, f32[7,8,128]{2,1,0:T(8,128)S(1)}, u32[]{:S(2)}, u32[]{:S(2)}) collective-permute-start(f32[7,8,128]{2,1,0:T(8,128)S(1)} %shard_map.58.refs_0_.refs_1_), channel_id=1, source_target_pairs={{0,5},{1,4},{2,7},{3,6},{4,1},{5,0},{6,3},{7,2},{8,13},{9,12},{10,... | collective-permute-start | bytes 86024 | tf_op jit(solution)/shard_map/ppermute | solution.py:412
  12.9 1.1 %collective-permute-start.4 = (f32[7,8,128]{2,1,0:T(8,128)S(1)}, f32[7,8,128]{2,1,0:T(8,128)S(1)}, u32[]{:S(2)}, u32[]{:S(2)}) collective-permute-start(f32[7,8,128]{2,1,0:T(8,128)S(1)} %shard_map.58.refs_0_.refs_1_), channel_id=1, source_target_pairs={{0,7},{1,6},{2,1},{3,0},{4,3},{5,2},{6,5},{7,4},{8,15},{9,14},{10,... | collective-permute-start | bytes 86024 | tf_op jit(solution)/shard_map/ppermute | solution.py:412
  14.0 0.7 %collective-permute-start.3 = (f32[7,8,128]{2,1,0:T(8,128)S(1)}, f32[7,8,128]{2,1,0:T(8,128)S(1)}, u32[]{:S(2)}, u32[]{:S(2)}) collective-permute-start(f32[7,8,128]{2,1,0:T(8,128)S(1)} %shard_map.58.refs_0_.refs_1_), channel_id=1, source_target_pairs={{0,3},{1,2},{2,5},{3,4},{4,7},{5,6},{6,1},{7,0},{8,11},{9,10},{10,... | collective-permute-start | bytes 86024 | tf_op jit(solution)/shard_map/ppermute | solution.py:412
  14.7 0.3 collective-permute-done.5.refs_3_
  14.9 1.3 %collective-permute-done.4.refs_2_ = f32[7,8,128]{2,1,0:T(8,128)S(1)} collective-permute-done((f32[7,8,128]{2,1,0:T(8,128)S(1)}, f32[7,8,128]{2,1,0:T(8,128)S(1)}, u32[]{:S(2)}, u32[]{:S(2)}) %collective-permute-start.4) | collective-permute-done | bytes 28704 | tf_op jit(solution)/shard_map/ppermute | solution.py:412
  16.2 2.3 %collective-permute-done.3.refs_1_ = f32[7,8,128]{2,1,0:T(8,128)S(1)} collective-permute-done((f32[7,8,128]{2,1,0:T(8,128)S(1)}, f32[7,8,128]{2,1,0:T(8,128)S(1)}, u32[]{:S(2)}, u32[]{:S(2)}) %collective-permute-start.3) | collective-permute-done | bytes 28704 | tf_op jit(solution)/shard_map/ppermute | solution.py:412
  18.6 3.4 %collective-permute-start.6 = (f32[7,8,128]{2,1,0:T(8,128)S(1)}, f32[7,8,128]{2,1,0:T(8,128)S(1)}, u32[]{:S(2)}, u32[]{:S(2)}) collective-permute-start(f32[7,8,128]{2,1,0:T(8,128)S(1)} %get-tuple-element.52.refs_3_), channel_id=1, source_target_pairs={{0,9},{1,8},{2,11},{3,10},{4,13},{5,12},{6,15},{7,14},{8,1},{9,0},... | collective-permute-start | bytes 86024 | tf_op jit(solution)/shard_map/ppermute | solution.py:406
  22.0 0.6 %shard_map.60 = (f32[1024,128]{1,0:T(8,128)S(1)}, f32[1024,128]{1,0:T(8,128)S(1)}, f32[1024,128]{1,0:T(8,128)S(1)}, f32[3,8,8,128]{3,2,1,0:T(8,128)S(1)}, f32[3,8,128]{2,1,0:T(8,128)S(1)}) custom-call(f32[1024,128]{1,0:T(8,128)S(1)} %get-tuple-element.41.cy_ref.c_ref, f32[2,8,128]{2,1,0:T(8,128)S(1)} %collective-permute-done.1.south_ref), custom_call_target="tpu_custom_call" | custom-call | flops 5000000 | bytes 5000000 | tf_op jit(solution)/shard_map/pallas_call | solution.py:394
  22.6 1.0 %collective-permute-done.6.refs_7_ = f32[7,8,128]{2,1,0:T(8,128)S(1)} collective-permute-done((f32[7,8,128]{2,1,0:T(8,128)S(1)}, f32[7,8,128]{2,1,0:T(8,128)S(1)}, u32[]{:S(2)}, u32[]{:S(2)}) %collective-permute-start.6) | collective-permute-done | bytes 28704 | tf_op jit(solution)/shard_map/ppermute | solution.py:406
  23.6 1.1 %shard_map.61 = (f32[1024,128]{1,0:T(8,128)S(1)}, f32[8,8,128]{2,1,0:T(8,128)S(1)}, f32[8,5,8,128]{3,2,1,0:T(8,128)S(1)}) custom-call(f32[7,8,128]{2,1,0:T(8,128)S(1)} %get-tuple-element.50.refs_0_, f32[7,8,128]{2,1,0:T(8,128)S(1)} %shard_map.58.refs_0_.refs_1_, f32[7,8,128]{2,1,0:T(8,128)S(1)} %get-tuple-element.51.refs_2_, ...), custom_call_target="tpu_custom_call" | custom-call | tf_op jit(solution)/shard_map/pallas_call | solution.py:394
  24.7 11.3 %all_to_all.5.all_ref = f32[8,5,8,128]{3,2,1,0:T(8,128)S(1)} all-to-all(f32[8,5,8,128]{3,2,1,0:T(8,128)S(1)} %get-tuple-element.62), channel_id=1, replica_groups=mesh['row'=8,'col'=16] {'row'}, dimensions={0} | all-to-all | bytes 327680 | tf_op jit(solution)/shard_map/all_to_all | solution.py:463
  36.0 1.3 %shard_map.62 = f32[1024,128]{1,0:T(8,128)} custom-call(f32[8,5,8,128]{3,2,1,0:T(8,128)S(1)} %all_to_all.5.all_ref, f32[1024,128]{1,0:T(8,128)S(1)} %get-tuple-element.57.refs_14_.pr_ref, f32[1024,128]{1,0:T(8,128)S(1)} %get-tuple-element.58.refs_15_.gr_ref, f32[1024,128]{1,0:T(8,128)S(1)} %get-tuple-element.63.rd_ref, ...), custom_call_target="tpu_custom_call" | custom-call | tf_op jit(solution)/shard_map/pallas_call | solution.py:394
  (2 shorter events, 0.1 us)
Async XLA Ops:
  1.4 6.6 %collective-permute-start = (f32[2,8,128]{2,1,0:T(8,128)S(1)}, f32[2,8,128]{2,1,0:T(8,128)S(1)}, u32[]{:S(2)}, u32[]{:S(2)}) collective-permute-start(f32[2,8,128]{2,1,0:T(8,128)S(1)} %get-tuple-element.42), channel_id=1, source_target_pairs={{0,16},{16,32},{32,48},{48,64},{64,80},{80,96},{96,112},{112,0},{1... | collective-permute-start | bytes 24584 | tf_op jit(solution)/shard_map/ppermute | solution.py:439
  3.5 4.5 %collective-permute-start.1 = (f32[2,8,128]{2,1,0:T(8,128)S(1)}, f32[2,8,128]{2,1,0:T(8,128)S(1)}, u32[]{:S(2)}, u32[]{:S(2)}) collective-permute-start(f32[2,8,128]{2,1,0:T(8,128)S(1)} %get-tuple-element.43), channel_id=1, source_target_pairs={{16,0},{32,16},{48,32},{64,48},{80,64},{96,80},{112,96},{0,112},{1... | collective-permute-start | bytes 24584 | tf_op jit(solution)/shard_map/ppermute | solution.py:438
  8.7 1.3 %collective-permute-start.2 = (f32[7,8,128]{2,1,0:T(8,128)S(1)}, f32[7,8,128]{2,1,0:T(8,128)S(1)}, u32[]{:S(2)}, u32[]{:S(2)}) collective-permute-start(f32[7,8,128]{2,1,0:T(8,128)S(1)} %get-tuple-element.50.refs_0_), channel_id=1, source_target_pairs={{0,1},{1,0},{2,3},{3,2},{4,5},{5,4},{6,7},{7,6},{8,9},{9,8},{10,11... | collective-permute-start | bytes 86024 | tf_op jit(solution)/shard_map/ppermute | solution.py:406
  10.0 4.9 %collective-permute-start.5 = (f32[7,8,128]{2,1,0:T(8,128)S(1)}, f32[7,8,128]{2,1,0:T(8,128)S(1)}, u32[]{:S(2)}, u32[]{:S(2)}) collective-permute-start(f32[7,8,128]{2,1,0:T(8,128)S(1)} %shard_map.58.refs_0_.refs_1_), channel_id=1, source_target_pairs={{0,5},{1,4},{2,7},{3,6},{4,1},{5,0},{6,3},{7,2},{8,13},{9,12},{10,... | collective-permute-start | bytes 86024 | tf_op jit(solution)/shard_map/ppermute | solution.py:412
  12.9 3.3 %collective-permute-start.4 = (f32[7,8,128]{2,1,0:T(8,128)S(1)}, f32[7,8,128]{2,1,0:T(8,128)S(1)}, u32[]{:S(2)}, u32[]{:S(2)}) collective-permute-start(f32[7,8,128]{2,1,0:T(8,128)S(1)} %shard_map.58.refs_0_.refs_1_), channel_id=1, source_target_pairs={{0,7},{1,6},{2,1},{3,0},{4,3},{5,2},{6,5},{7,4},{8,15},{9,14},{10,... | collective-permute-start | bytes 86024 | tf_op jit(solution)/shard_map/ppermute | solution.py:412
  14.0 4.5 %collective-permute-start.3 = (f32[7,8,128]{2,1,0:T(8,128)S(1)}, f32[7,8,128]{2,1,0:T(8,128)S(1)}, u32[]{:S(2)}, u32[]{:S(2)}) collective-permute-start(f32[7,8,128]{2,1,0:T(8,128)S(1)} %shard_map.58.refs_0_.refs_1_), channel_id=1, source_target_pairs={{0,3},{1,2},{2,5},{3,4},{4,7},{5,6},{6,1},{7,0},{8,11},{9,10},{10,... | collective-permute-start | bytes 86024 | tf_op jit(solution)/shard_map/ppermute | solution.py:412
  18.6 5.0 %collective-permute-start.6 = (f32[7,8,128]{2,1,0:T(8,128)S(1)}, f32[7,8,128]{2,1,0:T(8,128)S(1)}, u32[]{:S(2)}, u32[]{:S(2)}) collective-permute-start(f32[7,8,128]{2,1,0:T(8,128)S(1)} %get-tuple-element.52.refs_3_), channel_id=1, source_target_pairs={{0,9},{1,8},{2,11},{3,10},{4,13},{5,12},{6,15},{7,14},{8,1},{9,0},... | collective-permute-start | bytes 86024 | tf_op jit(solution)/shard_map/ppermute | solution.py:406

commit v4 on v3

--- a/solution.py
+++ b/solution.py
@@ -41,7 +41,7 @@
         dst[lines, :] = src[lines, :].T
         return 0
 
-    lax.fori_loop(0, Z, body, 0, unroll=2)
+    lax.fori_loop(0, Z, body, 0, unroll=True)
 
 
 def factor(c_ref, pr_ref, gr_ref, rr_ref, sep_ref, net_ref, south=None, there=None):
@@ -71,7 +71,7 @@
     def body(j, state):
         return [cell(c, j, *state[c]) for c in range(CHUNKS)]
 
-    state = lax.fori_loop(1, STEP - 1, body, start)
+    state = lax.fori_loop(1, STEP - 1, body, start, unroll=2)
     last = state[-1] if south is None else cell(CHUNKS - 1, STEP - 1, *state[-1], south)
     state = [cell(c, STEP - 1, *state[c]) for c in range(CHUNKS - 1)] + [last]
     q = state[0][0]
@@ -99,7 +99,7 @@
         i = c * STEP + j
         rd_ref[at(i), :] = rr_ref[at(i), :] * d
         beyond = gr_ref[at(i), :] * d
-        if not (c == CHUNKS - 1 and j is STEP - 1):
+        if not (c == CHUNKS - 1 and isinstance(j, int)):
             beyond = rhs(i + 1) + beyond
         return beyond, s + pr_ref[at(i), :] * d
 
@@ -107,7 +107,7 @@
         return [cell(c, j, *state[c]) for c in range(CHUNKS)]
 
     start = [(rhs(c * STEP + 1), jnp.zeros((Z, N), F32)) for c in range(CHUNKS)]
-    state = lax.fori_loop(1, STEP - 1, body, start)
+    state = lax.fori_loop(1, STEP - 1, body, start, unroll=True)
     last = cell(CHUNKS - 1, STEP - 1, *state[-1]) if shared else state[-1]
     state = [cell(c, STEP - 1, *state[c]) for c in range(CHUNKS - 1)] + [last]
     left = rhs(0) + state[0][1]
@@ -143,7 +143,7 @@
     def body(k, state):
         return [cell(c, STEP - 2 - k, state[c]) for c in range(CHUNKS)]
 
-    lax.fori_loop(0, STEP - 2, body, state)
+    lax.fori_loop(0, STEP - 2, body, state, unroll=True)
 
 
 def joined(own, other, left):
@@ -195,38 +195,45 @@
 
 
 def edge_kernel(
-    t_hbm, reg_hbm, s_hbm, mag_hbm, soft_hbm,
-    t_ref, reg_ref, s_ref, up_ref, down_ref, par_ref, mag_ref, soft_ref, sem,
+    t_hbm, reg_hbm, mag_hbm, soft_hbm,
+    up_ref, down_ref, par_ref, t_ref, reg_ref, mag_ref, soft_ref, sem,
 ):
-    pairs = (
-        (mag_hbm, mag_ref), (soft_hbm, soft_ref), (t_hbm, t_ref), (reg_hbm, reg_ref), (s_hbm, s_ref),
-    )
     copies = [
-        pltpu.make_async_copy(a, b if k < 2 else b.at[:, pl.ds(0, N), :], sem.at[k])
-        for k, (a, b) in enumerate(pairs)
+        pltpu.make_async_copy(mag_hbm, mag_ref, sem.at[0]),
+        pltpu.make_async_copy(soft_hbm, soft_ref, sem.at[1]),
     ]
+    for k, first in enumerate((0, N - 8)):
+        rows = pl.ds(first, 8)
+        copies.append(pltpu.make_async_copy(t_hbm.at[:, rows, :], t_ref.at[k], sem.at[2 + k]))
+        copies.append(pltpu.make_async_copy(reg_hbm.at[:, rows, :], reg_ref.at[k], sem.at[4 + k]))
+    for copy in copies[2:] + copies[:2]:
+        copy.start()
     for copy in copies:
-        copy.start()
-    copies[0].wait()
-    copies[1].wait()
+        copy.wait()
     mag = [jnp.full((Z, N), mag_ref[k] * 1000.0) for k in range(3)]
     soft = [jnp.full((Z, N), -soft_ref[k]) for k in range(3)]
     for k in range(3):
         par_ref[k] = mag[k]
         par_ref[3 + k] = soft[k]
-    copies[2].wait()
-    copies[3].wait()
-    for row, out in ((0, up_ref), (N - 1, down_ref)):
-        t = t_ref[:, row, :]
+    for k, row, out in ((0, 0, up_ref), (1, 7, down_ref)):
+        t = t_ref[k, :, row, :]
         out[0] = t
-        out[1] = conductivity(t, reg_ref[:, row, :], mag, soft)
-    copies[4].wait()
+        out[1] = conductivity(t, reg_ref[k, :, row, :], mag, soft)
 
 
 def first_kernel(
-    t_ref, reg_ref, s_ref, par_ref,
-    ty_ref, cy_ref, r_ref, pr_ref, gr_ref, rr_ref, sep_ref, net_ref, cend_ref, cx_ref,
+    par_ref, t_hbm, reg_hbm, s_hbm,
+    ty_ref, cy_ref, r_ref, pr_ref, gr_ref, rr_ref, sep_ref, net_ref, cend_ref,
+    cx_ref, t_box, reg_box, s_box, sem,
 ):
+    cuts = (0, N // 2 + 8, N)
+    copies = [[], []]
+    for k in range(2):
+        rows = pl.ds(cuts[k], cuts[k + 1] - cuts[k])
+        for j, (a, b) in enumerate(((t_hbm, t_box), (reg_hbm, reg_box), (s_hbm, s_box))):
+            copies[k].append(pltpu.make_async_copy(a.at[:, rows, :], b.at[:, rows, :], sem.at[k, j]))
+            copies[k][-1].start()
+    t_ref, reg_ref, s_ref = (box.reshape(Z * PITCH, N) for box in (t_box, reg_box, s_box))
     mag = [par_ref[k] for k in range(3)]
     soft = [par_ref[3 + k] for k in range(3)]
     z = lax.broadcasted_iota(jnp.int32, (Z, N), 0)
@@ -245,25 +252,27 @@
         up = flux - pltpu.roll(flux, 1, 0) - ground * (c * t)
         r_ref[at(y), :] = 2.0 * t + s_ref[strided(y), :] + 2.0 * (after - before) + up
 
-    def body(k, state):
-        t, c, before = state
-        for j in range(8):
-            y = k * 8 + j
-            tn, cn = load(y + 1)
-            after = link(c, cn) * (tn - t)
-            row(y, t, c, before, after)
-            t, c, before = tn, cn, after
-        return t, c, before
-
-    t, c = load(0)
-    state = lax.fori_loop(0, N // 8 - 1, body, (t, c, jnp.zeros((Z, N), F32)))
-    t, c, before = state
-    for y in range(N - 8, N - 1):
+    def step(y, t, c, before):
         tn, cn = load(y + 1)
         after = link(c, cn) * (tn - t)
         row(y, t, c, before, after)
-        t, c, before = tn, cn, after
-    row(N - 1, t, c, before, jnp.zeros((Z, N), F32))
+        return tn, cn, after
+
+    def body(k, state):
+        for j in range(8):
+            state = step(k * 8 + j, *state)
+        return state
+
+    for copy in copies[0]:
+        copy.wait()
+    state = *load(0), jnp.zeros((Z, N), F32)
+    state = lax.fori_loop(0, N // 16, body, state)
+    for copy in copies[1]:
+        copy.wait()
+    state = lax.fori_loop(N // 16, N // 8 - 1, body, state)
+    for y in range(N - 8, N - 1):
+        state = step(y, *state)
+    row(N - 1, *state, jnp.zeros((Z, N), F32))
     turn(cy_ref, cx_ref)
     factor(cx_ref, pr_ref, gr_ref, rr_ref, sep_ref, net_ref)
     cend_ref[0] = cx_ref[at(0), :]
@@ -387,19 +396,19 @@
     return VM(shape, F32)
 
 
-def call(kernel, args, outs, scratch=(), flops=0, out_space=VM):
+def call(kernel, args, outs, scratch=(), flops=0, out_space=VM, outside=()):
     args = [pltpu.with_memory_space_constraint(a, VM) for a in args]
     whole = pl.BlockSpec(memory_space=VM)
     many = isinstance(outs, tuple)
     return pl.pallas_call(
         kernel,
-        in_specs=[whole] * len(args),
+        in_specs=[whole] * len(args) + [pl.BlockSpec(memory_space=pltpu.HBM)] * len(outside),
         out_specs=(whole,) * len(outs) if many else pl.BlockSpec(memory_space=out_space),
         out_shape=outs,
         scratch_shapes=list(scratch),
         cost_estimate=pl.CostEstimate(flops=flops, bytes_accessed=flops, transcendentals=0),
         compiler_params=pltpu.CompilerParams(vmem_limit_bytes=16 * 1024 * 1024),
-    )(*args)
+    )(*args, *(pltpu.with_memory_space_constraint(a, pltpu.HBM) for a in outside))
 
 
 def partner(x, axis, mask):
@@ -415,9 +424,12 @@
 def spread_col(net, axis):
     owns, others = [net], [partner(net, axis, 1)]
     own = call(lambda *refs: merge_kernel(axis, *refs), [net, others[0]], vm(NET))
+    after = around(own, axis, 3)
+    before = around(own, axis, 1)
+    across = around(own, axis, 2)
     near, pair, rest, every = call(
         lambda *refs: ring_kernel(axis, *refs),
-        [own, around(own, axis, 1), around(own, axis, 3), around(own, axis, 2)],
+        [own, before, after, across],
         (vm(NET),) * 4,
     )
     return [net, own, pair, every], others + [near, rest, partner(every, axis, 9)]
@@ -425,23 +437,27 @@
 
 def local(t, region, source, mag, soft):
     n = lax.axis_size("row")
-    t, region, source, up, down, par = pl.pallas_call(
+    edge = (2, Z, 8, N)
+    up, down, par = pl.pallas_call(
         edge_kernel,
-        in_specs=[pl.BlockSpec(memory_space=pl.ANY)] * 5,
-        out_specs=(pl.BlockSpec(memory_space=VM),) * 6,
-        out_shape=(vm(SPACED), VM(SPACED, jnp.int32), vm(SPACED), vm((2, Z, N)), vm((2, Z, N)), vm((6, Z, N))),
+        in_specs=[pl.BlockSpec(memory_space=pltpu.HBM)] * 4,
+        out_specs=(pl.BlockSpec(memory_space=VM),) * 3,
+        out_shape=(vm((2, Z, N)), vm((2, Z, N)), vm((6, Z, N))),
         scratch_shapes=[
-            pltpu.SMEM((3,), F32), pltpu.SMEM((3,), F32), pltpu.SemaphoreType.DMA((5,)),
+            vm(edge), VM(edge, jnp.int32), pltpu.SMEM((3,), F32), pltpu.SMEM((3,), F32),
+            pltpu.SemaphoreType.DMA((6,)),
         ],
-    )(t, region, source, mag, soft)
-    t, region, source = (a.reshape((Z * PITCH, N)) for a in (t, region, source))
+    )(t, region, mag, soft)
     south = lax.ppermute(up, "row", [((i + 1) % n, i) for i in range(n)])
     north = lax.ppermute(down, "row", [(i, (i + 1) % n) for i in range(n)])
     ty, cy, r, pr, gr, rr, sep, net, cend = call(
         first_kernel,
-        [t, region, source, par],
+        [par],
         (vm(FIELD),) * 6 + (vm(SEPS), vm(PART), vm((2, Z, N))),
-        scratch=[vm(FIELD)],
+        scratch=[
+            vm(FIELD), vm(SPACED), VM(SPACED, jnp.int32), vm(SPACED), pltpu.SemaphoreType.DMA((2, 3)),
+        ],
+        outside=[t, region, source],
         flops=20_000_000,
     )
     rd, srd, own = call(

time: 37.4 us -> 36 us (0.963)
  Pallas kernels: 7.15 us -> 6.24 us
  blocking collectives: 11.3 us -> 10.5 us
    pallas_call x8, Pallas kernels: 7.15 us -> 6.24 us  [the longest x7 5.34 us: call(): pl.pallas_call(kernel, in_specs=[whole] * len(args) + [pl.BlockSpec(memor...]
    all_to_all x1, blocking collectives: 11.3 us -> 10.5 us  [local(): got = lax.all_to_all(send, 'row', 0, 0, tiled=True)]
  transfers between devices with their start and end apart: 7 -> 7, of which waited for: 5 -> 5; matrix products, arithmetic and copies ran while one was open for 0% -> 0% of each run, Pallas kernels for 7% -> 9%
where the time goes in v4:
time: 36 us; the launch traced here: 35.7 us
  starting transfers between devices  12.7 us (35%)
  blocking collectives  10.5 us (29%)
  Pallas kernels  6.24 us (17%)
  waiting for transfers between devices  6.16 us (17%)
    all_to_all x1, blocking collectives, local(): got = lax.all_to_all(send, 'row', 0, 0, tiled=True)  10.5 us
    pallas_call x7, Pallas kernels, call(): pl.pallas_call(kernel, in_specs=[whole] * len(args) + [pl.BlockSpec(memor...  5.34 us
    ppermute x3, starting transfers between devices, around(): return lax.ppermute(x, axis, [(i, to(i)) for i in range(n)])  4.62 us
    ppermute x3, waiting for transfers between devices, around(): return lax.ppermute(x, axis, [(i, to(i)) for i in range(n)])  3.85 us
    ppermute x2, starting transfers between devices, partner(): lax.ppermute(x, axis, [(i, i ^ mask) for i in range(lax.axis_size(axis))])  3.52 us
    ppermute x1, starting transfers between devices, local(): south = lax.ppermute(up, 'row', [((i + 1) % n, i) for i in range(n)])  2.53 us
    ppermute x2, waiting for transfers between devices, partner(): lax.ppermute(x, axis, [(i, i ^ mask) for i in range(lax.axis_size(axis))])  2.3 us
    ppermute x1, starting transfers between devices, local(): north = lax.ppermute(down, 'row', [(i, (i + 1) % n) for i in range(n)])  2.07 us
  transfers between devices with their start and end apart: 7, of which 5 were waited for; matrix products, arithmetic and copies ran while one was open for 0% of the time, Pallas kernels for 9%

profile of v4, /device:TPU:0, one launch (start us, length us, event | category | flops | bytes accessed | tf_op | source)
XLA Modules:
  0.0 35.7 jit_solution(16981072369855049776)
XLA Ops:
  0.0 0.9 %shard_map.55 = (f32[2,8,128]{2,1,0:T(8,128)S(1)}, f32[2,8,128]{2,1,0:T(8,128)S(1)}, f32[6,8,128]{2,1,0:T(8,128)S(1)}) custom-call(f32[8,128,128]{2,1,0:T(8,128)} %t_hbm.3, s32[8,128,128]{2,1,0:T(8,128)} %reg_hbm.3, f32[3]{0:T(128)} %mag_hbm.1, f32[3]{0:T(128)} %soft_hbm.1), custom_call_target="tpu_custom_call" | custom-call | tf_op jit(solution)/shard_map/pallas_call | solution.py:441
  0.9 2.1 %collective-permute-start = (f32[2,8,128]{2,1,0:T(8,128)S(1)}, f32[2,8,128]{2,1,0:T(8,128)S(1)}, u32[]{:S(2)}, u32[]{:S(2)}) collective-permute-start(f32[2,8,128]{2,1,0:T(8,128)S(1)} %get-tuple-element.36), channel_id=1, source_target_pairs={{0,16},{16,32},{32,48},{48,64},{64,80},{80,96},{96,112},{112,0},{1... | collective-permute-start | bytes 24584 | tf_op jit(solution)/shard_map/ppermute | solution.py:452
  3.0 2.5 %collective-permute-start.1 = (f32[2,8,128]{2,1,0:T(8,128)S(1)}, f32[2,8,128]{2,1,0:T(8,128)S(1)}, u32[]{:S(2)}, u32[]{:S(2)}) collective-permute-start(f32[2,8,128]{2,1,0:T(8,128)S(1)} %get-tuple-element.37), channel_id=1, source_target_pairs={{16,0},{32,16},{48,32},{64,48},{80,64},{96,80},{112,96},{0,112},{1... | collective-permute-start | bytes 24584 | tf_op jit(solution)/shard_map/ppermute | solution.py:451
  5.5 2.8 %shard_map.56 = (f32[1024,128]{1,0:T(8,128)S(1)}, f32[1024,128]{1,0:T(8,128)S(1)}, f32[1024,128]{1,0:T(8,128)S(1)}, f32[1024,128]{1,0:T(8,128)S(1)}, f32[1024,12...) custom-call(f32[6,8,128]{2,1,0:T(8,128)S(1)} %get-tuple-element.32.p, ...), custom_call_target="tpu_custom_call" | custom-call | flops 20000000 | bytes 20000000 | tf_op jit(solution)/shard_map/pallas_call | solution.py:403
  8.3 0.0 collective-permute-done.north_ref
  8.3 0.0 collective-permute-done.1.south_ref
  8.3 0.4 %shard_map.57 = (f32[1024,128]{1,0:T(8,128)S(1)}, f32[8,8,128]{2,1,0:T(8,128)S(1)}, f32[7,8,128]{2,1,0:T(8,128)S(1)}) custom-call(f32[1024,128]{1,0:T(8,128)S(1)} %get-tuple-element.33.r_ref, f32[1024,128]{1,0:T(8,128)S(1)} %get-tuple-element.34.ty_ref.refs_13_, f32[1024,128]{1,0:T(8,128)S(1)} %get-tuple-element.35.cy_ref.c_ref, ...), custom_call_target="tpu_custom_call" | custom-call | tf_op jit(solution)/shard_map/pallas_call | solution.py:403
  8.7 0.1 collective-permute-start.2
  8.8 1.2 %collective-permute-done.2.refs_1_.refs_4_ = f32[7,8,128]{2,1,0:T(8,128)S(1)} collective-permute-done((f32[7,8,128]{2,1,0:T(8,128)S(1)}, f32[7,8,128]{2,1,0:T(8,128)S(1)}, u32[]{:S(2)}, u32[]{:S(2)}) %collective-permute-start.2) | collective-permute-done | bytes 28704 | tf_op jit(solution)/shard_map/ppermute | solution.py:415
  10.0 2.9 %collective-permute-start.5 = (f32[7,8,128]{2,1,0:T(8,128)S(1)}, f32[7,8,128]{2,1,0:T(8,128)S(1)}, u32[]{:S(2)}, u32[]{:S(2)}) collective-permute-start(f32[7,8,128]{2,1,0:T(8,128)S(1)} %shard_map.58.refs_0_.refs_1_), channel_id=1, source_target_pairs={{0,5},{1,4},{2,7},{3,6},{4,1},{5,0},{6,3},{7,2},{8,13},{9,12},{10,... | collective-permute-start | bytes 86024 | tf_op jit(solution)/shard_map/ppermute | solution.py:421
  12.9 1.1 %collective-permute-start.4 = (f32[7,8,128]{2,1,0:T(8,128)S(1)}, f32[7,8,128]{2,1,0:T(8,128)S(1)}, u32[]{:S(2)}, u32[]{:S(2)}) collective-permute-start(f32[7,8,128]{2,1,0:T(8,128)S(1)} %shard_map.58.refs_0_.refs_1_), channel_id=1, source_target_pairs={{0,7},{1,6},{2,1},{3,0},{4,3},{5,2},{6,5},{7,4},{8,15},{9,14},{10,... | collective-permute-start | bytes 86024 | tf_op jit(solution)/shard_map/ppermute | solution.py:421
  14.0 0.7 %collective-permute-start.3 = (f32[7,8,128]{2,1,0:T(8,128)S(1)}, f32[7,8,128]{2,1,0:T(8,128)S(1)}, u32[]{:S(2)}, u32[]{:S(2)}) collective-permute-start(f32[7,8,128]{2,1,0:T(8,128)S(1)} %shard_map.58.refs_0_.refs_1_), channel_id=1, source_target_pairs={{0,3},{1,2},{2,5},{3,4},{4,7},{5,6},{6,1},{7,0},{8,11},{9,10},{10,... | collective-permute-start | bytes 86024 | tf_op jit(solution)/shard_map/ppermute | solution.py:421
  14.6 0.3 collective-permute-done.5.refs_3_
  14.9 1.3 %collective-permute-done.4.refs_2_ = f32[7,8,128]{2,1,0:T(8,128)S(1)} collective-permute-done((f32[7,8,128]{2,1,0:T(8,128)S(1)}, f32[7,8,128]{2,1,0:T(8,128)S(1)}, u32[]{:S(2)}, u32[]{:S(2)}) %collective-permute-start.4) | collective-permute-done | bytes 28704 | tf_op jit(solution)/shard_map/ppermute | solution.py:421
  16.2 2.3 %collective-permute-done.3.refs_1_ = f32[7,8,128]{2,1,0:T(8,128)S(1)} collective-permute-done((f32[7,8,128]{2,1,0:T(8,128)S(1)}, f32[7,8,128]{2,1,0:T(8,128)S(1)}, u32[]{:S(2)}, u32[]{:S(2)}) %collective-permute-start.3) | collective-permute-done | bytes 28704 | tf_op jit(solution)/shard_map/ppermute | solution.py:421
  18.5 3.4 %collective-permute-start.6 = (f32[7,8,128]{2,1,0:T(8,128)S(1)}, f32[7,8,128]{2,1,0:T(8,128)S(1)}, u32[]{:S(2)}, u32[]{:S(2)}) collective-permute-start(f32[7,8,128]{2,1,0:T(8,128)S(1)} %get-tuple-element.46.refs_3_), channel_id=1, source_target_pairs={{0,9},{1,8},{2,11},{3,10},{4,13},{5,12},{6,15},{7,14},{8,1},{9,0},... | collective-permute-start | bytes 86024 | tf_op jit(solution)/shard_map/ppermute | solution.py:415
  22.0 0.4 %shard_map.60 = (f32[1024,128]{1,0:T(8,128)S(1)}, f32[1024,128]{1,0:T(8,128)S(1)}, f32[1024,128]{1,0:T(8,128)S(1)}, f32[3,8,8,128]{3,2,1,0:T(8,128)S(1)}, f32[3,8,128]{2,1,0:T(8,128)S(1)}) custom-call(f32[1024,128]{1,0:T(8,128)S(1)} %get-tuple-element.35.cy_ref.c_ref, f32[2,8,128]{2,1,0:T(8,128)S(1)} %collective-permute-done.1.south_ref), custom_call_target="tpu_custom_call" | custom-call | flops 5000000 | bytes 5000000 | tf_op jit(solution)/shard_map/pallas_call | solution.py:403
  22.4 1.1 %collective-permute-done.6.refs_7_ = f32[7,8,128]{2,1,0:T(8,128)S(1)} collective-permute-done((f32[7,8,128]{2,1,0:T(8,128)S(1)}, f32[7,8,128]{2,1,0:T(8,128)S(1)}, u32[]{:S(2)}, u32[]{:S(2)}) %collective-permute-start.6) | collective-permute-done | bytes 28704 | tf_op jit(solution)/shard_map/ppermute | solution.py:415
  23.5 0.6 %shard_map.61 = (f32[1024,128]{1,0:T(8,128)S(1)}, f32[8,8,128]{2,1,0:T(8,128)S(1)}, f32[8,5,8,128]{3,2,1,0:T(8,128)S(1)}) custom-call(f32[7,8,128]{2,1,0:T(8,128)S(1)} %get-tuple-element.44.refs_0_, f32[7,8,128]{2,1,0:T(8,128)S(1)} %shard_map.58.refs_0_.refs_1_, f32[7,8,128]{2,1,0:T(8,128)S(1)} %get-tuple-element.45.refs_2_, ...), custom_call_target="tpu_custom_call" | custom-call | tf_op jit(solution)/shard_map/pallas_call | solution.py:403
  24.1 10.5 %all_to_all.5.all_ref = f32[8,5,8,128]{3,2,1,0:T(8,128)S(1)} all-to-all(f32[8,5,8,128]{3,2,1,0:T(8,128)S(1)} %get-tuple-element.56), channel_id=1, replica_groups=mesh['row'=8,'col'=16] {'row'}, dimensions={0} | all-to-all | bytes 327680 | tf_op jit(solution)/shard_map/all_to_all | solution.py:479
  34.6 1.1 %shard_map.62 = f32[1024,128]{1,0:T(8,128)} custom-call(f32[8,5,8,128]{3,2,1,0:T(8,128)S(1)} %all_to_all.5.all_ref, f32[1024,128]{1,0:T(8,128)S(1)} %get-tuple-element.51.refs_14_.pr_ref, f32[1024,128]{1,0:T(8,128)S(1)} %get-tuple-element.52.refs_15_.gr_ref, f32[1024,128]{1,0:T(8,128)S(1)} %get-tuple-element.57.rd_ref, ...), custom_call_target="tpu_custom_call" | custom-call | tf_op jit(solution)/shard_map/pallas_call | solution.py:403
  (2 shorter events, 0.1 us)
Async XLA Ops:
  0.9 7.4 %collective-permute-start = (f32[2,8,128]{2,1,0:T(8,128)S(1)}, f32[2,8,128]{2,1,0:T(8,128)S(1)}, u32[]{:S(2)}, u32[]{:S(2)}) collective-permute-start(f32[2,8,128]{2,1,0:T(8,128)S(1)} %get-tuple-element.36), channel_id=1, source_target_pairs={{0,16},{16,32},{32,48},{48,64},{64,80},{80,96},{96,112},{112,0},{1... | collective-permute-start | bytes 24584 | tf_op jit(solution)/shard_map/ppermute | solution.py:452
  3.0 5.3 %collective-permute-start.1 = (f32[2,8,128]{2,1,0:T(8,128)S(1)}, f32[2,8,128]{2,1,0:T(8,128)S(1)}, u32[]{:S(2)}, u32[]{:S(2)}) collective-permute-start(f32[2,8,128]{2,1,0:T(8,128)S(1)} %get-tuple-element.37), channel_id=1, source_target_pairs={{16,0},{32,16},{48,32},{64,48},{80,64},{96,80},{112,96},{0,112},{1... | collective-permute-start | bytes 24584 | tf_op jit(solution)/shard_map/ppermute | solution.py:451
  8.7 1.3 %collective-permute-start.2 = (f32[7,8,128]{2,1,0:T(8,128)S(1)}, f32[7,8,128]{2,1,0:T(8,128)S(1)}, u32[]{:S(2)}, u32[]{:S(2)}) collective-permute-start(f32[7,8,128]{2,1,0:T(8,128)S(1)} %get-tuple-element.44.refs_0_), channel_id=1, source_target_pairs={{0,1},{1,0},{2,3},{3,2},{4,5},{5,4},{6,7},{7,6},{8,9},{9,8},{10,11... | collective-permute-start | bytes 86024 | tf_op jit(solution)/shard_map/ppermute | solution.py:415
  10.0 4.9 %collective-permute-start.5 = (f32[7,8,128]{2,1,0:T(8,128)S(1)}, f32[7,8,128]{2,1,0:T(8,128)S(1)}, u32[]{:S(2)}, u32[]{:S(2)}) collective-permute-start(f32[7,8,128]{2,1,0:T(8,128)S(1)} %shard_map.58.refs_0_.refs_1_), channel_id=1, source_target_pairs={{0,5},{1,4},{2,7},{3,6},{4,1},{5,0},{6,3},{7,2},{8,13},{9,12},{10,... | collective-permute-start | bytes 86024 | tf_op jit(solution)/shard_map/ppermute | solution.py:421
  12.9 3.3 %collective-permute-start.4 = (f32[7,8,128]{2,1,0:T(8,128)S(1)}, f32[7,8,128]{2,1,0:T(8,128)S(1)}, u32[]{:S(2)}, u32[]{:S(2)}) collective-permute-start(f32[7,8,128]{2,1,0:T(8,128)S(1)} %shard_map.58.refs_0_.refs_1_), channel_id=1, source_target_pairs={{0,7},{1,6},{2,1},{3,0},{4,3},{5,2},{6,5},{7,4},{8,15},{9,14},{10,... | collective-permute-start | bytes 86024 | tf_op jit(solution)/shard_map/ppermute | solution.py:421
  14.0 4.5 %collective-permute-start.3 = (f32[7,8,128]{2,1,0:T(8,128)S(1)}, f32[7,8,128]{2,1,0:T(8,128)S(1)}, u32[]{:S(2)}, u32[]{:S(2)}) collective-permute-start(f32[7,8,128]{2,1,0:T(8,128)S(1)} %shard_map.58.refs_0_.refs_1_), channel_id=1, source_target_pairs={{0,3},{1,2},{2,5},{3,4},{4,7},{5,6},{6,1},{7,0},{8,11},{9,10},{10,... | collective-permute-start | bytes 86024 | tf_op jit(solution)/shard_map/ppermute | solution.py:421
  18.5 5.0 %collective-permute-start.6 = (f32[7,8,128]{2,1,0:T(8,128)S(1)}, f32[7,8,128]{2,1,0:T(8,128)S(1)}, u32[]{:S(2)}, u32[]{:S(2)}) collective-permute-start(f32[7,8,128]{2,1,0:T(8,128)S(1)} %get-tuple-element.46.refs_3_), channel_id=1, source_target_pairs={{0,9},{1,8},{2,11},{3,10},{4,13},{5,12},{6,15},{7,14},{8,1},{9,0},... | collective-permute-start | bytes 86024 | tf_op jit(solution)/shard_map/ppermute | solution.py:415

commit v5 on v4

--- a/solution.py
+++ b/solution.py
@@ -149,29 +149,17 @@
 def joined(own, other, left):
     a = [jnp.where(left, x, y) for x, y in zip(own, other)]
     b = [jnp.where(left, y, x) for x, y in zip(own, other)]
-    if len(a) == 5:
-        s, d = a[2] + b[1], a[4] + b[3]
-        r = rcp(a[0] + b[0] + s)
-        f, h = a[0] * r, b[0] * r
-        return [f * b[0], a[1] + f * s, b[2] + h * s, a[3] + f * d, b[4] + h * d]
-    between = link(a[6], b[5])
-    r = rcp(a[0] + between + a[2])
-    f, h = a[0] * r, between * r
-    g1 = f * between
-    s1 = b[1] + h * a[2]
-    d1 = b[3] + h * a[4]
-    left_s = a[1] + f * a[2]
-    left_d = a[3] + f * a[4]
-    r = rcp(g1 + b[0] + s1)
-    f, h = g1 * r, b[0] * r
-    return [f * b[0], left_s + f * s1, b[2] + h * s1, left_d + f * d1, b[4] + h * d1, a[5], b[6]]
-
-
-def ends(me, owns, others):
+    s, d = a[2] + b[1], a[4] + b[3]
+    r = rcp(a[0] + b[0] + s)
+    f, h = a[0] * r, b[0] * r
+    return [f * b[0], a[1] + f * s, b[2] + h * s, a[3] + f * d, b[4] + h * d]
+
+
+def ends(me, own, others):
     zero = jnp.zeros((Z, N), F32)
     yl = il = yr = ir = zero
     for k in reversed(range(len(others))):
-        p, m = others[k], owns[k]
+        p = others[k]
         left = (me >> k) % 2 == 1
         far_s = jnp.where(left, p[1] + yl, p[2] + yr)
         far_d = jnp.where(left, p[3] + il, p[4] + ir)
@@ -179,18 +167,13 @@
         near_d = jnp.where(left, p[4], p[3])
         f = p[0] * rcp(p[0] + far_s)
         y, i = near_s + f * far_s, near_d + f * far_d
-        if len(p) == 7:
-            between = link(jnp.where(left, p[6], p[5]), jnp.where(left, m[5], m[6]))
-            f = between * rcp(between + y)
-            y, i = f * y, f * i
         yl, il = jnp.where(left, y, yl), jnp.where(left, i, il)
         yr, ir = jnp.where(left, yr, y), jnp.where(left, ir, i)
-    m = owns[0]
-    sl, dl, sr, dr = m[1] + yl, m[3] + il, m[2] + yr, m[4] + ir
-    r = rcp(m[0] + sl)
-    f = m[0] * r
+    sl, dl, sr, dr = own[1] + yl, own[3] + il, own[2] + yr, own[4] + ir
+    r = rcp(own[0] + sl)
+    f = own[0] * r
     ur = (dr + f * dl) * rcp(sr + f * sl)
-    ul = (dl + m[0] * ur) * r
+    ul = (dl + own[0] * ur) * r
     return ul, ur
 
 
@@ -223,7 +206,7 @@
 
 def first_kernel(
     par_ref, t_hbm, reg_hbm, s_hbm,
-    ty_ref, cy_ref, r_ref, pr_ref, gr_ref, rr_ref, sep_ref, net_ref, cend_ref,
+    ty_ref, cy_ref, r_ref, pr_ref, gr_ref, rr_ref, sep_ref, net_ref, face_ref,
     cx_ref, t_box, reg_box, s_box, sem,
 ):
     cuts = (0, N // 2 + 8, N)
@@ -275,13 +258,26 @@
     row(N - 1, *state, jnp.zeros((Z, N), F32))
     turn(cy_ref, cx_ref)
     factor(cx_ref, pr_ref, gr_ref, rr_ref, sep_ref, net_ref)
-    cend_ref[0] = cx_ref[at(0), :]
-    cend_ref[1] = cx_ref[at(N - 1), :]
+    g, sl, sr = (net_ref[k] for k in range(3))
+    cl, cr = cx_ref[at(0), :], cx_ref[at(N - 1), :]
+    r = rcp(cl + g + sl)
+    a, b = cl * r, g * r
+    for k, v in enumerate((r, a, b)):
+        face_ref[k] = v
+    g, sr = a * g, sr + b * sl
+    sl = a * sl
+    r = rcp(g + cr + sr)
+    a, b = g * r, cr * r
+    for k, v in enumerate((r, a, b)):
+        face_ref[3 + k] = v
+    net_ref[0] = a * cr
+    net_ref[1] = sl + a * sr
+    net_ref[2] = b * sr
 
 
 def side_kernel(
     r_ref, ty_ref, cy_ref, north_ref, south_ref, pr_ref, gr_ref, rr_ref, sep_ref, net_ref,
-    cx_ref, rd_ref, srd_ref, out_ref, rx_ref, ry_ref,
+    face_ref, rd_ref, srd_ref, frd_ref, out_ref, rx_ref, ry_ref,
 ):
     me = lax.axis_index("row")
     ry_ref[...] = r_ref[...]
@@ -295,10 +291,11 @@
     )
     for k in range(3):
         out_ref[k] = net_ref[k]
-    out_ref[3] = left
-    out_ref[4] = right
-    out_ref[5] = cx_ref[0]
-    out_ref[6] = cx_ref[1]
+    right = right + face_ref[2] * left
+    frd_ref[0] = face_ref[0] * left
+    frd_ref[1] = face_ref[3] * right
+    out_ref[3] = face_ref[1] * left + face_ref[4] * right
+    out_ref[4] = face_ref[5] * right
 
 
 def lines_kernel(c_ref, south_ref, *outs):
@@ -308,8 +305,8 @@
 
 def merge_kernel(axis, own_ref, other_ref, out_ref):
     left = lax.axis_index(axis) % 2 == 0
-    new = joined([own_ref[k] for k in range(7)], [other_ref[k] for k in range(7)], left)
-    for k in range(7):
+    new = joined([own_ref[k] for k in range(5)], [other_ref[k] for k in range(5)], left)
+    for k in range(5):
         out_ref[k] = new[k]
 
 
@@ -317,27 +314,29 @@
     place = lax.axis_index(axis) // 2 % 4
     even = place % 2 == 0
     own, before, after, across = (
-        [r[k] for k in range(7)] for r in (own_ref, before_ref, after_ref, across_ref)
+        [r[k] for k in range(5)] for r in (own_ref, before_ref, after_ref, across_ref)
     )
     near = [jnp.where(even, a, b) for a, b in zip(after, before)]
     far = [jnp.where(even, b, a) for a, b in zip(after, before)]
     pair = joined(own, near, even)
     rest = joined(across, far, even)
     every = joined(pair, rest, place < 2)
-    for out, net in zip(outs, (near, pair, rest, every)):
-        for k in range(7):
+    for out, net in zip(outs, (near, rest, every)):
+        for k in range(5):
             out[k] = net[k]
 
 
 def middle_kernel(*refs):
-    owns, others, refs = refs[:4], refs[4:8], refs[8:]
+    nets, refs = refs[:5], refs[5:]
     (
-        pr_ref, gr_ref, rd_ref, sep_ref, srd_ref, ty_ref,
+        face_ref, frd_ref, pr_ref, gr_ref, rd_ref, sep_ref, srd_ref, ty_ref,
         ypr_ref, ygr_ref, yrr_ref, ysep_ref, ynet_ref,
         yrd_ref, ysrd_ref, out_ref, wx_ref, wy_ref,
     ) = refs
-    nets = [[[r[k] for k in range(7)] for r in group] for group in (owns, others)]
-    ul, ur = ends(lax.axis_index("col"), *nets)
+    own, *others = ([r[k] for k in range(5)] for r in nets)
+    ul, ur = ends(lax.axis_index("col"), own, others)
+    ur = frd_ref[1] + face_ref[4] * ul + face_ref[5] * ur
+    ul = frd_ref[0] + face_ref[1] * ul + face_ref[2] * ur
 
     def put(i, v):
         wx_ref[at(i), :] = v
@@ -362,10 +361,9 @@
     place = lambda m: [all_ref[me ^ m, k] for k in range(5)]
     one, two = me % 2 == 0, me // 2 % 2 == 0
     own = place(0)
-    pair = joined(own, place(1), one)
     far = joined(place(2), place(3), one)
     half = joined(joined(place(4), place(5), one), joined(place(6), place(7), one), two)
-    ul, ur = ends(me, [own, pair, None], [place(1), far, half])
+    ul, ur = ends(me, own, [place(1), far, half])
 
     def put(i, v):
         new_ref[strided(i), :] = v + ty_ref[at(i), :]
@@ -385,8 +383,7 @@
 
 FIELD = (ROWS, N)
 SPACED = (Z, PITCH, N)
-NET = (7, Z, N)
-SHARED = (5, Z, N)
+NET = (5, Z, N)
 PART = (3, Z, N)
 SEPS = (3, CHUNKS, Z, N)
 SEPD = (CHUNKS, Z, N)
@@ -422,17 +419,15 @@
 
 
 def spread_col(net, axis):
-    owns, others = [net], [partner(net, axis, 1)]
-    own = call(lambda *refs: merge_kernel(axis, *refs), [net, others[0]], vm(NET))
+    other = partner(net, axis, 1)
+    own = call(lambda *refs: merge_kernel(axis, *refs), [net, other], vm(NET))
     after = around(own, axis, 3)
     before = around(own, axis, 1)
     across = around(own, axis, 2)
-    near, pair, rest, every = call(
-        lambda *refs: ring_kernel(axis, *refs),
-        [own, before, after, across],
-        (vm(NET),) * 4,
-    )
-    return [net, own, pair, every], others + [near, rest, partner(every, axis, 9)]
+    near, rest, every = call(
+        lambda *refs: ring_kernel(axis, *refs), [own, before, after, across], (vm(NET),) * 3
+    )
+    return [other, near, rest, partner(every, axis, 9)]
 
 
 def local(t, region, source, mag, soft):
@@ -450,30 +445,30 @@
     )(t, region, mag, soft)
     south = lax.ppermute(up, "row", [((i + 1) % n, i) for i in range(n)])
     north = lax.ppermute(down, "row", [(i, (i + 1) % n) for i in range(n)])
-    ty, cy, r, pr, gr, rr, sep, net, cend = call(
+    ty, cy, r, pr, gr, rr, sep, net, face = call(
         first_kernel,
         [par],
-        (vm(FIELD),) * 6 + (vm(SEPS), vm(PART), vm((2, Z, N))),
+        (vm(FIELD),) * 6 + (vm(SEPS), vm(PART), vm((6, Z, N))),
         scratch=[
             vm(FIELD), vm(SPACED), VM(SPACED, jnp.int32), vm(SPACED), pltpu.SemaphoreType.DMA((2, 3)),
         ],
         outside=[t, region, source],
         flops=20_000_000,
     )
-    rd, srd, own = call(
+    rd, srd, frd, own = call(
         side_kernel,
-        [r, ty, cy, north, south, pr, gr, rr, sep, net, cend],
-        (vm(FIELD), vm(SEPD), vm(NET)),
+        [r, ty, cy, north, south, pr, gr, rr, sep, net, face],
+        (vm(FIELD), vm(SEPD), vm((2, Z, N)), vm(NET)),
         scratch=[vm(FIELD), vm(FIELD)],
     )
     ypr, ygr, yrr, ysep, ynet = call(
         lines_kernel, [cy, south], (vm(FIELD),) * 3 + (vm(SEPS), vm(PART)), flops=5_000_000
     )
-    owns, others = spread_col(own, "col")
+    others = spread_col(own, "col")
     yrd, ysrd, send = call(
         middle_kernel,
-        owns + others + [pr, gr, rd, sep, srd, ty, ypr, ygr, yrr, ysep, ynet],
-        (vm(FIELD), vm(SEPD), vm((n,) + SHARED)),
+        [own] + others + [face, frd, pr, gr, rd, sep, srd, ty, ypr, ygr, yrr, ysep, ynet],
+        (vm(FIELD), vm(SEPD), vm((n,) + NET)),
         scratch=[vm(FIELD), vm(FIELD)],
     )
     got = lax.all_to_all(send, "row", 0, 0, tiled=True)

time: 36 us -> 35.6 us (0.989)
  no operation moved by 1% of the time
where the time goes in v5:
time: 35.6 us; the launch traced here: 35.4 us
  starting transfers between devices  12.7 us (36%)
  blocking collectives  10.5 us (29%)
  Pallas kernels  6.12 us (17%)
  waiting for transfers between devices  5.95 us (17%)
    all_to_all x1, blocking collectives, local(): got = lax.all_to_all(send, 'row', 0, 0, tiled=True)  10.5 us
    pallas_call x7, Pallas kernels, call(): pl.pallas_call(kernel, in_specs=[whole] * len(args) + [pl.BlockSpec(memor...  5.22 us
    ppermute x3, starting transfers between devices, around(): return lax.ppermute(x, axis, [(i, to(i)) for i in range(n)])  4.62 us
    ppermute x3, waiting for transfers between devices, around(): return lax.ppermute(x, axis, [(i, to(i)) for i in range(n)])  3.76 us
    ppermute x2, starting transfers between devices, partner(): lax.ppermute(x, axis, [(i, i ^ mask) for i in range(lax.axis_size(axis))])  3.52 us
    ppermute x1, starting transfers between devices, local(): south = lax.ppermute(up, 'row', [((i + 1) % n, i) for i in range(n)])  2.53 us
    ppermute x2, waiting for transfers between devices, partner(): lax.ppermute(x, axis, [(i, i ^ mask) for i in range(lax.axis_size(axis))])  2.18 us
    ppermute x1, starting transfers between devices, local(): north = lax.ppermute(down, 'row', [(i, (i + 1) % n) for i in range(n)])  2.07 us
  transfers between devices with their start and end apart: 7, of which 5 were waited for; matrix products, arithmetic and copies ran while one was open for 0% of the time, Pallas kernels for 9%

profile of v5, /device:TPU:0, one launch (start us, length us, event | category | flops | bytes accessed | tf_op | source)
XLA Modules:
  0.0 35.4 jit_solution(8830308151210664901)
XLA Ops:
  0.0 0.9 %shard_map.55 = (f32[2,8,128]{2,1,0:T(8,128)S(1)}, f32[2,8,128]{2,1,0:T(8,128)S(1)}, f32[6,8,128]{2,1,0:T(8,128)S(1)}) custom-call(f32[8,128,128]{2,1,0:T(8,128)} %t_hbm.3, s32[8,128,128]{2,1,0:T(8,128)} %reg_hbm.3, f32[3]{0:T(128)} %mag_hbm.1, f32[3]{0:T(128)} %soft_hbm.1), custom_call_target="tpu_custom_call" | custom-call | tf_op jit(solution)/shard_map/pallas_call | solution.py:436
  0.9 2.1 %collective-permute-start = (f32[2,8,128]{2,1,0:T(8,128)S(1)}, f32[2,8,128]{2,1,0:T(8,128)S(1)}, u32[]{:S(2)}, u32[]{:S(2)}) collective-permute-start(f32[2,8,128]{2,1,0:T(8,128)S(1)} %get-tuple-element.36), channel_id=1, source_target_pairs={{0,16},{16,32},{32,48},{48,64},{64,80},{80,96},{96,112},{112,0},{1... | collective-permute-start | bytes 24584 | tf_op jit(solution)/shard_map/ppermute | solution.py:447
  3.0 2.5 %collective-permute-start.1 = (f32[2,8,128]{2,1,0:T(8,128)S(1)}, f32[2,8,128]{2,1,0:T(8,128)S(1)}, u32[]{:S(2)}, u32[]{:S(2)}) collective-permute-start(f32[2,8,128]{2,1,0:T(8,128)S(1)} %get-tuple-element.37), channel_id=1, source_target_pairs={{16,0},{32,16},{48,32},{64,48},{80,64},{96,80},{112,96},{0,112},{1... | collective-permute-start | bytes 24584 | tf_op jit(solution)/shard_map/ppermute | solution.py:446
  5.5 2.8 %shard_map.56 = (f32[1024,128]{1,0:T(8,128)S(1)}, f32[1024,128]{1,0:T(8,128)S(1)}, f32[1024,128]{1,0:T(8,128)S(1)}, f32[1024,128]{1,0:T(8,128)S(1)}, f32[1024,12...) custom-call(f32[6,8,128]{2,1,0:T(8,128)S(1)} %get-tuple-element.32.p, ...), custom_call_target="tpu_custom_call" | custom-call | flops 20000000 | bytes 20000000 | tf_op jit(solution)/shard_map/pallas_call | solution.py:400
  8.3 0.0 collective-permute-done.north_ref
  8.3 0.0 collective-permute-done.1.south_ref
  8.3 0.4 %shard_map.57 = (f32[1024,128]{1,0:T(8,128)S(1)}, f32[8,8,128]{2,1,0:T(8,128)S(1)}, f32[2,8,128]{2,1,0:T(8,128)S(1)}, f32[5,8,128]{2,1,0:T(8,128)S(1)}) custom-call(f32[1024,128]{1,0:T(8,128)S(1)} %get-tuple-element.33.r_ref, f32[1024,128]{1,0:T(8,128)S(1)} %get-tuple-element.34.ty_ref.refs_12_, f32[1024,128]{1,0:T(8,128)S(1)} %get-tuple-element.35.cy_ref.c_ref, ...), custom_call_target="tpu_custom_call" | custom-call | tf_op jit(solution)/shard_map/pallas_call | solution.py:400
  8.7 0.1 collective-permute-start.2
  8.8 1.2 %collective-permute-done.2.refs_1_ = f32[5,8,128]{2,1,0:T(8,128)S(1)} collective-permute-done((f32[5,8,128]{2,1,0:T(8,128)S(1)}, f32[5,8,128]{2,1,0:T(8,128)S(1)}, u32[]{:S(2)}, u32[]{:S(2)}) %collective-permute-start.2) | collective-permute-done | bytes 20512 | tf_op jit(solution)/shard_map/ppermute | solution.py:412
  10.0 2.9 %collective-permute-start.5 = (f32[5,8,128]{2,1,0:T(8,128)S(1)}, f32[5,8,128]{2,1,0:T(8,128)S(1)}, u32[]{:S(2)}, u32[]{:S(2)}) collective-permute-start(f32[5,8,128]{2,1,0:T(8,128)S(1)} %shard_map.58.refs_0_), channel_id=1, source_target_pairs={{0,5},{1,4},{2,7},{3,6},{4,1},{5,0},{6,3},{7,2},{8,13},{9,12},{10,... | collective-permute-start | bytes 61448 | tf_op jit(solution)/shard_map/ppermute | solution.py:418
  12.9 1.1 %collective-permute-start.4 = (f32[5,8,128]{2,1,0:T(8,128)S(1)}, f32[5,8,128]{2,1,0:T(8,128)S(1)}, u32[]{:S(2)}, u32[]{:S(2)}) collective-permute-start(f32[5,8,128]{2,1,0:T(8,128)S(1)} %shard_map.58.refs_0_), channel_id=1, source_target_pairs={{0,7},{1,6},{2,1},{3,0},{4,3},{5,2},{6,5},{7,4},{8,15},{9,14},{10,... | collective-permute-start | bytes 61448 | tf_op jit(solution)/shard_map/ppermute | solution.py:418
  14.0 0.7 %collective-permute-start.3 = (f32[5,8,128]{2,1,0:T(8,128)S(1)}, f32[5,8,128]{2,1,0:T(8,128)S(1)}, u32[]{:S(2)}, u32[]{:S(2)}) collective-permute-start(f32[5,8,128]{2,1,0:T(8,128)S(1)} %shard_map.58.refs_0_), channel_id=1, source_target_pairs={{0,3},{1,2},{2,5},{3,4},{4,7},{5,6},{6,1},{7,0},{8,11},{9,10},{10,... | collective-permute-start | bytes 61448 | tf_op jit(solution)/shard_map/ppermute | solution.py:418
  14.6 0.2 collective-permute-done.5.refs_3_
  14.8 1.3 %collective-permute-done.4.refs_2_ = f32[5,8,128]{2,1,0:T(8,128)S(1)} collective-permute-done((f32[5,8,128]{2,1,0:T(8,128)S(1)}, f32[5,8,128]{2,1,0:T(8,128)S(1)}, u32[]{:S(2)}, u32[]{:S(2)}) %collective-permute-start.4) | collective-permute-done | bytes 20512 | tf_op jit(solution)/shard_map/ppermute | solution.py:418
  16.1 2.3 %collective-permute-done.3.refs_1_ = f32[5,8,128]{2,1,0:T(8,128)S(1)} collective-permute-done((f32[5,8,128]{2,1,0:T(8,128)S(1)}, f32[5,8,128]{2,1,0:T(8,128)S(1)}, u32[]{:S(2)}, u32[]{:S(2)}) %collective-permute-start.3) | collective-permute-done | bytes 20512 | tf_op jit(solution)/shard_map/ppermute | solution.py:418
  18.4 3.4 %collective-permute-start.6 = (f32[5,8,128]{2,1,0:T(8,128)S(1)}, f32[5,8,128]{2,1,0:T(8,128)S(1)}, u32[]{:S(2)}, u32[]{:S(2)}) collective-permute-start(f32[5,8,128]{2,1,0:T(8,128)S(1)} %get-tuple-element.47), channel_id=1, source_target_pairs={{0,9},{1,8},{2,11},{3,10},{4,13},{5,12},{6,15},{7,14},{8,1},{9,0},... | collective-permute-start | bytes 61448 | tf_op jit(solution)/shard_map/ppermute | solution.py:412
  21.8 0.5 %shard_map.60 = (f32[1024,128]{1,0:T(8,128)S(1)}, f32[1024,128]{1,0:T(8,128)S(1)}, f32[1024,128]{1,0:T(8,128)S(1)}, f32[3,8,8,128]{3,2,1,0:T(8,128)S(1)}, f32[3,8,128]{2,1,0:T(8,128)S(1)}) custom-call(f32[1024,128]{1,0:T(8,128)S(1)} %get-tuple-element.35.cy_ref.c_ref, f32[2,8,128]{2,1,0:T(8,128)S(1)} %collective-permute-done.1.south_ref), custom_call_target="tpu_custom_call" | custom-call | flops 5000000 | bytes 5000000 | tf_op jit(solution)/shard_map/pallas_call | solution.py:400
  22.3 1.0 %collective-permute-done.6.refs_4_ = f32[5,8,128]{2,1,0:T(8,128)S(1)} collective-permute-done((f32[5,8,128]{2,1,0:T(8,128)S(1)}, f32[5,8,128]{2,1,0:T(8,128)S(1)}, u32[]{:S(2)}, u32[]{:S(2)}) %collective-permute-start.6) | collective-permute-done | bytes 20512 | tf_op jit(solution)/shard_map/ppermute | solution.py:412
  23.3 0.5 %shard_map.61 = (f32[1024,128]{1,0:T(8,128)S(1)}, f32[8,8,128]{2,1,0:T(8,128)S(1)}, f32[8,5,8,128]{3,2,1,0:T(8,128)S(1)}) custom-call(f32[5,8,128]{2,1,0:T(8,128)S(1)} %get-tuple-element.44.refs_0_, f32[5,8,128]{2,1,0:T(8,128)S(1)} %collective-permute-done.2.refs_1_, f32[5,8,128]{2,1,0:T(8,128)S(1)} %get-tuple-element.45.refs_2_, ...), custom_call_target="tpu_custom_call" | custom-call | tf_op jit(solution)/shard_map/pallas_call | solution.py:400
  23.8 10.5 %all_to_all.5.all_ref = f32[8,5,8,128]{3,2,1,0:T(8,128)S(1)} all-to-all(f32[8,5,8,128]{3,2,1,0:T(8,128)S(1)} %get-tuple-element.56), channel_id=1, replica_groups=mesh['row'=8,'col'=16] {'row'}, dimensions={0} | all-to-all | bytes 327680 | tf_op jit(solution)/shard_map/all_to_all | solution.py:474
  34.3 1.1 %shard_map.62 = f32[1024,128]{1,0:T(8,128)} custom-call(f32[8,5,8,128]{3,2,1,0:T(8,128)S(1)} %all_to_all.5.all_ref, f32[1024,128]{1,0:T(8,128)S(1)} %get-tuple-element.51.refs_13_.pr_ref, f32[1024,128]{1,0:T(8,128)S(1)} %get-tuple-element.52.refs_14_.gr_ref, f32[1024,128]{1,0:T(8,128)S(1)} %get-tuple-element.57.rd_ref, ...), custom_call_target="tpu_custom_call" | custom-call | tf_op jit(solution)/shard_map/pallas_call | solution.py:400
  (2 shorter events, 0.0 us)
Async XLA Ops:
  0.9 7.4 %collective-permute-start = (f32[2,8,128]{2,1,0:T(8,128)S(1)}, f32[2,8,128]{2,1,0:T(8,128)S(1)}, u32[]{:S(2)}, u32[]{:S(2)}) collective-permute-start(f32[2,8,128]{2,1,0:T(8,128)S(1)} %get-tuple-element.36), channel_id=1, source_target_pairs={{0,16},{16,32},{32,48},{48,64},{64,80},{80,96},{96,112},{112,0},{1... | collective-permute-start | bytes 24584 | tf_op jit(solution)/shard_map/ppermute | solution.py:447
  3.0 5.4 %collective-permute-start.1 = (f32[2,8,128]{2,1,0:T(8,128)S(1)}, f32[2,8,128]{2,1,0:T(8,128)S(1)}, u32[]{:S(2)}, u32[]{:S(2)}) collective-permute-start(f32[2,8,128]{2,1,0:T(8,128)S(1)} %get-tuple-element.37), channel_id=1, source_target_pairs={{16,0},{32,16},{48,32},{64,48},{80,64},{96,80},{112,96},{0,112},{1... | collective-permute-start | bytes 24584 | tf_op jit(solution)/shard_map/ppermute | solution.py:446
  8.7 1.3 %collective-permute-start.2 = (f32[5,8,128]{2,1,0:T(8,128)S(1)}, f32[5,8,128]{2,1,0:T(8,128)S(1)}, u32[]{:S(2)}, u32[]{:S(2)}) collective-permute-start(f32[5,8,128]{2,1,0:T(8,128)S(1)} %get-tuple-element.44.refs_0_), channel_id=1, source_target_pairs={{0,1},{1,0},{2,3},{3,2},{4,5},{5,4},{6,7},{7,6},{8,9},{9,8},{10,11... | collective-permute-start | bytes 61448 | tf_op jit(solution)/shard_map/ppermute | solution.py:412
  10.0 4.8 %collective-permute-start.5 = (f32[5,8,128]{2,1,0:T(8,128)S(1)}, f32[5,8,128]{2,1,0:T(8,128)S(1)}, u32[]{:S(2)}, u32[]{:S(2)}) collective-permute-start(f32[5,8,128]{2,1,0:T(8,128)S(1)} %shard_map.58.refs_0_), channel_id=1, source_target_pairs={{0,5},{1,4},{2,7},{3,6},{4,1},{5,0},{6,3},{7,2},{8,13},{9,12},{10,... | collective-permute-start | bytes 61448 | tf_op jit(solution)/shard_map/ppermute | solution.py:418
  12.9 3.2 %collective-permute-start.4 = (f32[5,8,128]{2,1,0:T(8,128)S(1)}, f32[5,8,128]{2,1,0:T(8,128)S(1)}, u32[]{:S(2)}, u32[]{:S(2)}) collective-permute-start(f32[5,8,128]{2,1,0:T(8,128)S(1)} %shard_map.58.refs_0_), channel_id=1, source_target_pairs={{0,7},{1,6},{2,1},{3,0},{4,3},{5,2},{6,5},{7,4},{8,15},{9,14},{10,... | collective-permute-start | bytes 61448 | tf_op jit(solution)/shard_map/ppermute | solution.py:418
  14.0 4.4 %collective-permute-start.3 = (f32[5,8,128]{2,1,0:T(8,128)S(1)}, f32[5,8,128]{2,1,0:T(8,128)S(1)}, u32[]{:S(2)}, u32[]{:S(2)}) collective-permute-start(f32[5,8,128]{2,1,0:T(8,128)S(1)} %shard_map.58.refs_0_), channel_id=1, source_target_pairs={{0,3},{1,2},{2,5},{3,4},{4,7},{5,6},{6,1},{7,0},{8,11},{9,10},{10,... | collective-permute-start | bytes 61448 | tf_op jit(solution)/shard_map/ppermute | solution.py:418
  18.4 4.9 %collective-permute-start.6 = (f32[5,8,128]{2,1,0:T(8,128)S(1)}, f32[5,8,128]{2,1,0:T(8,128)S(1)}, u32[]{:S(2)}, u32[]{:S(2)}) collective-permute-start(f32[5,8,128]{2,1,0:T(8,128)S(1)} %get-tuple-element.47), channel_id=1, source_target_pairs={{0,9},{1,8},{2,11},{3,10},{4,13},{5,12},{6,15},{7,14},{8,1},{9,0},... | collective-permute-start | bytes 61448 | tf_op jit(solution)/shard_map/ppermute | solution.py:412

commit v6 on v5

--- a/solution.py
+++ b/solution.py
@@ -121,13 +121,11 @@
     return left, d
 
 
-def back(ul, ur, pr_ref, gr_ref, rd_ref, sep_ref, srd_ref, put, shared):
+def back(ul, ur, pr_ref, gr_ref, rd_ref, sep_ref, srd_ref, put, shared, groups=1, done=None):
     seps = [None] * CHUNKS + [ur]
     for c in range(CHUNKS - 1, 0, -1):
         seps[c] = srd_ref[c] + sep_ref[0, c] * ul + sep_ref[1, c] * seps[c + 1]
     seps[0] = ul
-    for c in range(CHUNKS):
-        put(c * STEP, seps[c])
 
     def cell(c, j, u):
         i = c * STEP + j
@@ -137,13 +135,21 @@
 
     if not shared:
         put(N - 1, ur)
-    last = cell(CHUNKS - 1, STEP - 1, ur) if shared else ur
-    state = [cell(c, STEP - 1, seps[c + 1]) for c in range(CHUNKS - 1)] + [last]
-
-    def body(k, state):
-        return [cell(c, STEP - 2 - k, state[c]) for c in range(CHUNKS)]
-
-    lax.fori_loop(0, STEP - 2, body, state, unroll=True)
+    size = CHUNKS // groups
+    for group in reversed(range(groups)):
+        chunks = range(group * size, group * size + size)
+        state = []
+        for c in chunks:
+            put(c * STEP, seps[c])
+            whole = shared or c < CHUNKS - 1
+            state.append(cell(c, STEP - 1, seps[c + 1]) if whole else ur)
+
+        def body(k, state):
+            return [cell(c, STEP - 2 - k, u) for c, u in zip(chunks, state)]
+
+        lax.fori_loop(0, STEP - 2, body, state, unroll=True)
+        if done is not None:
+            done(group)
 
 
 def joined(own, other, left):
@@ -177,38 +183,32 @@
     return ul, ur
 
 
-def edge_kernel(
-    t_hbm, reg_hbm, mag_hbm, soft_hbm,
-    up_ref, down_ref, par_ref, t_ref, reg_ref, mag_ref, soft_ref, sem,
-):
-    copies = [
-        pltpu.make_async_copy(mag_hbm, mag_ref, sem.at[0]),
-        pltpu.make_async_copy(soft_hbm, soft_ref, sem.at[1]),
-    ]
+def edge_kernel(t_hbm, reg_hbm, up_ref, down_ref, t_ref, reg_ref, sem):
+    copies = []
     for k, first in enumerate((0, N - 8)):
         rows = pl.ds(first, 8)
-        copies.append(pltpu.make_async_copy(t_hbm.at[:, rows, :], t_ref.at[k], sem.at[2 + k]))
-        copies.append(pltpu.make_async_copy(reg_hbm.at[:, rows, :], reg_ref.at[k], sem.at[4 + k]))
-    for copy in copies[2:] + copies[:2]:
+        copies.append(pltpu.make_async_copy(t_hbm.at[:, rows, :], t_ref.at[k], sem.at[0, k]))
+        copies.append(pltpu.make_async_copy(reg_hbm.at[:, rows, :], reg_ref.at[k], sem.at[1, k]))
+    for copy in copies:
         copy.start()
     for copy in copies:
         copy.wait()
-    mag = [jnp.full((Z, N), mag_ref[k] * 1000.0) for k in range(3)]
-    soft = [jnp.full((Z, N), -soft_ref[k]) for k in range(3)]
-    for k in range(3):
-        par_ref[k] = mag[k]
-        par_ref[3 + k] = soft[k]
     for k, row, out in ((0, 0, up_ref), (1, 7, down_ref)):
-        t = t_ref[k, :, row, :]
-        out[0] = t
-        out[1] = conductivity(t, reg_ref[k, :, row, :], mag, soft)
+        out[0] = t_ref[k, :, row, :]
+        out[1] = reg_ref[k, :, row, :].astype(F32)
 
 
 def first_kernel(
-    par_ref, t_hbm, reg_hbm, s_hbm,
-    ty_ref, cy_ref, r_ref, pr_ref, gr_ref, rr_ref, sep_ref, net_ref, face_ref,
-    cx_ref, t_box, reg_box, s_box, sem,
+    t_hbm, reg_hbm, s_hbm, mag_hbm, soft_hbm,
+    par_ref, ty_ref, cy_ref, r_ref, pr_ref, gr_ref, rr_ref, sep_ref, net_ref, face_ref,
+    cx_ref, t_box, reg_box, s_box, mag_ref, soft_ref, sem, small_sem,
 ):
+    small = [
+        pltpu.make_async_copy(mag_hbm, mag_ref, small_sem.at[0]),
+        pltpu.make_async_copy(soft_hbm, soft_ref, small_sem.at[1]),
+    ]
+    for copy in small:
+        copy.start()
     cuts = (0, N // 2 + 8, N)
     copies = [[], []]
     for k in range(2):
@@ -217,8 +217,13 @@
             copies[k].append(pltpu.make_async_copy(a.at[:, rows, :], b.at[:, rows, :], sem.at[k, j]))
             copies[k][-1].start()
     t_ref, reg_ref, s_ref = (box.reshape(Z * PITCH, N) for box in (t_box, reg_box, s_box))
-    mag = [par_ref[k] for k in range(3)]
-    soft = [par_ref[3 + k] for k in range(3)]
+    for copy in small:
+        copy.wait()
+    mag = [jnp.full((Z, N), mag_ref[k] * 1000.0) for k in range(3)]
+    soft = [jnp.full((Z, N), -soft_ref[k]) for k in range(3)]
+    for k in range(3):
+        par_ref[k] = mag[k]
+        par_ref[3 + k] = soft[k]
     z = lax.broadcasted_iota(jnp.int32, (Z, N), 0)
     inner = jnp.where(z < Z - 1, 1.6e-4, 0.0)
     ground = jnp.where(z == 0, 8e-5, 0.0)
@@ -276,15 +281,19 @@
 
 
 def side_kernel(
-    r_ref, ty_ref, cy_ref, north_ref, south_ref, pr_ref, gr_ref, rr_ref, sep_ref, net_ref,
-    face_ref, rd_ref, srd_ref, frd_ref, out_ref, rx_ref, ry_ref,
+    par_ref, r_ref, ty_ref, cy_ref, north_ref, south_ref, pr_ref, gr_ref, rr_ref, sep_ref, net_ref,
+    face_ref, rd_ref, srd_ref, frd_ref, out_ref, beyond_ref, rx_ref, ry_ref,
 ):
     me = lax.axis_index("row")
+    mag = [par_ref[k] for k in range(3)]
+    soft = [par_ref[3 + k] for k in range(3)]
     ry_ref[...] = r_ref[...]
     for row, halo, there in ((0, north_ref, me > 0), (N - 1, south_ref, me < lax.axis_size("row") - 1)):
         i = slice(row * Z, row * Z + Z)
-        flux = link(cy_ref[i, :], halo[1]) * (halo[0] - ty_ref[i, :])
+        beyond = conductivity(halo[0], halo[1], mag, soft)
+        flux = link(cy_ref[i, :], beyond) * (halo[0] - ty_ref[i, :])
         ry_ref[i, :] = r_ref[i, :] + jnp.where(there, 2.0 * flux, 0.0)
+    beyond_ref[...] = beyond
     turn(ry_ref, rx_ref)
     left, right = sweep(
         lambda i: rx_ref[at(i), :], pr_ref, gr_ref, rr_ref, sep_ref, rd_ref, srd_ref, False
@@ -300,7 +309,7 @@
 
 def lines_kernel(c_ref, south_ref, *outs):
     there = lax.axis_index("row") < lax.axis_size("row") - 1
-    factor(c_ref, *outs, south=south_ref[1], there=there)
+    factor(c_ref, *outs, south=south_ref[...], there=there)
 
 
 def merge_kernel(axis, own_ref, other_ref, out_ref):
@@ -355,8 +364,9 @@
 
 
 def last_kernel(
-    all_ref, pr_ref, gr_ref, rd_ref, sep_ref, srd_ref, ty_ref, out_hbm, new_ref, sem
+    all_ref, pr_ref, gr_ref, rd_ref, sep_ref, srd_ref, ty_ref, out_hbm, box, sem
 ):
+    new_ref = box.reshape(Z * PITCH, N)
     me = lax.axis_index("row")
     place = lambda m: [all_ref[me ^ m, k] for k in range(5)]
     one, two = me % 2 == 0, me // 2 % 2 == 0
@@ -368,15 +378,16 @@
     def put(i, v):
         new_ref[strided(i), :] = v + ty_ref[at(i), :]
 
-    back(ul, ur, pr_ref, gr_ref, rd_ref, sep_ref, srd_ref, put, True)
-    copies = [
-        pltpu.make_async_copy(
-            new_ref.at[pl.ds(z * PITCH, N), :], out_hbm.at[pl.ds(z * N, N), :], sem.at[z]
+    copies = []
+
+    def send(group):
+        rows = pl.ds(group * (N // 2), N // 2)
+        copies.append(
+            pltpu.make_async_copy(box.at[:, rows, :], out_hbm.at[:, rows, :], sem.at[group])
         )
-        for z in range(Z)
-    ]
-    for copy in copies:
-        copy.start()
+        copies[-1].start()
+
+    back(ul, ur, pr_ref, gr_ref, rd_ref, sep_ref, srd_ref, put, True, 2, send)
     for copy in copies:
         copy.wait()
 
@@ -433,36 +444,35 @@
 def local(t, region, source, mag, soft):
     n = lax.axis_size("row")
     edge = (2, Z, 8, N)
-    up, down, par = pl.pallas_call(
+    up, down = pl.pallas_call(
         edge_kernel,
-        in_specs=[pl.BlockSpec(memory_space=pltpu.HBM)] * 4,
-        out_specs=(pl.BlockSpec(memory_space=VM),) * 3,
-        out_shape=(vm((2, Z, N)), vm((2, Z, N)), vm((6, Z, N))),
-        scratch_shapes=[
-            vm(edge), VM(edge, jnp.int32), pltpu.SMEM((3,), F32), pltpu.SMEM((3,), F32),
-            pltpu.SemaphoreType.DMA((6,)),
-        ],
-    )(t, region, mag, soft)
+        in_specs=[pl.BlockSpec(memory_space=pltpu.HBM)] * 2,
+        out_specs=(pl.BlockSpec(memory_space=VM),) * 2,
+        out_shape=(vm((2, Z, N)),) * 2,
+        scratch_shapes=[vm(edge), VM(edge, jnp.int32), pltpu.SemaphoreType.DMA((2, 2))],
+    )(t, region)
     south = lax.ppermute(up, "row", [((i + 1) % n, i) for i in range(n)])
     north = lax.ppermute(down, "row", [(i, (i + 1) % n) for i in range(n)])
-    ty, cy, r, pr, gr, rr, sep, net, face = call(
+    par, ty, cy, r, pr, gr, rr, sep, net, face = call(
         first_kernel,
-        [par],
-        (vm(FIELD),) * 6 + (vm(SEPS), vm(PART), vm((6, Z, N))),
+        [],
+        (vm((6, Z, N)),) + (vm(FIELD),) * 6 + (vm(SEPS), vm(PART), vm((6, Z, N))),
         scratch=[
-            vm(FIELD), vm(SPACED), VM(SPACED, jnp.int32), vm(SPACED), pltpu.SemaphoreType.DMA((2, 3)),
+            vm(FIELD), vm(SPACED), VM(SPACED, jnp.int32), vm(SPACED),
+            pltpu.SMEM((3,), F32), pltpu.SMEM((3,), F32),
+            pltpu.SemaphoreType.DMA((2, 3)), pltpu.SemaphoreType.DMA((2,)),
         ],
-        outside=[t, region, source],
+        outside=[t, region, source, mag, soft],
         flops=20_000_000,
     )
-    rd, srd, frd, own = call(
+    rd, srd, frd, own, beyond = call(
         side_kernel,
-        [r, ty, cy, north, south, pr, gr, rr, sep, net, face],
-        (vm(FIELD), vm(SEPD), vm((2, Z, N)), vm(NET)),
+        [par, r, ty, cy, north, south, pr, gr, rr, sep, net, face],
+        (vm(FIELD), vm(SEPD), vm((2, Z, N)), vm(NET), vm((Z, N))),
         scratch=[vm(FIELD), vm(FIELD)],
     )
     ypr, ygr, yrr, ysep, ynet = call(
-        lines_kernel, [cy, south], (vm(FIELD),) * 3 + (vm(SEPS), vm(PART)), flops=5_000_000
+        lines_kernel, [cy, beyond], (vm(FIELD),) * 3 + (vm(SEPS), vm(PART)), flops=5_000_000
     )
     others = spread_col(own, "col")
     yrd, ysrd, send = call(
@@ -475,11 +485,11 @@
     out = call(
         last_kernel,
         [got, ypr, ygr, yrd, ysep, ysrd, ty],
-        jax.ShapeDtypeStruct(FIELD, F32),
-        scratch=[vm((Z * PITCH, N)), pltpu.SemaphoreType.DMA((Z,))],
+        jax.ShapeDtypeStruct((Z, N, N), F32),
+        scratch=[vm(SPACED), pltpu.SemaphoreType.DMA((2,))],
         out_space=pl.ANY,
     )
-    return out.reshape((Z, N, N))
+    return out
 
 
 def solution(mesh):

time: 35.6 us -> 35.5 us (level)
  no operation moved by 1% of the time
where the time goes in v6:
time: 35.5 us; the launch traced here: 35.2 us
  starting transfers between devices  12.7 us (36%)
  blocking collectives  10.5 us (30%)
  Pallas kernels  5.99 us (17%)
  waiting for transfers between devices  5.95 us (17%)
    all_to_all x1, blocking collectives, local(): got = lax.all_to_all(send, 'row', 0, 0, tiled=True)  10.5 us
    pallas_call x7, Pallas kernels, call(): pl.pallas_call(kernel, in_specs=[whole] * len(args) + [pl.BlockSpec(memor...  5.14 us
    ppermute x3, starting transfers between devices, around(): return lax.ppermute(x, axis, [(i, to(i)) for i in range(n)])  4.62 us
    ppermute x3, waiting for transfers between devices, around(): return lax.ppermute(x, axis, [(i, to(i)) for i in range(n)])  3.76 us
    ppermute x2, starting transfers between devices, partner(): lax.ppermute(x, axis, [(i, i ^ mask) for i in range(lax.axis_size(axis))])  3.52 us
    ppermute x1, starting transfers between devices, local(): south = lax.ppermute(up, 'row', [((i + 1) % n, i) for i in range(n)])  2.53 us
    ppermute x2, waiting for transfers between devices, partner(): lax.ppermute(x, axis, [(i, i ^ mask) for i in range(lax.axis_size(axis))])  2.18 us
    ppermute x1, starting transfers between devices, local(): north = lax.ppermute(down, 'row', [(i, (i + 1) % n) for i in range(n)])  2.07 us
  transfers between devices with their start and end apart: 7, of which 5 were waited for; matrix products, arithmetic and copies ran while one was open for 0% of the time, Pallas kernels for 9%

profile of v6, /device:TPU:0, one launch (start us, length us, event | category | flops | bytes accessed | tf_op | source)
XLA Modules:
  0.0 35.2 jit_solution(5350086962740295043)
XLA Ops:
  0.0 0.9 %shard_map.56 = (f32[2,8,128]{2,1,0:T(8,128)S(1)}, f32[2,8,128]{2,1,0:T(8,128)S(1)}) custom-call(f32[8,128,128]{2,1,0:T(8,128)} %t_hbm.3, s32[8,128,128]{2,1,0:T(8,128)} %reg_hbm.3), custom_call_target="tpu_custom_call" | custom-call | tf_op jit(solution)/shard_map/pallas_call | solution.py:447
  0.9 2.1 %collective-permute-start = (f32[2,8,128]{2,1,0:T(8,128)S(1)}, f32[2,8,128]{2,1,0:T(8,128)S(1)}, u32[]{:S(2)}, u32[]{:S(2)}) collective-permute-start(f32[2,8,128]{2,1,0:T(8,128)S(1)} %get-tuple-element.37), channel_id=1, source_target_pairs={{0,16},{16,32},{32,48},{48,64},{64,80},{80,96},{96,112},{112,0},{1... | collective-permute-start | bytes 24584 | tf_op jit(solution)/shard_map/ppermute | solution.py:455
  2.9 2.5 %collective-permute-start.1 = (f32[2,8,128]{2,1,0:T(8,128)S(1)}, f32[2,8,128]{2,1,0:T(8,128)S(1)}, u32[]{:S(2)}, u32[]{:S(2)}) collective-permute-start(f32[2,8,128]{2,1,0:T(8,128)S(1)} %get-tuple-element.38), channel_id=1, source_target_pairs={{16,0},{32,16},{48,32},{64,48},{80,64},{96,80},{112,96},{0,112},{1... | collective-permute-start | bytes 24584 | tf_op jit(solution)/shard_map/ppermute | solution.py:454
  5.5 2.8 %shard_map.55 = (f32[6,8,128]{2,1,0:T(8,128)S(1)}, f32[1024,128]{1,0:T(8,128)S(1)}, f32[1024,128]{1,0:T(8,128)S(1)}, f32[1024,128]{1,0:T(8,128)S(1)}, f32[1024,1...) custom-call(f32[8,128,128]{2,1,0:T(8,128)} %t_hbm.3, ...), custom_call_target="tpu_custom_call" | custom-call | flops 20000000 | bytes 20000000 | tf_op jit(solution)/shard_map/pallas_call | solution.py:411
  8.3 0.0 collective-permute-done.north_ref
  8.3 0.0 collective-permute-done.1.south_ref
  8.3 0.4 %shard_map.57 = (f32[1024,128]{1,0:T(8,128)S(1)}, f32[8,8,128]{2,1,0:T(8,128)S(1)}, f32[2,8,128]{2,1,0:T(8,128)S(1)}, f32[5,8,128]{2,1,0:T(8,128)S(1)}, f32[8,128]{1,0:T(8,128)S(1)}) custom-call(f32[6,8,128]{2,1,0:T(8,128)S(1)} %get-tuple-element.33.par_ref, f32[1024,128]{1,0:T(8,128)S(1)} %get-tuple-element.34.r_ref, ...), custom_call_target="tpu_custom_call" | custom-call | tf_op jit(solution)/shard_map/pallas_call | solution.py:411
  8.7 0.1 collective-permute-start.2
  8.8 1.2 %collective-permute-done.2.refs_1_ = f32[5,8,128]{2,1,0:T(8,128)S(1)} collective-permute-done((f32[5,8,128]{2,1,0:T(8,128)S(1)}, f32[5,8,128]{2,1,0:T(8,128)S(1)}, u32[]{:S(2)}, u32[]{:S(2)}) %collective-permute-start.2) | collective-permute-done | bytes 20512 | tf_op jit(solution)/shard_map/ppermute | solution.py:423
  10.0 2.9 %collective-permute-start.5 = (f32[5,8,128]{2,1,0:T(8,128)S(1)}, f32[5,8,128]{2,1,0:T(8,128)S(1)}, u32[]{:S(2)}, u32[]{:S(2)}) collective-permute-start(f32[5,8,128]{2,1,0:T(8,128)S(1)} %shard_map.58.refs_0_), channel_id=1, source_target_pairs={{0,5},{1,4},{2,7},{3,6},{4,1},{5,0},{6,3},{7,2},{8,13},{9,12},{10,... | collective-permute-start | bytes 61448 | tf_op jit(solution)/shard_map/ppermute | solution.py:429
  12.9 1.1 %collective-permute-start.4 = (f32[5,8,128]{2,1,0:T(8,128)S(1)}, f32[5,8,128]{2,1,0:T(8,128)S(1)}, u32[]{:S(2)}, u32[]{:S(2)}) collective-permute-start(f32[5,8,128]{2,1,0:T(8,128)S(1)} %shard_map.58.refs_0_), channel_id=1, source_target_pairs={{0,7},{1,6},{2,1},{3,0},{4,3},{5,2},{6,5},{7,4},{8,15},{9,14},{10,... | collective-permute-start | bytes 61448 | tf_op jit(solution)/shard_map/ppermute | solution.py:429
  13.9 0.7 %collective-permute-start.3 = (f32[5,8,128]{2,1,0:T(8,128)S(1)}, f32[5,8,128]{2,1,0:T(8,128)S(1)}, u32[]{:S(2)}, u32[]{:S(2)}) collective-permute-start(f32[5,8,128]{2,1,0:T(8,128)S(1)} %shard_map.58.refs_0_), channel_id=1, source_target_pairs={{0,3},{1,2},{2,5},{3,4},{4,7},{5,6},{6,1},{7,0},{8,11},{9,10},{10,... | collective-permute-start | bytes 61448 | tf_op jit(solution)/shard_map/ppermute | solution.py:429
  14.6 0.2 collective-permute-done.5.refs_3_
  14.8 1.3 %collective-permute-done.4.refs_2_ = f32[5,8,128]{2,1,0:T(8,128)S(1)} collective-permute-done((f32[5,8,128]{2,1,0:T(8,128)S(1)}, f32[5,8,128]{2,1,0:T(8,128)S(1)}, u32[]{:S(2)}, u32[]{:S(2)}) %collective-permute-start.4) | collective-permute-done | bytes 20512 | tf_op jit(solution)/shard_map/ppermute | solution.py:429
  16.1 2.3 %collective-permute-done.3.refs_1_ = f32[5,8,128]{2,1,0:T(8,128)S(1)} collective-permute-done((f32[5,8,128]{2,1,0:T(8,128)S(1)}, f32[5,8,128]{2,1,0:T(8,128)S(1)}, u32[]{:S(2)}, u32[]{:S(2)}) %collective-permute-start.3) | collective-permute-done | bytes 20512 | tf_op jit(solution)/shard_map/ppermute | solution.py:429
  18.4 3.4 %collective-permute-start.6 = (f32[5,8,128]{2,1,0:T(8,128)S(1)}, f32[5,8,128]{2,1,0:T(8,128)S(1)}, u32[]{:S(2)}, u32[]{:S(2)}) collective-permute-start(f32[5,8,128]{2,1,0:T(8,128)S(1)} %get-tuple-element.48), channel_id=1, source_target_pairs={{0,9},{1,8},{2,11},{3,10},{4,13},{5,12},{6,15},{7,14},{8,1},{9,0},... | collective-permute-start | bytes 61448 | tf_op jit(solution)/shard_map/ppermute | solution.py:423
  21.8 0.5 %shard_map.60 = (f32[1024,128]{1,0:T(8,128)S(1)}, f32[1024,128]{1,0:T(8,128)S(1)}, f32[1024,128]{1,0:T(8,128)S(1)}, f32[3,8,8,128]{3,2,1,0:T(8,128)S(1)}, f32[3,8,128]{2,1,0:T(8,128)S(1)}) custom-call(f32[1024,128]{1,0:T(8,128)S(1)} %get-tuple-element.36.cy_ref.c_ref, f32[8,128]{1,0:T(8,128)S(1)} %get-tuple-element.52.south_ref), custom_call_target="tpu_custom_call" | custom-call | flops 5000000 | bytes 5000000 | tf_op jit(solution)/shard_map/pallas_call | solution.py:411
  22.3 1.0 %collective-permute-done.6.refs_4_ = f32[5,8,128]{2,1,0:T(8,128)S(1)} collective-permute-done((f32[5,8,128]{2,1,0:T(8,128)S(1)}, f32[5,8,128]{2,1,0:T(8,128)S(1)}, u32[]{:S(2)}, u32[]{:S(2)}) %collective-permute-start.6) | collective-permute-done | bytes 20512 | tf_op jit(solution)/shard_map/ppermute | solution.py:423
  23.3 0.5 %shard_map.61 = (f32[1024,128]{1,0:T(8,128)S(1)}, f32[8,8,128]{2,1,0:T(8,128)S(1)}, f32[8,5,8,128]{3,2,1,0:T(8,128)S(1)}) custom-call(f32[5,8,128]{2,1,0:T(8,128)S(1)} %get-tuple-element.45.refs_0_, f32[5,8,128]{2,1,0:T(8,128)S(1)} %collective-permute-done.2.refs_1_, f32[5,8,128]{2,1,0:T(8,128)S(1)} %get-tuple-element.46.refs_2_, ...), custom_call_target="tpu_custom_call" | custom-call | tf_op jit(solution)/shard_map/pallas_call | solution.py:411
  23.8 10.5 %all_to_all.5.all_ref = f32[8,5,8,128]{3,2,1,0:T(8,128)S(1)} all-to-all(f32[8,5,8,128]{3,2,1,0:T(8,128)S(1)} %get-tuple-element.58), channel_id=1, replica_groups=mesh['row'=8,'col'=16] {'row'}, dimensions={0} | all-to-all | bytes 327680 | tf_op jit(solution)/shard_map/all_to_all | solution.py:484
  34.3 1.0 %shard_map.62 = f32[8,128,128]{2,1,0:T(8,128)} custom-call(f32[8,5,8,128]{3,2,1,0:T(8,128)S(1)} %all_to_all.5.all_ref, f32[1024,128]{1,0:T(8,128)S(1)} %get-tuple-element.53.refs_13_.pr_ref, f32[1024,128]{1,0:T(8,128)S(1)} %get-tuple-element.54.refs_14_.gr_ref, f32[1024,128]{1,0:T(8,128)S(1)} %get-tuple-element.59.rd_ref, ...), custom_call_target="tpu_custom_call" | custom-call | tf_op jit(solution)/shard_map/pallas_call | solution.py:411
  (2 shorter events, 0.0 us)
Async XLA Ops:
  0.9 7.4 %collective-permute-start = (f32[2,8,128]{2,1,0:T(8,128)S(1)}, f32[2,8,128]{2,1,0:T(8,128)S(1)}, u32[]{:S(2)}, u32[]{:S(2)}) collective-permute-start(f32[2,8,128]{2,1,0:T(8,128)S(1)} %get-tuple-element.37), channel_id=1, source_target_pairs={{0,16},{16,32},{32,48},{48,64},{64,80},{80,96},{96,112},{112,0},{1... | collective-permute-start | bytes 24584 | tf_op jit(solution)/shard_map/ppermute | solution.py:455
  2.9 5.4 %collective-permute-start.1 = (f32[2,8,128]{2,1,0:T(8,128)S(1)}, f32[2,8,128]{2,1,0:T(8,128)S(1)}, u32[]{:S(2)}, u32[]{:S(2)}) collective-permute-start(f32[2,8,128]{2,1,0:T(8,128)S(1)} %get-tuple-element.38), channel_id=1, source_target_pairs={{16,0},{32,16},{48,32},{64,48},{80,64},{96,80},{112,96},{0,112},{1... | collective-permute-start | bytes 24584 | tf_op jit(solution)/shard_map/ppermute | solution.py:454
  8.7 1.3 %collective-permute-start.2 = (f32[5,8,128]{2,1,0:T(8,128)S(1)}, f32[5,8,128]{2,1,0:T(8,128)S(1)}, u32[]{:S(2)}, u32[]{:S(2)}) collective-permute-start(f32[5,8,128]{2,1,0:T(8,128)S(1)} %get-tuple-element.45.refs_0_), channel_id=1, source_target_pairs={{0,1},{1,0},{2,3},{3,2},{4,5},{5,4},{6,7},{7,6},{8,9},{9,8},{10,11... | collective-permute-start | bytes 61448 | tf_op jit(solution)/shard_map/ppermute | solution.py:423
  10.0 4.8 %collective-permute-start.5 = (f32[5,8,128]{2,1,0:T(8,128)S(1)}, f32[5,8,128]{2,1,0:T(8,128)S(1)}, u32[]{:S(2)}, u32[]{:S(2)}) collective-permute-start(f32[5,8,128]{2,1,0:T(8,128)S(1)} %shard_map.58.refs_0_), channel_id=1, source_target_pairs={{0,5},{1,4},{2,7},{3,6},{4,1},{5,0},{6,3},{7,2},{8,13},{9,12},{10,... | collective-permute-start | bytes 61448 | tf_op jit(solution)/shard_map/ppermute | solution.py:429
  12.9 3.2 %collective-permute-start.4 = (f32[5,8,128]{2,1,0:T(8,128)S(1)}, f32[5,8,128]{2,1,0:T(8,128)S(1)}, u32[]{:S(2)}, u32[]{:S(2)}) collective-permute-start(f32[5,8,128]{2,1,0:T(8,128)S(1)} %shard_map.58.refs_0_), channel_id=1, source_target_pairs={{0,7},{1,6},{2,1},{3,0},{4,3},{5,2},{6,5},{7,4},{8,15},{9,14},{10,... | collective-permute-start | bytes 61448 | tf_op jit(solution)/shard_map/ppermute | solution.py:429
  13.9 4.4 %collective-permute-start.3 = (f32[5,8,128]{2,1,0:T(8,128)S(1)}, f32[5,8,128]{2,1,0:T(8,128)S(1)}, u32[]{:S(2)}, u32[]{:S(2)}) collective-permute-start(f32[5,8,128]{2,1,0:T(8,128)S(1)} %shard_map.58.refs_0_), channel_id=1, source_target_pairs={{0,3},{1,2},{2,5},{3,4},{4,7},{5,6},{6,1},{7,0},{8,11},{9,10},{10,... | collective-permute-start | bytes 61448 | tf_op jit(solution)/shard_map/ppermute | solution.py:429
  18.4 4.9 %collective-permute-start.6 = (f32[5,8,128]{2,1,0:T(8,128)S(1)}, f32[5,8,128]{2,1,0:T(8,128)S(1)}, u32[]{:S(2)}, u32[]{:S(2)}) collective-permute-start(f32[5,8,128]{2,1,0:T(8,128)S(1)} %get-tuple-element.48), channel_id=1, source_target_pairs={{0,9},{1,8},{2,11},{3,10},{4,13},{5,12},{6,15},{7,14},{8,1},{9,0},... | collective-permute-start | bytes 61448 | tf_op jit(solution)/shard_map/ppermute | solution.py:423

commit v7 on v6

--- a/solution.py
+++ b/solution.py
@@ -312,27 +312,11 @@
     factor(c_ref, *outs, south=south_ref[...], there=there)
 
 
-def merge_kernel(axis, own_ref, other_ref, out_ref):
-    left = lax.axis_index(axis) % 2 == 0
+def level_kernel(axis, level, own_ref, other_ref, out_ref):
+    left = (lax.axis_index(axis) >> level) % 2 == 0
     new = joined([own_ref[k] for k in range(5)], [other_ref[k] for k in range(5)], left)
     for k in range(5):
         out_ref[k] = new[k]
-
-
-def ring_kernel(axis, own_ref, before_ref, after_ref, across_ref, *outs):
-    place = lax.axis_index(axis) // 2 % 4
-    even = place % 2 == 0
-    own, before, after, across = (
-        [r[k] for k in range(5)] for r in (own_ref, before_ref, after_ref, across_ref)
-    )
-    near = [jnp.where(even, a, b) for a, b in zip(after, before)]
-    far = [jnp.where(even, b, a) for a, b in zip(after, before)]
-    pair = joined(own, near, even)
-    rest = joined(across, far, even)
-    every = joined(pair, rest, place < 2)
-    for out, net in zip(outs, (near, rest, every)):
-        for k in range(5):
-            out[k] = net[k]
 
 
 def middle_kernel(*refs):
@@ -423,22 +407,14 @@
     return lax.ppermute(x, axis, [(i, i ^ mask) for i in range(lax.axis_size(axis))])
 
 
-def around(x, axis, shift):
-    n = lax.axis_size(axis)
-    to = lambda i: i // 8 * 8 + (i // 2 + shift) % 4 * 2 + (i + 1) % 2
-    return lax.ppermute(x, axis, [(i, to(i)) for i in range(n)])
-
-
 def spread_col(net, axis):
-    other = partner(net, axis, 1)
-    own = call(lambda *refs: merge_kernel(axis, *refs), [net, other], vm(NET))
-    after = around(own, axis, 3)
-    before = around(own, axis, 1)
-    across = around(own, axis, 2)
-    near, rest, every = call(
-        lambda *refs: ring_kernel(axis, *refs), [own, before, after, across], (vm(NET),) * 3
-    )
-    return [other, near, rest, partner(every, axis, 9)]
+    others = []
+    for level, mask in enumerate((1, 3, 5, 9)):
+        others.append(partner(net, axis, mask))
+        if level < 3:
+            kernel = lambda *refs, level=level: level_kernel(axis, level, *refs)
+            net = call(kernel, [net, others[-1]], vm(NET))
+    return others
 
 
 def local(t, region, source, mag, soft):

time: 35.5 us -> 35.1 us (0.989)
  starting transfers between devices: 12.7 us -> 12.3 us
    ppermute x3 -> x0, starting transfers between devices: 4.62 us -> none  [around(): return lax.ppermute(x, axis, [(i, to(i)) for i in range(n)])]
    ppermute x2 -> x4, starting transfers between devices: 3.52 us -> 7.73 us  [partner(): lax.ppermute(x, axis, [(i, i ^ mask) for i in range(lax.axis_size(axis))])]
    ppermute x2 -> x4, waiting for transfers between devices: 2.18 us -> 6.05 us  [partner(): lax.ppermute(x, axis, [(i, i ^ mask) for i in range(lax.axis_size(axis))])]
    ppermute x3 -> x0, waiting for transfers between devices: 3.76 us -> none  [around(): return lax.ppermute(x, axis, [(i, to(i)) for i in range(n)])]
    pallas_call x7 -> x8, Pallas kernels: 5.14 us -> 5.14 us  [call(): pl.pallas_call(kernel, in_specs=[whole] * len(args) + [pl.BlockSpec(memor...]
  transfers between devices with their start and end apart: 7 -> 6, of which waited for: 5 -> 4; matrix products, arithmetic and copies ran while one was open for 0% -> 0% of each run, Pallas kernels for 9% -> 9%
where the time goes in v7:
time: 35.1 us; the launch traced here: 34.9 us
  starting transfers between devices  12.3 us (35%)
  blocking collectives  10.5 us (30%)
  waiting for transfers between devices  6.05 us (17%)
  Pallas kernels  5.99 us (17%)
    all_to_all x1, blocking collectives, local(): got = lax.all_to_all(send, 'row', 0, 0, tiled=True)  10.5 us
    ppermute x4, starting transfers between devices, partner(): lax.ppermute(x, axis, [(i, i ^ mask) for i in range(lax.axis_size(axis))])  7.73 us
    ppermute x4, waiting for transfers between devices, partner(): lax.ppermute(x, axis, [(i, i ^ mask) for i in range(lax.axis_size(axis))])  6.05 us
    pallas_call x8, Pallas kernels, call(): pl.pallas_call(kernel, in_specs=[whole] * len(args) + [pl.BlockSpec(memor...  5.14 us
    ppermute x1, starting transfers between devices, local(): south = lax.ppermute(up, 'row', [((i + 1) % n, i) for i in range(n)])  2.53 us
    ppermute x1, starting transfers between devices, local(): north = lax.ppermute(down, 'row', [(i, (i + 1) % n) for i in range(n)])  2.07 us
    pallas_call x1, Pallas kernels, local(): pl.pallas_call(edge_kernel, in_specs=[pl.BlockSpec(memory_space=pltpu.HBM...  0.85 us
  transfers between devices with their start and end apart: 6, of which 4 were waited for; matrix products, arithmetic and copies ran while one was open for 0% of the time, Pallas kernels for 9%

profile of v7, /device:TPU:0, one launch (start us, length us, event | category | flops | bytes accessed | tf_op | source)
XLA Modules:
  0.0 34.9 jit_solution(10067047058163900559)
XLA Ops:
  0.0 0.9 %shard_map.56 = (f32[2,8,128]{2,1,0:T(8,128)S(1)}, f32[2,8,128]{2,1,0:T(8,128)S(1)}) custom-call(f32[8,128,128]{2,1,0:T(8,128)} %t_hbm.3, s32[8,128,128]{2,1,0:T(8,128)} %reg_hbm.3), custom_call_target="tpu_custom_call" | custom-call | tf_op jit(solution)/shard_map/pallas_call | solution.py:423
  0.9 2.1 %collective-permute-start = (f32[2,8,128]{2,1,0:T(8,128)S(1)}, f32[2,8,128]{2,1,0:T(8,128)S(1)}, u32[]{:S(2)}, u32[]{:S(2)}) collective-permute-start(f32[2,8,128]{2,1,0:T(8,128)S(1)} %get-tuple-element.34), channel_id=1, source_target_pairs={{0,16},{16,32},{32,48},{48,64},{64,80},{80,96},{96,112},{112,0},{1... | collective-permute-start | bytes 24584 | tf_op jit(solution)/shard_map/ppermute | solution.py:431
  2.9 2.5 %collective-permute-start.1 = (f32[2,8,128]{2,1,0:T(8,128)S(1)}, f32[2,8,128]{2,1,0:T(8,128)S(1)}, u32[]{:S(2)}, u32[]{:S(2)}) collective-permute-start(f32[2,8,128]{2,1,0:T(8,128)S(1)} %get-tuple-element.35), channel_id=1, source_target_pairs={{16,0},{32,16},{48,32},{64,48},{80,64},{96,80},{112,96},{0,112},{1... | collective-permute-start | bytes 24584 | tf_op jit(solution)/shard_map/ppermute | solution.py:430
  5.5 2.8 %shard_map.55 = (f32[6,8,128]{2,1,0:T(8,128)S(1)}, f32[1024,128]{1,0:T(8,128)S(1)}, f32[1024,128]{1,0:T(8,128)S(1)}, f32[1024,128]{1,0:T(8,128)S(1)}, f32[1024,1...) custom-call(f32[8,128,128]{2,1,0:T(8,128)} %t_hbm.3, ...), custom_call_target="tpu_custom_call" | custom-call | flops 20000000 | bytes 20000000 | tf_op jit(solution)/shard_map/pallas_call | solution.py:395
  8.3 0.0 collective-permute-done.north_ref
  8.3 0.0 collective-permute-done.1.south_ref
  8.3 0.4 %shard_map.57 = (f32[1024,128]{1,0:T(8,128)S(1)}, f32[8,8,128]{2,1,0:T(8,128)S(1)}, f32[2,8,128]{2,1,0:T(8,128)S(1)}, f32[5,8,128]{2,1,0:T(8,128)S(1)}, f32[8,128]{1,0:T(8,128)S(1)}) custom-call(f32[6,8,128]{2,1,0:T(8,128)S(1)} %get-tuple-element.30.par_ref, f32[1024,128]{1,0:T(8,128)S(1)} %get-tuple-element.31.r_ref, ...), custom_call_target="tpu_custom_call" | custom-call | tf_op jit(solution)/shard_map/pallas_call | solution.py:395
  8.7 0.1 collective-permute-start.2
  8.8 1.2 %collective-permute-done.2.refs_1_ = f32[5,8,128]{2,1,0:T(8,128)S(1)} collective-permute-done((f32[5,8,128]{2,1,0:T(8,128)S(1)}, f32[5,8,128]{2,1,0:T(8,128)S(1)}, u32[]{:S(2)}, u32[]{:S(2)}) %collective-permute-start.2) | collective-permute-done | bytes 20512 | tf_op jit(solution)/shard_map/ppermute | solution.py:407
  10.0 1.3 %collective-permute-start.3 = (f32[5,8,128]{2,1,0:T(8,128)S(1)}, f32[5,8,128]{2,1,0:T(8,128)S(1)}, u32[]{:S(2)}, u32[]{:S(2)}) collective-permute-start(f32[5,8,128]{2,1,0:T(8,128)S(1)} %shard_map.58.refs_0_), channel_id=1, source_target_pairs={{0,3},{1,2},{2,1},{3,0},{4,7},{5,6},{6,5},{7,4},{8,11},{9,10},{10,... | collective-permute-start | bytes 61448 | tf_op jit(solution)/shard_map/ppermute | solution.py:407
  11.3 1.9 %collective-permute-done.3.refs_1_.refs_2_ = f32[5,8,128]{2,1,0:T(8,128)S(1)} collective-permute-done((f32[5,8,128]{2,1,0:T(8,128)S(1)}, f32[5,8,128]{2,1,0:T(8,128)S(1)}, u32[]{:S(2)}, u32[]{:S(2)}) %collective-permute-start.3) | collective-permute-done | bytes 20512 | tf_op jit(solution)/shard_map/ppermute | solution.py:407
  13.3 2.9 %collective-permute-start.4 = (f32[5,8,128]{2,1,0:T(8,128)S(1)}, f32[5,8,128]{2,1,0:T(8,128)S(1)}, u32[]{:S(2)}, u32[]{:S(2)}) collective-permute-start(f32[5,8,128]{2,1,0:T(8,128)S(1)} %shard_map.59.refs_0_), channel_id=1, source_target_pairs={{0,5},{1,4},{2,7},{3,6},{4,1},{5,0},{6,3},{7,2},{8,13},{9,12},{10,... | collective-permute-start | bytes 61448 | tf_op jit(solution)/shard_map/ppermute | solution.py:407
  16.2 1.9 %collective-permute-done.4.refs_1_.refs_3_ = f32[5,8,128]{2,1,0:T(8,128)S(1)} collective-permute-done((f32[5,8,128]{2,1,0:T(8,128)S(1)}, f32[5,8,128]{2,1,0:T(8,128)S(1)}, u32[]{:S(2)}, u32[]{:S(2)}) %collective-permute-start.4) | collective-permute-done | bytes 20512 | tf_op jit(solution)/shard_map/ppermute | solution.py:407
  18.1 3.4 %collective-permute-start.5 = (f32[5,8,128]{2,1,0:T(8,128)S(1)}, f32[5,8,128]{2,1,0:T(8,128)S(1)}, u32[]{:S(2)}, u32[]{:S(2)}) collective-permute-start(f32[5,8,128]{2,1,0:T(8,128)S(1)} %shard_map.60), channel_id=1, source_target_pairs={{0,9},{1,8},{2,11},{3,10},{4,13},{5,12},{6,15},{7,14},{8,1},{9,0},... | collective-permute-start | bytes 61448 | tf_op jit(solution)/shard_map/ppermute | solution.py:407
  21.5 0.5 %shard_map.61 = (f32[1024,128]{1,0:T(8,128)S(1)}, f32[1024,128]{1,0:T(8,128)S(1)}, f32[1024,128]{1,0:T(8,128)S(1)}, f32[3,8,8,128]{3,2,1,0:T(8,128)S(1)}, f32[3,8,128]{2,1,0:T(8,128)S(1)}) custom-call(f32[1024,128]{1,0:T(8,128)S(1)} %get-tuple-element.33.cy_ref.c_ref, f32[8,128]{1,0:T(8,128)S(1)} %get-tuple-element.46.south_ref), custom_call_target="tpu_custom_call" | custom-call | flops 5000000 | bytes 5000000 | tf_op jit(solution)/shard_map/pallas_call | solution.py:395
  22.0 1.0 %collective-permute-done.5.refs_4_ = f32[5,8,128]{2,1,0:T(8,128)S(1)} collective-permute-done((f32[5,8,128]{2,1,0:T(8,128)S(1)}, f32[5,8,128]{2,1,0:T(8,128)S(1)}, u32[]{:S(2)}, u32[]{:S(2)}) %collective-permute-start.5) | collective-permute-done | bytes 20512 | tf_op jit(solution)/shard_map/ppermute | solution.py:407
  23.0 0.5 %shard_map.62 = (f32[1024,128]{1,0:T(8,128)S(1)}, f32[8,8,128]{2,1,0:T(8,128)S(1)}, f32[8,5,8,128]{3,2,1,0:T(8,128)S(1)}) custom-call(f32[5,8,128]{2,1,0:T(8,128)S(1)} %get-tuple-element.42.refs_0_, f32[5,8,128]{2,1,0:T(8,128)S(1)} %collective-permute-done.2.refs_1_, f32[5,8,128]{2,1,0:T(8,128)S(1)} %collective-permute-done.3.refs_1_.refs_2_, ...), custom_call_target="tpu_custom_call" | custom-call | tf_op jit(solution)/shard_map/pallas_call | solution.py:395
  23.5 10.5 %all_to_all.5.all_ref = f32[8,5,8,128]{3,2,1,0:T(8,128)S(1)} all-to-all(f32[8,5,8,128]{3,2,1,0:T(8,128)S(1)} %get-tuple-element.52), channel_id=1, replica_groups=mesh['row'=8,'col'=16] {'row'}, dimensions={0} | all-to-all | bytes 327680 | tf_op jit(solution)/shard_map/all_to_all | solution.py:460
  34.0 1.0 %shard_map.63 = f32[8,128,128]{2,1,0:T(8,128)} custom-call(f32[8,5,8,128]{3,2,1,0:T(8,128)S(1)} %all_to_all.5.all_ref, f32[1024,128]{1,0:T(8,128)S(1)} %get-tuple-element.47.refs_13_.pr_ref, f32[1024,128]{1,0:T(8,128)S(1)} %get-tuple-element.48.refs_14_.gr_ref, f32[1024,128]{1,0:T(8,128)S(1)} %get-tuple-element.53.rd_ref, ...), custom_call_target="tpu_custom_call" | custom-call | tf_op jit(solution)/shard_map/pallas_call | solution.py:395
  (3 shorter events, 0.0 us)
Async XLA Ops:
  0.9 7.4 %collective-permute-start = (f32[2,8,128]{2,1,0:T(8,128)S(1)}, f32[2,8,128]{2,1,0:T(8,128)S(1)}, u32[]{:S(2)}, u32[]{:S(2)}) collective-permute-start(f32[2,8,128]{2,1,0:T(8,128)S(1)} %get-tuple-element.34), channel_id=1, source_target_pairs={{0,16},{16,32},{32,48},{48,64},{64,80},{80,96},{96,112},{112,0},{1... | collective-permute-start | bytes 24584 | tf_op jit(solution)/shard_map/ppermute | solution.py:431
  2.9 5.4 %collective-permute-start.1 = (f32[2,8,128]{2,1,0:T(8,128)S(1)}, f32[2,8,128]{2,1,0:T(8,128)S(1)}, u32[]{:S(2)}, u32[]{:S(2)}) collective-permute-start(f32[2,8,128]{2,1,0:T(8,128)S(1)} %get-tuple-element.35), channel_id=1, source_target_pairs={{16,0},{32,16},{48,32},{64,48},{80,64},{96,80},{112,96},{0,112},{1... | collective-permute-start | bytes 24584 | tf_op jit(solution)/shard_map/ppermute | solution.py:430
  8.7 1.3 %collective-permute-start.2 = (f32[5,8,128]{2,1,0:T(8,128)S(1)}, f32[5,8,128]{2,1,0:T(8,128)S(1)}, u32[]{:S(2)}, u32[]{:S(2)}) collective-permute-start(f32[5,8,128]{2,1,0:T(8,128)S(1)} %get-tuple-element.42.refs_0_), channel_id=1, source_target_pairs={{0,1},{1,0},{2,3},{3,2},{4,5},{5,4},{6,7},{7,6},{8,9},{9,8},{10,11... | collective-permute-start | bytes 61448 | tf_op jit(solution)/shard_map/ppermute | solution.py:407
  10.0 3.3 %collective-permute-start.3 = (f32[5,8,128]{2,1,0:T(8,128)S(1)}, f32[5,8,128]{2,1,0:T(8,128)S(1)}, u32[]{:S(2)}, u32[]{:S(2)}) collective-permute-start(f32[5,8,128]{2,1,0:T(8,128)S(1)} %shard_map.58.refs_0_), channel_id=1, source_target_pairs={{0,3},{1,2},{2,1},{3,0},{4,7},{5,6},{6,5},{7,4},{8,11},{9,10},{10,... | collective-permute-start | bytes 61448 | tf_op jit(solution)/shard_map/ppermute | solution.py:407
  13.3 4.8 %collective-permute-start.4 = (f32[5,8,128]{2,1,0:T(8,128)S(1)}, f32[5,8,128]{2,1,0:T(8,128)S(1)}, u32[]{:S(2)}, u32[]{:S(2)}) collective-permute-start(f32[5,8,128]{2,1,0:T(8,128)S(1)} %shard_map.59.refs_0_), channel_id=1, source_target_pairs={{0,5},{1,4},{2,7},{3,6},{4,1},{5,0},{6,3},{7,2},{8,13},{9,12},{10,... | collective-permute-start | bytes 61448 | tf_op jit(solution)/shard_map/ppermute | solution.py:407
  18.1 4.9 %collective-permute-start.5 = (f32[5,8,128]{2,1,0:T(8,128)S(1)}, f32[5,8,128]{2,1,0:T(8,128)S(1)}, u32[]{:S(2)}, u32[]{:S(2)}) collective-permute-start(f32[5,8,128]{2,1,0:T(8,128)S(1)} %shard_map.60), channel_id=1, source_target_pairs={{0,9},{1,8},{2,11},{3,10},{4,13},{5,12},{6,15},{7,14},{8,1},{9,0},... | collective-permute-start | bytes 61448 | tf_op jit(solution)/shard_map/ppermute | solution.py:407

commit v8 on v7

--- a/solution.py
+++ b/solution.py
@@ -409,7 +409,7 @@
 
 def spread_col(net, axis):
     others = []
-    for level, mask in enumerate((1, 3, 5, 9)):
+    for level, mask in enumerate((1, 3, 7, 9)):
         others.append(partner(net, axis, mask))
         if level < 3:
             kernel = lambda *refs, level=level: level_kernel(axis, level, *refs)

time: 35.1 us -> 34.9 us (level)
  transfers between devices with their start and end apart: 6 -> 6, of which waited for: 4 -> 4; matrix products, arithmetic and copies ran while one was open for 0% -> 0% of each run, Pallas kernels for 9% -> 10%
where the time goes in v8:
time: 34.9 us; the launch traced here: 34.6 us
  starting transfers between devices  12.1 us (35%)
  blocking collectives  10.5 us (30%)
  waiting for transfers between devices  6.03 us (17%)
  Pallas kernels  5.99 us (17%)
    all_to_all x1, blocking collectives, local(): got = lax.all_to_all(send, 'row', 0, 0, tiled=True)  10.5 us
    ppermute x4, starting transfers between devices, partner(): lax.ppermute(x, axis, [(i, i ^ mask) for i in range(lax.axis_size(axis))])  7.46 us
    ppermute x4, waiting for transfers between devices, partner(): lax.ppermute(x, axis, [(i, i ^ mask) for i in range(lax.axis_size(axis))])  6.02 us
    pallas_call x8, Pallas kernels, call(): pl.pallas_call(kernel, in_specs=[whole] * len(args) + [pl.BlockSpec(memor...  5.14 us
    ppermute x1, starting transfers between devices, local(): south = lax.ppermute(up, 'row', [((i + 1) % n, i) for i in range(n)])  2.53 us
    ppermute x1, starting transfers between devices, local(): north = lax.ppermute(down, 'row', [(i, (i + 1) % n) for i in range(n)])  2.07 us
    pallas_call x1, Pallas kernels, local(): pl.pallas_call(edge_kernel, in_specs=[pl.BlockSpec(memory_space=pltpu.HBM...  0.85 us
  transfers between devices with their start and end apart: 6, of which 4 were waited for; matrix products, arithmetic and copies ran while one was open for 0% of the time, Pallas kernels for 10%

profile of v8, /device:TPU:0, one launch (start us, length us, event | category | flops | bytes accessed | tf_op | source)
XLA Modules:
  0.0 34.6 jit_solution(14290040164183690231)
XLA Ops:
  0.0 0.9 %shard_map.56 = (f32[2,8,128]{2,1,0:T(8,128)S(1)}, f32[2,8,128]{2,1,0:T(8,128)S(1)}) custom-call(f32[8,128,128]{2,1,0:T(8,128)} %t_hbm.3, s32[8,128,128]{2,1,0:T(8,128)} %reg_hbm.3), custom_call_target="tpu_custom_call" | custom-call | tf_op jit(solution)/shard_map/pallas_call | solution.py:423
  0.9 2.1 %collective-permute-start = (f32[2,8,128]{2,1,0:T(8,128)S(1)}, f32[2,8,128]{2,1,0:T(8,128)S(1)}, u32[]{:S(2)}, u32[]{:S(2)}) collective-permute-start(f32[2,8,128]{2,1,0:T(8,128)S(1)} %get-tuple-element.34), channel_id=1, source_target_pairs={{0,16},{16,32},{32,48},{48,64},{64,80},{80,96},{96,112},{112,0},{1... | collective-permute-start | bytes 24584 | tf_op jit(solution)/shard_map/ppermute | solution.py:431
  2.9 2.5 %collective-permute-start.1 = (f32[2,8,128]{2,1,0:T(8,128)S(1)}, f32[2,8,128]{2,1,0:T(8,128)S(1)}, u32[]{:S(2)}, u32[]{:S(2)}) collective-permute-start(f32[2,8,128]{2,1,0:T(8,128)S(1)} %get-tuple-element.35), channel_id=1, source_target_pairs={{16,0},{32,16},{48,32},{64,48},{80,64},{96,80},{112,96},{0,112},{1... | collective-permute-start | bytes 24584 | tf_op jit(solution)/shard_map/ppermute | solution.py:430
  5.5 2.8 %shard_map.55 = (f32[6,8,128]{2,1,0:T(8,128)S(1)}, f32[1024,128]{1,0:T(8,128)S(1)}, f32[1024,128]{1,0:T(8,128)S(1)}, f32[1024,128]{1,0:T(8,128)S(1)}, f32[1024,1...) custom-call(f32[8,128,128]{2,1,0:T(8,128)} %t_hbm.3, ...), custom_call_target="tpu_custom_call" | custom-call | flops 20000000 | bytes 20000000 | tf_op jit(solution)/shard_map/pallas_call | solution.py:395
  8.3 0.0 collective-permute-done.north_ref
  8.3 0.0 collective-permute-done.1.south_ref
  8.3 0.4 %shard_map.57 = (f32[1024,128]{1,0:T(8,128)S(1)}, f32[8,8,128]{2,1,0:T(8,128)S(1)}, f32[2,8,128]{2,1,0:T(8,128)S(1)}, f32[5,8,128]{2,1,0:T(8,128)S(1)}, f32[8,128]{1,0:T(8,128)S(1)}) custom-call(f32[6,8,128]{2,1,0:T(8,128)S(1)} %get-tuple-element.30.par_ref, f32[1024,128]{1,0:T(8,128)S(1)} %get-tuple-element.31.r_ref, ...), custom_call_target="tpu_custom_call" | custom-call | tf_op jit(solution)/shard_map/pallas_call | solution.py:395
  8.7 0.1 collective-permute-start.2
  8.8 1.2 %collective-permute-done.2.refs_1_ = f32[5,8,128]{2,1,0:T(8,128)S(1)} collective-permute-done((f32[5,8,128]{2,1,0:T(8,128)S(1)}, f32[5,8,128]{2,1,0:T(8,128)S(1)}, u32[]{:S(2)}, u32[]{:S(2)}) %collective-permute-start.2) | collective-permute-done | bytes 20512 | tf_op jit(solution)/shard_map/ppermute | solution.py:407
  10.0 1.3 %collective-permute-start.3 = (f32[5,8,128]{2,1,0:T(8,128)S(1)}, f32[5,8,128]{2,1,0:T(8,128)S(1)}, u32[]{:S(2)}, u32[]{:S(2)}) collective-permute-start(f32[5,8,128]{2,1,0:T(8,128)S(1)} %shard_map.58.refs_0_), channel_id=1, source_target_pairs={{0,3},{1,2},{2,1},{3,0},{4,7},{5,6},{6,5},{7,4},{8,11},{9,10},{10,... | collective-permute-start | bytes 61448 | tf_op jit(solution)/shard_map/ppermute | solution.py:407
  11.3 1.9 %collective-permute-done.3.refs_1_.refs_2_ = f32[5,8,128]{2,1,0:T(8,128)S(1)} collective-permute-done((f32[5,8,128]{2,1,0:T(8,128)S(1)}, f32[5,8,128]{2,1,0:T(8,128)S(1)}, u32[]{:S(2)}, u32[]{:S(2)}) %collective-permute-start.3) | collective-permute-done | bytes 20512 | tf_op jit(solution)/shard_map/ppermute | solution.py:407
  13.3 2.6 %collective-permute-start.4 = (f32[5,8,128]{2,1,0:T(8,128)S(1)}, f32[5,8,128]{2,1,0:T(8,128)S(1)}, u32[]{:S(2)}, u32[]{:S(2)}) collective-permute-start(f32[5,8,128]{2,1,0:T(8,128)S(1)} %shard_map.59.refs_0_), channel_id=1, source_target_pairs={{0,7},{1,6},{2,5},{3,4},{4,3},{5,2},{6,1},{7,0},{8,15},{9,14},{10,... | collective-permute-start | bytes 61448 | tf_op jit(solution)/shard_map/ppermute | solution.py:407
  15.9 1.9 %collective-permute-done.4.refs_1_.refs_3_ = f32[5,8,128]{2,1,0:T(8,128)S(1)} collective-permute-done((f32[5,8,128]{2,1,0:T(8,128)S(1)}, f32[5,8,128]{2,1,0:T(8,128)S(1)}, u32[]{:S(2)}, u32[]{:S(2)}) %collective-permute-start.4) | collective-permute-done | bytes 20512 | tf_op jit(solution)/shard_map/ppermute | solution.py:407
  17.8 3.4 %collective-permute-start.5 = (f32[5,8,128]{2,1,0:T(8,128)S(1)}, f32[5,8,128]{2,1,0:T(8,128)S(1)}, u32[]{:S(2)}, u32[]{:S(2)}) collective-permute-start(f32[5,8,128]{2,1,0:T(8,128)S(1)} %shard_map.60), channel_id=1, source_target_pairs={{0,9},{1,8},{2,11},{3,10},{4,13},{5,12},{6,15},{7,14},{8,1},{9,0},... | collective-permute-start | bytes 61448 | tf_op jit(solution)/shard_map/ppermute | solution.py:407
  21.2 0.5 %shard_map.61 = (f32[1024,128]{1,0:T(8,128)S(1)}, f32[1024,128]{1,0:T(8,128)S(1)}, f32[1024,128]{1,0:T(8,128)S(1)}, f32[3,8,8,128]{3,2,1,0:T(8,128)S(1)}, f32[3,8,128]{2,1,0:T(8,128)S(1)}) custom-call(f32[1024,128]{1,0:T(8,128)S(1)} %get-tuple-element.33.cy_ref.c_ref, f32[8,128]{1,0:T(8,128)S(1)} %get-tuple-element.46.south_ref), custom_call_target="tpu_custom_call" | custom-call | flops 5000000 | bytes 5000000 | tf_op jit(solution)/shard_map/pallas_call | solution.py:395
  21.7 1.0 %collective-permute-done.5.refs_4_ = f32[5,8,128]{2,1,0:T(8,128)S(1)} collective-permute-done((f32[5,8,128]{2,1,0:T(8,128)S(1)}, f32[5,8,128]{2,1,0:T(8,128)S(1)}, u32[]{:S(2)}, u32[]{:S(2)}) %collective-permute-start.5) | collective-permute-done | bytes 20512 | tf_op jit(solution)/shard_map/ppermute | solution.py:407
  22.7 0.5 %shard_map.62 = (f32[1024,128]{1,0:T(8,128)S(1)}, f32[8,8,128]{2,1,0:T(8,128)S(1)}, f32[8,5,8,128]{3,2,1,0:T(8,128)S(1)}) custom-call(f32[5,8,128]{2,1,0:T(8,128)S(1)} %get-tuple-element.42.refs_0_, f32[5,8,128]{2,1,0:T(8,128)S(1)} %collective-permute-done.2.refs_1_, f32[5,8,128]{2,1,0:T(8,128)S(1)} %collective-permute-done.3.refs_1_.refs_2_, ...), custom_call_target="tpu_custom_call" | custom-call | tf_op jit(solution)/shard_map/pallas_call | solution.py:395
  23.2 10.5 %all_to_all.5.all_ref = f32[8,5,8,128]{3,2,1,0:T(8,128)S(1)} all-to-all(f32[8,5,8,128]{3,2,1,0:T(8,128)S(1)} %get-tuple-element.52), channel_id=1, replica_groups=mesh['row'=8,'col'=16] {'row'}, dimensions={0} | all-to-all | bytes 327680 | tf_op jit(solution)/shard_map/all_to_all | solution.py:460
  33.7 1.0 %shard_map.63 = f32[8,128,128]{2,1,0:T(8,128)} custom-call(f32[8,5,8,128]{3,2,1,0:T(8,128)S(1)} %all_to_all.5.all_ref, f32[1024,128]{1,0:T(8,128)S(1)} %get-tuple-element.47.refs_13_.pr_ref, f32[1024,128]{1,0:T(8,128)S(1)} %get-tuple-element.48.refs_14_.gr_ref, f32[1024,128]{1,0:T(8,128)S(1)} %get-tuple-element.53.rd_ref, ...), custom_call_target="tpu_custom_call" | custom-call | tf_op jit(solution)/shard_map/pallas_call | solution.py:395
  (3 shorter events, 0.0 us)
Async XLA Ops:
  0.9 7.4 %collective-permute-start = (f32[2,8,128]{2,1,0:T(8,128)S(1)}, f32[2,8,128]{2,1,0:T(8,128)S(1)}, u32[]{:S(2)}, u32[]{:S(2)}) collective-permute-start(f32[2,8,128]{2,1,0:T(8,128)S(1)} %get-tuple-element.34), channel_id=1, source_target_pairs={{0,16},{16,32},{32,48},{48,64},{64,80},{80,96},{96,112},{112,0},{1... | collective-permute-start | bytes 24584 | tf_op jit(solution)/shard_map/ppermute | solution.py:431
  2.9 5.4 %collective-permute-start.1 = (f32[2,8,128]{2,1,0:T(8,128)S(1)}, f32[2,8,128]{2,1,0:T(8,128)S(1)}, u32[]{:S(2)}, u32[]{:S(2)}) collective-permute-start(f32[2,8,128]{2,1,0:T(8,128)S(1)} %get-tuple-element.35), channel_id=1, source_target_pairs={{16,0},{32,16},{48,32},{64,48},{80,64},{96,80},{112,96},{0,112},{1... | collective-permute-start | bytes 24584 | tf_op jit(solution)/shard_map/ppermute | solution.py:430
  8.7 1.3 %collective-permute-start.2 = (f32[5,8,128]{2,1,0:T(8,128)S(1)}, f32[5,8,128]{2,1,0:T(8,128)S(1)}, u32[]{:S(2)}, u32[]{:S(2)}) collective-permute-start(f32[5,8,128]{2,1,0:T(8,128)S(1)} %get-tuple-element.42.refs_0_), channel_id=1, source_target_pairs={{0,1},{1,0},{2,3},{3,2},{4,5},{5,4},{6,7},{7,6},{8,9},{9,8},{10,11... | collective-permute-start | bytes 61448 | tf_op jit(solution)/shard_map/ppermute | solution.py:407
  10.0 3.3 %collective-permute-start.3 = (f32[5,8,128]{2,1,0:T(8,128)S(1)}, f32[5,8,128]{2,1,0:T(8,128)S(1)}, u32[]{:S(2)}, u32[]{:S(2)}) collective-permute-start(f32[5,8,128]{2,1,0:T(8,128)S(1)} %shard_map.58.refs_0_), channel_id=1, source_target_pairs={{0,3},{1,2},{2,1},{3,0},{4,7},{5,6},{6,5},{7,4},{8,11},{9,10},{10,... | collective-permute-start | bytes 61448 | tf_op jit(solution)/shard_map/ppermute | solution.py:407
  13.3 4.5 %collective-permute-start.4 = (f32[5,8,128]{2,1,0:T(8,128)S(1)}, f32[5,8,128]{2,1,0:T(8,128)S(1)}, u32[]{:S(2)}, u32[]{:S(2)}) collective-permute-start(f32[5,8,128]{2,1,0:T(8,128)S(1)} %shard_map.59.refs_0_), channel_id=1, source_target_pairs={{0,7},{1,6},{2,5},{3,4},{4,3},{5,2},{6,1},{7,0},{8,15},{9,14},{10,... | collective-permute-start | bytes 61448 | tf_op jit(solution)/shard_map/ppermute | solution.py:407
  17.8 4.9 %collective-permute-start.5 = (f32[5,8,128]{2,1,0:T(8,128)S(1)}, f32[5,8,128]{2,1,0:T(8,128)S(1)}, u32[]{:S(2)}, u32[]{:S(2)}) collective-permute-start(f32[5,8,128]{2,1,0:T(8,128)S(1)} %shard_map.60), channel_id=1, source_target_pairs={{0,9},{1,8},{2,11},{3,10},{4,13},{5,12},{6,15},{7,14},{8,1},{9,0},... | collective-permute-start | bytes 61448 | tf_op jit(solution)/shard_map/ppermute | solution.py:407

commit v9 on v8

--- a/solution.py
+++ b/solution.py
@@ -193,9 +193,12 @@
         copy.start()
     for copy in copies:
         copy.wait()
-    for k, row, out in ((0, 0, up_ref), (1, 7, down_ref)):
-        out[0] = t_ref[k, :, row, :]
-        out[1] = reg_ref[k, :, row, :].astype(F32)
+    even = lax.axis_index("row") % 2 == 0
+    up = t_ref[0, :, 0, :], reg_ref[0, :, 0, :].astype(F32)
+    down = t_ref[1, :, 7, :], reg_ref[1, :, 7, :].astype(F32)
+    for k in range(2):
+        up_ref[k] = jnp.where(even, up[k], down[k])
+        down_ref[k] = jnp.where(even, down[k], up[k])
 
 
 def first_kernel(
@@ -288,7 +291,10 @@
     mag = [par_ref[k] for k in range(3)]
     soft = [par_ref[3 + k] for k in range(3)]
     ry_ref[...] = r_ref[...]
-    for row, halo, there in ((0, north_ref, me > 0), (N - 1, south_ref, me < lax.axis_size("row") - 1)):
+    even = me % 2 == 0
+    first = [jnp.where(even, north_ref[k], south_ref[k]) for k in range(2)]
+    last = [jnp.where(even, south_ref[k], north_ref[k]) for k in range(2)]
+    for row, halo, there in ((0, first, me > 0), (N - 1, last, me < lax.axis_size("row") - 1)):
         i = slice(row * Z, row * Z + Z)
         beyond = conductivity(halo[0], halo[1], mag, soft)
         flux = link(cy_ref[i, :], beyond) * (halo[0] - ty_ref[i, :])
@@ -427,8 +433,8 @@
         out_shape=(vm((2, Z, N)),) * 2,
         scratch_shapes=[vm(edge), VM(edge, jnp.int32), pltpu.SemaphoreType.DMA((2, 2))],
     )(t, region)
-    south = lax.ppermute(up, "row", [((i + 1) % n, i) for i in range(n)])
-    north = lax.ppermute(down, "row", [(i, (i + 1) % n) for i in range(n)])
+    south = partner(down, "row", 1)
+    north = lax.ppermute(up, "row", [(i, (i + i % 2 * 2 - 1) % n) for i in range(n)])
     par, ty, cy, r, pr, gr, rr, sep, net, face = call(
         first_kernel,
         [],

time: 34.9 us -> 34.8 us (level)
  blocking collectives: 10.5 us -> 9.69 us
  waiting for transfers between devices: 6.03 us -> 6.83 us
    ppermute x4 -> x5, waiting for transfers between devices: 6.02 us -> 6.83 us  [partner(): lax.ppermute(x, axis, [(i, i ^ mask) for i in range(lax.axis_size(axis))])]
    all_to_all x1, blocking collectives: 10.5 us -> 9.69 us  [local(): got = lax.all_to_all(send, 'row', 0, 0, tiled=True)]
    ppermute x2 -> x1, starting transfers between devices: 4.6 us -> 4.53 us  [local(): lax.ppermute(up, 'row', [(i, (i + i % 2 * 2 - 1) % n) for i in range(n)])]
    ppermute x4 -> x5, starting transfers between devices: 7.46 us -> 7.47 us  [partner(): lax.ppermute(x, axis, [(i, i ^ mask) for i in range(lax.axis_size(axis))])]
  transfers between devices with their start and end apart: 6 -> 6, of which waited for: 4 -> 5; matrix products, arithmetic and copies ran while one was open for 0% -> 0% of each run, Pallas kernels for 10% -> 10%
where the time goes in v9:
time: 34.8 us; the launch traced here: 34.6 us
  starting transfers between devices  12 us (34%)
  blocking collectives  9.69 us (28%)
  waiting for transfers between devices  6.83 us (20%)
  Pallas kernels  6 us (17%)
    all_to_all x1, blocking collectives, local(): got = lax.all_to_all(send, 'row', 0, 0, tiled=True)  9.69 us
    ppermute x5, starting transfers between devices, partner(): lax.ppermute(x, axis, [(i, i ^ mask) for i in range(lax.axis_size(axis))])  7.47 us
    ppermute x5, waiting for transfers between devices, partner(): lax.ppermute(x, axis, [(i, i ^ mask) for i in range(lax.axis_size(axis))])  6.83 us
    pallas_call x8, Pallas kernels, call(): pl.pallas_call(kernel, in_specs=[whole] * len(args) + [pl.BlockSpec(memor...  5.13 us
    ppermute x1, starting transfers between devices, local(): lax.ppermute(up, 'row', [(i, (i + i % 2 * 2 - 1) % n) for i in range(n)])  4.53 us
    pallas_call x1, Pallas kernels, local(): pl.pallas_call(edge_kernel, in_specs=[pl.BlockSpec(memory_space=pltpu.HBM...  0.86 us
  transfers between devices with their start and end apart: 6, of which 5 were waited for; matrix products, arithmetic and copies ran while one was open for 0% of the time, Pallas kernels for 10%

profile of v9, /device:TPU:0, one launch (start us, length us, event | category | flops | bytes accessed | tf_op | source)
XLA Modules:
  0.0 34.6 jit_solution(13605947459039130856)
XLA Ops:
  0.0 0.9 %shard_map.56 = (f32[2,8,128]{2,1,0:T(8,128)S(1)}, f32[2,8,128]{2,1,0:T(8,128)S(1)}) custom-call(f32[8,128,128]{2,1,0:T(8,128)} %t_hbm.3, s32[8,128,128]{2,1,0:T(8,128)} %reg_hbm.3), custom_call_target="tpu_custom_call" | custom-call | tf_op jit(solution)/shard_map/pallas_call | solution.py:429
  0.9 4.5 %collective-permute-start = (f32[2,8,128]{2,1,0:T(8,128)S(1)}, f32[2,8,128]{2,1,0:T(8,128)S(1)}, u32[]{:S(2)}, u32[]{:S(2)}) collective-permute-start(f32[2,8,128]{2,1,0:T(8,128)S(1)} %get-tuple-element.34), channel_id=1, source_target_pairs={{0,112},{16,32},{32,16},{48,64},{64,48},{80,96},{96,80},{112,0},{1... | collective-permute-start | bytes 24584 | tf_op jit(solution)/shard_map/ppermute | solution.py:437
  5.4 0.0 collective-permute-start.1
  5.4 2.8 %shard_map.55 = (f32[6,8,128]{2,1,0:T(8,128)S(1)}, f32[1024,128]{1,0:T(8,128)S(1)}, f32[1024,128]{1,0:T(8,128)S(1)}, f32[1024,128]{1,0:T(8,128)S(1)}, f32[1024,1...) custom-call(f32[8,128,128]{2,1,0:T(8,128)} %t_hbm.3, ...), custom_call_target="tpu_custom_call" | custom-call | flops 20000000 | bytes 20000000 | tf_op jit(solution)/shard_map/pallas_call | solution.py:401
  8.2 0.0 collective-permute-done.north_ref
  8.2 0.8 %collective-permute-done.1.south_ref = f32[2,8,128]{2,1,0:T(8,128)S(1)} collective-permute-done((f32[2,8,128]{2,1,0:T(8,128)S(1)}, f32[2,8,128]{2,1,0:T(8,128)S(1)}, u32[]{:S(2)}, u32[]{:S(2)}) %collective-permute-start.1) | collective-permute-done | bytes 8224 | tf_op jit(solution)/shard_map/ppermute | solution.py:413
  9.1 0.4 %shard_map.57 = (f32[1024,128]{1,0:T(8,128)S(1)}, f32[8,8,128]{2,1,0:T(8,128)S(1)}, f32[2,8,128]{2,1,0:T(8,128)S(1)}, f32[5,8,128]{2,1,0:T(8,128)S(1)}, f32[8,128]{1,0:T(8,128)S(1)}) custom-call(f32[6,8,128]{2,1,0:T(8,128)S(1)} %get-tuple-element.30.par_ref, f32[1024,128]{1,0:T(8,128)S(1)} %get-tuple-element.31.r_ref, ...), custom_call_target="tpu_custom_call" | custom-call | tf_op jit(solution)/shard_map/pallas_call | solution.py:401
  9.4 0.1 collective-permute-start.2
  9.5 1.2 %collective-permute-done.2.refs_1_ = f32[5,8,128]{2,1,0:T(8,128)S(1)} collective-permute-done((f32[5,8,128]{2,1,0:T(8,128)S(1)}, f32[5,8,128]{2,1,0:T(8,128)S(1)}, u32[]{:S(2)}, u32[]{:S(2)}) %collective-permute-start.2) | collective-permute-done | bytes 20512 | tf_op jit(solution)/shard_map/ppermute | solution.py:413
  10.7 1.3 %collective-permute-start.3 = (f32[5,8,128]{2,1,0:T(8,128)S(1)}, f32[5,8,128]{2,1,0:T(8,128)S(1)}, u32[]{:S(2)}, u32[]{:S(2)}) collective-permute-start(f32[5,8,128]{2,1,0:T(8,128)S(1)} %shard_map.58.refs_0_), channel_id=1, source_target_pairs={{0,3},{1,2},{2,1},{3,0},{4,7},{5,6},{6,5},{7,4},{8,11},{9,10},{10,... | collective-permute-start | bytes 61448 | tf_op jit(solution)/shard_map/ppermute | solution.py:413
  12.1 1.9 %collective-permute-done.3.refs_1_.refs_2_ = f32[5,8,128]{2,1,0:T(8,128)S(1)} collective-permute-done((f32[5,8,128]{2,1,0:T(8,128)S(1)}, f32[5,8,128]{2,1,0:T(8,128)S(1)}, u32[]{:S(2)}, u32[]{:S(2)}) %collective-permute-start.3) | collective-permute-done | bytes 20512 | tf_op jit(solution)/shard_map/ppermute | solution.py:413
  14.0 2.6 %collective-permute-start.4 = (f32[5,8,128]{2,1,0:T(8,128)S(1)}, f32[5,8,128]{2,1,0:T(8,128)S(1)}, u32[]{:S(2)}, u32[]{:S(2)}) collective-permute-start(f32[5,8,128]{2,1,0:T(8,128)S(1)} %shard_map.59.refs_0_), channel_id=1, source_target_pairs={{0,7},{1,6},{2,5},{3,4},{4,3},{5,2},{6,1},{7,0},{8,15},{9,14},{10,... | collective-permute-start | bytes 61448 | tf_op jit(solution)/shard_map/ppermute | solution.py:413
  16.6 1.9 %collective-permute-done.4.refs_1_.refs_3_ = f32[5,8,128]{2,1,0:T(8,128)S(1)} collective-permute-done((f32[5,8,128]{2,1,0:T(8,128)S(1)}, f32[5,8,128]{2,1,0:T(8,128)S(1)}, u32[]{:S(2)}, u32[]{:S(2)}) %collective-permute-start.4) | collective-permute-done | bytes 20512 | tf_op jit(solution)/shard_map/ppermute | solution.py:413
  18.5 3.4 %collective-permute-start.5 = (f32[5,8,128]{2,1,0:T(8,128)S(1)}, f32[5,8,128]{2,1,0:T(8,128)S(1)}, u32[]{:S(2)}, u32[]{:S(2)}) collective-permute-start(f32[5,8,128]{2,1,0:T(8,128)S(1)} %shard_map.60), channel_id=1, source_target_pairs={{0,9},{1,8},{2,11},{3,10},{4,13},{5,12},{6,15},{7,14},{8,1},{9,0},... | collective-permute-start | bytes 61448 | tf_op jit(solution)/shard_map/ppermute | solution.py:413
  22.0 0.5 %shard_map.61 = (f32[1024,128]{1,0:T(8,128)S(1)}, f32[1024,128]{1,0:T(8,128)S(1)}, f32[1024,128]{1,0:T(8,128)S(1)}, f32[3,8,8,128]{3,2,1,0:T(8,128)S(1)}, f32[3,8,128]{2,1,0:T(8,128)S(1)}) custom-call(f32[1024,128]{1,0:T(8,128)S(1)} %get-tuple-element.33.cy_ref.c_ref, f32[8,128]{1,0:T(8,128)S(1)} %get-tuple-element.46.south_ref), custom_call_target="tpu_custom_call" | custom-call | flops 5000000 | bytes 5000000 | tf_op jit(solution)/shard_map/pallas_call | solution.py:401
  22.4 1.0 %collective-permute-done.5.refs_4_ = f32[5,8,128]{2,1,0:T(8,128)S(1)} collective-permute-done((f32[5,8,128]{2,1,0:T(8,128)S(1)}, f32[5,8,128]{2,1,0:T(8,128)S(1)}, u32[]{:S(2)}, u32[]{:S(2)}) %collective-permute-start.5) | collective-permute-done | bytes 20512 | tf_op jit(solution)/shard_map/ppermute | solution.py:413
  23.4 0.5 %shard_map.62 = (f32[1024,128]{1,0:T(8,128)S(1)}, f32[8,8,128]{2,1,0:T(8,128)S(1)}, f32[8,5,8,128]{3,2,1,0:T(8,128)S(1)}) custom-call(f32[5,8,128]{2,1,0:T(8,128)S(1)} %get-tuple-element.42.refs_0_, f32[5,8,128]{2,1,0:T(8,128)S(1)} %collective-permute-done.2.refs_1_, f32[5,8,128]{2,1,0:T(8,128)S(1)} %collective-permute-done.3.refs_1_.refs_2_, ...), custom_call_target="tpu_custom_call" | custom-call | tf_op jit(solution)/shard_map/pallas_call | solution.py:401
  23.9 9.7 %all_to_all.5.all_ref = f32[8,5,8,128]{3,2,1,0:T(8,128)S(1)} all-to-all(f32[8,5,8,128]{3,2,1,0:T(8,128)S(1)} %get-tuple-element.52), channel_id=1, replica_groups=mesh['row'=8,'col'=16] {'row'}, dimensions={0} | all-to-all | bytes 327680 | tf_op jit(solution)/shard_map/all_to_all | solution.py:466
  33.6 1.0 %shard_map.63 = f32[8,128,128]{2,1,0:T(8,128)} custom-call(f32[8,5,8,128]{3,2,1,0:T(8,128)S(1)} %all_to_all.5.all_ref, f32[1024,128]{1,0:T(8,128)S(1)} %get-tuple-element.47.refs_13_.pr_ref, f32[1024,128]{1,0:T(8,128)S(1)} %get-tuple-element.48.refs_14_.gr_ref, f32[1024,128]{1,0:T(8,128)S(1)} %get-tuple-element.53.rd_ref, ...), custom_call_target="tpu_custom_call" | custom-call | tf_op jit(solution)/shard_map/pallas_call | solution.py:401
  (3 shorter events, 0.0 us)
Async XLA Ops:
  0.9 7.4 %collective-permute-start = (f32[2,8,128]{2,1,0:T(8,128)S(1)}, f32[2,8,128]{2,1,0:T(8,128)S(1)}, u32[]{:S(2)}, u32[]{:S(2)}) collective-permute-start(f32[2,8,128]{2,1,0:T(8,128)S(1)} %get-tuple-element.34), channel_id=1, source_target_pairs={{0,112},{16,32},{32,16},{48,64},{64,48},{80,96},{96,80},{112,0},{1... | collective-permute-start | bytes 24584 | tf_op jit(solution)/shard_map/ppermute | solution.py:437
  5.4 3.7 %collective-permute-start.1 = (f32[2,8,128]{2,1,0:T(8,128)S(1)}, f32[2,8,128]{2,1,0:T(8,128)S(1)}, u32[]{:S(2)}, u32[]{:S(2)}) collective-permute-start(f32[2,8,128]{2,1,0:T(8,128)S(1)} %get-tuple-element.35), channel_id=1, source_target_pairs={{0,16},{16,0},{32,48},{48,32},{64,80},{80,64},{96,112},{112,96},{1... | collective-permute-start | bytes 24584 | tf_op jit(solution)/shard_map/ppermute | solution.py:413
  9.4 1.3 %collective-permute-start.2 = (f32[5,8,128]{2,1,0:T(8,128)S(1)}, f32[5,8,128]{2,1,0:T(8,128)S(1)}, u32[]{:S(2)}, u32[]{:S(2)}) collective-permute-start(f32[5,8,128]{2,1,0:T(8,128)S(1)} %get-tuple-element.42.refs_0_), channel_id=1, source_target_pairs={{0,1},{1,0},{2,3},{3,2},{4,5},{5,4},{6,7},{7,6},{8,9},{9,8},{10,11... | collective-permute-start | bytes 61448 | tf_op jit(solution)/shard_map/ppermute | solution.py:413
  10.7 3.3 %collective-permute-start.3 = (f32[5,8,128]{2,1,0:T(8,128)S(1)}, f32[5,8,128]{2,1,0:T(8,128)S(1)}, u32[]{:S(2)}, u32[]{:S(2)}) collective-permute-start(f32[5,8,128]{2,1,0:T(8,128)S(1)} %shard_map.58.refs_0_), channel_id=1, source_target_pairs={{0,3},{1,2},{2,1},{3,0},{4,7},{5,6},{6,5},{7,4},{8,11},{9,10},{10,... | collective-permute-start | bytes 61448 | tf_op jit(solution)/shard_map/ppermute | solution.py:413
  14.0 4.5 %collective-permute-start.4 = (f32[5,8,128]{2,1,0:T(8,128)S(1)}, f32[5,8,128]{2,1,0:T(8,128)S(1)}, u32[]{:S(2)}, u32[]{:S(2)}) collective-permute-start(f32[5,8,128]{2,1,0:T(8,128)S(1)} %shard_map.59.refs_0_), channel_id=1, source_target_pairs={{0,7},{1,6},{2,5},{3,4},{4,3},{5,2},{6,1},{7,0},{8,15},{9,14},{10,... | collective-permute-start | bytes 61448 | tf_op jit(solution)/shard_map/ppermute | solution.py:413
  18.5 4.9 %collective-permute-start.5 = (f32[5,8,128]{2,1,0:T(8,128)S(1)}, f32[5,8,128]{2,1,0:T(8,128)S(1)}, u32[]{:S(2)}, u32[]{:S(2)}) collective-permute-start(f32[5,8,128]{2,1,0:T(8,128)S(1)} %shard_map.60), channel_id=1, source_target_pairs={{0,9},{1,8},{2,11},{3,10},{4,13},{5,12},{6,15},{7,14},{8,1},{9,0},... | collective-permute-start | bytes 61448 | tf_op jit(solution)/shard_map/ppermute | solution.py:413

commit v10 on v9

--- a/solution.py
+++ b/solution.py
@@ -371,13 +371,13 @@
     copies = []
 
     def send(group):
-        rows = pl.ds(group * (N // 2), N // 2)
+        rows = pl.ds(group * (N // 4), N // 4)
         copies.append(
             pltpu.make_async_copy(box.at[:, rows, :], out_hbm.at[:, rows, :], sem.at[group])
         )
         copies[-1].start()
 
-    back(ul, ur, pr_ref, gr_ref, rd_ref, sep_ref, srd_ref, put, True, 2, send)
+    back(ul, ur, pr_ref, gr_ref, rd_ref, sep_ref, srd_ref, put, True, 4, send)
     for copy in copies:
         copy.wait()
 
@@ -468,7 +468,7 @@
         last_kernel,
         [got, ypr, ygr, yrd, ysep, ysrd, ty],
         jax.ShapeDtypeStruct((Z, N, N), F32),
-        scratch=[vm(SPACED), pltpu.SemaphoreType.DMA((2,))],
+        scratch=[vm(SPACED), pltpu.SemaphoreType.DMA((4,))],
         out_space=pl.ANY,
     )
     return out

time: 34.8 us -> 34.8 us (level)
  no operation moved by 1% of the time
where the time goes in v10:
time: 34.8 us; the launch traced here: 34.6 us
  starting transfers between devices  12 us (34%)
  blocking collectives  9.69 us (28%)
  waiting for transfers between devices  6.83 us (20%)
  Pallas kernels  5.99 us (17%)
    all_to_all x1, blocking collectives, local(): got = lax.all_to_all(send, 'row', 0, 0, tiled=True)  9.69 us
    ppermute x5, starting transfers between devices, partner(): lax.ppermute(x, axis, [(i, i ^ mask) for i in range(lax.axis_size(axis))])  7.47 us
    ppermute x5, waiting for transfers between devices, partner(): lax.ppermute(x, axis, [(i, i ^ mask) for i in range(lax.axis_size(axis))])  6.83 us
    pallas_call x8, Pallas kernels, call(): pl.pallas_call(kernel, in_specs=[whole] * len(args) + [pl.BlockSpec(memor...  5.13 us
    ppermute x1, starting transfers between devices, local(): lax.ppermute(up, 'row', [(i, (i + i % 2 * 2 - 1) % n) for i in range(n)])  4.53 us
    pallas_call x1, Pallas kernels, local(): pl.pallas_call(edge_kernel, in_specs=[pl.BlockSpec(memory_space=pltpu.HBM...  0.86 us
  transfers between devices with their start and end apart: 6, of which 5 were waited for; matrix products, arithmetic and copies ran while one was open for 0% of the time, Pallas kernels for 10%

profile of v10, /device:TPU:0, one launch (start us, length us, event | category | flops | bytes accessed | tf_op | source)
XLA Modules:
  0.0 34.6 jit_solution(854826650164447460)
XLA Ops:
  0.0 0.9 %shard_map.56 = (f32[2,8,128]{2,1,0:T(8,128)S(1)}, f32[2,8,128]{2,1,0:T(8,128)S(1)}) custom-call(f32[8,128,128]{2,1,0:T(8,128)} %t_hbm.3, s32[8,128,128]{2,1,0:T(8,128)} %reg_hbm.3), custom_call_target="tpu_custom_call" | custom-call | tf_op jit(solution)/shard_map/pallas_call | solution.py:429
  0.9 4.5 %collective-permute-start = (f32[2,8,128]{2,1,0:T(8,128)S(1)}, f32[2,8,128]{2,1,0:T(8,128)S(1)}, u32[]{:S(2)}, u32[]{:S(2)}) collective-permute-start(f32[2,8,128]{2,1,0:T(8,128)S(1)} %get-tuple-element.34), channel_id=1, source_target_pairs={{0,112},{16,32},{32,16},{48,64},{64,48},{80,96},{96,80},{112,0},{1... | collective-permute-start | bytes 24584 | tf_op jit(solution)/shard_map/ppermute | solution.py:437
  5.4 0.0 collective-permute-start.1
  5.4 2.8 %shard_map.55 = (f32[6,8,128]{2,1,0:T(8,128)S(1)}, f32[1024,128]{1,0:T(8,128)S(1)}, f32[1024,128]{1,0:T(8,128)S(1)}, f32[1024,128]{1,0:T(8,128)S(1)}, f32[1024,1...) custom-call(f32[8,128,128]{2,1,0:T(8,128)} %t_hbm.3, ...), custom_call_target="tpu_custom_call" | custom-call | flops 20000000 | bytes 20000000 | tf_op jit(solution)/shard_map/pallas_call | solution.py:401
  8.2 0.0 collective-permute-done.north_ref
  8.2 0.8 %collective-permute-done.1.south_ref = f32[2,8,128]{2,1,0:T(8,128)S(1)} collective-permute-done((f32[2,8,128]{2,1,0:T(8,128)S(1)}, f32[2,8,128]{2,1,0:T(8,128)S(1)}, u32[]{:S(2)}, u32[]{:S(2)}) %collective-permute-start.1) | collective-permute-done | bytes 8224 | tf_op jit(solution)/shard_map/ppermute | solution.py:413
  9.1 0.4 %shard_map.57 = (f32[1024,128]{1,0:T(8,128)S(1)}, f32[8,8,128]{2,1,0:T(8,128)S(1)}, f32[2,8,128]{2,1,0:T(8,128)S(1)}, f32[5,8,128]{2,1,0:T(8,128)S(1)}, f32[8,128]{1,0:T(8,128)S(1)}) custom-call(f32[6,8,128]{2,1,0:T(8,128)S(1)} %get-tuple-element.30.par_ref, f32[1024,128]{1,0:T(8,128)S(1)} %get-tuple-element.31.r_ref, ...), custom_call_target="tpu_custom_call" | custom-call | tf_op jit(solution)/shard_map/pallas_call | solution.py:401
  9.4 0.1 collective-permute-start.2
  9.5 1.2 %collective-permute-done.2.refs_1_ = f32[5,8,128]{2,1,0:T(8,128)S(1)} collective-permute-done((f32[5,8,128]{2,1,0:T(8,128)S(1)}, f32[5,8,128]{2,1,0:T(8,128)S(1)}, u32[]{:S(2)}, u32[]{:S(2)}) %collective-permute-start.2) | collective-permute-done | bytes 20512 | tf_op jit(solution)/shard_map/ppermute | solution.py:413
  10.7 1.3 %collective-permute-start.3 = (f32[5,8,128]{2,1,0:T(8,128)S(1)}, f32[5,8,128]{2,1,0:T(8,128)S(1)}, u32[]{:S(2)}, u32[]{:S(2)}) collective-permute-start(f32[5,8,128]{2,1,0:T(8,128)S(1)} %shard_map.58.refs_0_), channel_id=1, source_target_pairs={{0,3},{1,2},{2,1},{3,0},{4,7},{5,6},{6,5},{7,4},{8,11},{9,10},{10,... | collective-permute-start | bytes 61448 | tf_op jit(solution)/shard_map/ppermute | solution.py:413
  12.1 1.9 %collective-permute-done.3.refs_1_.refs_2_ = f32[5,8,128]{2,1,0:T(8,128)S(1)} collective-permute-done((f32[5,8,128]{2,1,0:T(8,128)S(1)}, f32[5,8,128]{2,1,0:T(8,128)S(1)}, u32[]{:S(2)}, u32[]{:S(2)}) %collective-permute-start.3) | collective-permute-done | bytes 20512 | tf_op jit(solution)/shard_map/ppermute | solution.py:413
  14.0 2.6 %collective-permute-start.4 = (f32[5,8,128]{2,1,0:T(8,128)S(1)}, f32[5,8,128]{2,1,0:T(8,128)S(1)}, u32[]{:S(2)}, u32[]{:S(2)}) collective-permute-start(f32[5,8,128]{2,1,0:T(8,128)S(1)} %shard_map.59.refs_0_), channel_id=1, source_target_pairs={{0,7},{1,6},{2,5},{3,4},{4,3},{5,2},{6,1},{7,0},{8,15},{9,14},{10,... | collective-permute-start | bytes 61448 | tf_op jit(solution)/shard_map/ppermute | solution.py:413
  16.6 1.9 %collective-permute-done.4.refs_1_.refs_3_ = f32[5,8,128]{2,1,0:T(8,128)S(1)} collective-permute-done((f32[5,8,128]{2,1,0:T(8,128)S(1)}, f32[5,8,128]{2,1,0:T(8,128)S(1)}, u32[]{:S(2)}, u32[]{:S(2)}) %collective-permute-start.4) | collective-permute-done | bytes 20512 | tf_op jit(solution)/shard_map/ppermute | solution.py:413
  18.5 3.4 %collective-permute-start.5 = (f32[5,8,128]{2,1,0:T(8,128)S(1)}, f32[5,8,128]{2,1,0:T(8,128)S(1)}, u32[]{:S(2)}, u32[]{:S(2)}) collective-permute-start(f32[5,8,128]{2,1,0:T(8,128)S(1)} %shard_map.60), channel_id=1, source_target_pairs={{0,9},{1,8},{2,11},{3,10},{4,13},{5,12},{6,15},{7,14},{8,1},{9,0},... | collective-permute-start | bytes 61448 | tf_op jit(solution)/shard_map/ppermute | solution.py:413
  22.0 0.5 %shard_map.61 = (f32[1024,128]{1,0:T(8,128)S(1)}, f32[1024,128]{1,0:T(8,128)S(1)}, f32[1024,128]{1,0:T(8,128)S(1)}, f32[3,8,8,128]{3,2,1,0:T(8,128)S(1)}, f32[3,8,128]{2,1,0:T(8,128)S(1)}) custom-call(f32[1024,128]{1,0:T(8,128)S(1)} %get-tuple-element.33.cy_ref.c_ref, f32[8,128]{1,0:T(8,128)S(1)} %get-tuple-element.46.south_ref), custom_call_target="tpu_custom_call" | custom-call | flops 5000000 | bytes 5000000 | tf_op jit(solution)/shard_map/pallas_call | solution.py:401
  22.4 1.0 %collective-permute-done.5.refs_4_ = f32[5,8,128]{2,1,0:T(8,128)S(1)} collective-permute-done((f32[5,8,128]{2,1,0:T(8,128)S(1)}, f32[5,8,128]{2,1,0:T(8,128)S(1)}, u32[]{:S(2)}, u32[]{:S(2)}) %collective-permute-start.5) | collective-permute-done | bytes 20512 | tf_op jit(solution)/shard_map/ppermute | solution.py:413
  23.4 0.5 %shard_map.62 = (f32[1024,128]{1,0:T(8,128)S(1)}, f32[8,8,128]{2,1,0:T(8,128)S(1)}, f32[8,5,8,128]{3,2,1,0:T(8,128)S(1)}) custom-call(f32[5,8,128]{2,1,0:T(8,128)S(1)} %get-tuple-element.42.refs_0_, f32[5,8,128]{2,1,0:T(8,128)S(1)} %collective-permute-done.2.refs_1_, f32[5,8,128]{2,1,0:T(8,128)S(1)} %collective-permute-done.3.refs_1_.refs_2_, ...), custom_call_target="tpu_custom_call" | custom-call | tf_op jit(solution)/shard_map/pallas_call | solution.py:401
  23.9 9.7 %all_to_all.5.all_ref = f32[8,5,8,128]{3,2,1,0:T(8,128)S(1)} all-to-all(f32[8,5,8,128]{3,2,1,0:T(8,128)S(1)} %get-tuple-element.52), channel_id=1, replica_groups=mesh['row'=8,'col'=16] {'row'}, dimensions={0} | all-to-all | bytes 327680 | tf_op jit(solution)/shard_map/all_to_all | solution.py:466
  33.6 0.9 %shard_map.63 = f32[8,128,128]{2,1,0:T(8,128)} custom-call(f32[8,5,8,128]{3,2,1,0:T(8,128)S(1)} %all_to_all.5.all_ref, f32[1024,128]{1,0:T(8,128)S(1)} %get-tuple-element.47.refs_13_.pr_ref, f32[1024,128]{1,0:T(8,128)S(1)} %get-tuple-element.48.refs_14_.gr_ref, f32[1024,128]{1,0:T(8,128)S(1)} %get-tuple-element.53.rd_ref, ...), custom_call_target="tpu_custom_call" | custom-call | tf_op jit(solution)/shard_map/pallas_call | solution.py:401
  (3 shorter events, 0.0 us)
Async XLA Ops:
  0.9 7.4 %collective-permute-start = (f32[2,8,128]{2,1,0:T(8,128)S(1)}, f32[2,8,128]{2,1,0:T(8,128)S(1)}, u32[]{:S(2)}, u32[]{:S(2)}) collective-permute-start(f32[2,8,128]{2,1,0:T(8,128)S(1)} %get-tuple-element.34), channel_id=1, source_target_pairs={{0,112},{16,32},{32,16},{48,64},{64,48},{80,96},{96,80},{112,0},{1... | collective-permute-start | bytes 24584 | tf_op jit(solution)/shard_map/ppermute | solution.py:437
  5.4 3.7 %collective-permute-start.1 = (f32[2,8,128]{2,1,0:T(8,128)S(1)}, f32[2,8,128]{2,1,0:T(8,128)S(1)}, u32[]{:S(2)}, u32[]{:S(2)}) collective-permute-start(f32[2,8,128]{2,1,0:T(8,128)S(1)} %get-tuple-element.35), channel_id=1, source_target_pairs={{0,16},{16,0},{32,48},{48,32},{64,80},{80,64},{96,112},{112,96},{1... | collective-permute-start | bytes 24584 | tf_op jit(solution)/shard_map/ppermute | solution.py:413
  9.4 1.3 %collective-permute-start.2 = (f32[5,8,128]{2,1,0:T(8,128)S(1)}, f32[5,8,128]{2,1,0:T(8,128)S(1)}, u32[]{:S(2)}, u32[]{:S(2)}) collective-permute-start(f32[5,8,128]{2,1,0:T(8,128)S(1)} %get-tuple-element.42.refs_0_), channel_id=1, source_target_pairs={{0,1},{1,0},{2,3},{3,2},{4,5},{5,4},{6,7},{7,6},{8,9},{9,8},{10,11... | collective-permute-start | bytes 61448 | tf_op jit(solution)/shard_map/ppermute | solution.py:413
  10.7 3.3 %collective-permute-start.3 = (f32[5,8,128]{2,1,0:T(8,128)S(1)}, f32[5,8,128]{2,1,0:T(8,128)S(1)}, u32[]{:S(2)}, u32[]{:S(2)}) collective-permute-start(f32[5,8,128]{2,1,0:T(8,128)S(1)} %shard_map.58.refs_0_), channel_id=1, source_target_pairs={{0,3},{1,2},{2,1},{3,0},{4,7},{5,6},{6,5},{7,4},{8,11},{9,10},{10,... | collective-permute-start | bytes 61448 | tf_op jit(solution)/shard_map/ppermute | solution.py:413
  14.0 4.5 %collective-permute-start.4 = (f32[5,8,128]{2,1,0:T(8,128)S(1)}, f32[5,8,128]{2,1,0:T(8,128)S(1)}, u32[]{:S(2)}, u32[]{:S(2)}) collective-permute-start(f32[5,8,128]{2,1,0:T(8,128)S(1)} %shard_map.59.refs_0_), channel_id=1, source_target_pairs={{0,7},{1,6},{2,5},{3,4},{4,3},{5,2},{6,1},{7,0},{8,15},{9,14},{10,... | collective-permute-start | bytes 61448 | tf_op jit(solution)/shard_map/ppermute | solution.py:413
  18.5 4.9 %collective-permute-start.5 = (f32[5,8,128]{2,1,0:T(8,128)S(1)}, f32[5,8,128]{2,1,0:T(8,128)S(1)}, u32[]{:S(2)}, u32[]{:S(2)}) collective-permute-start(f32[5,8,128]{2,1,0:T(8,128)S(1)} %shard_map.60), channel_id=1, source_target_pairs={{0,9},{1,8},{2,11},{3,10},{4,13},{5,12},{6,15},{7,14},{8,1},{9,0},... | collective-permute-start | bytes 61448 | tf_op jit(solution)/shard_map/ppermute | solution.py:413
